TPU v7x, 512 devices: a whole 4x8x8 slice. The times are simulated.
512 devices in a mesh: clip: 4 (over y_lo), cfg: 2 (over core), patch: 64 (over z, x, y_hi).
Axes of the slice: x: 4, y: 8 (y_hi: 2, y_lo: 4; y = y_hi * 4 + y_lo), z: 8, core: 2. Of those that a mesh axis runs over, the one named last changes fastest.
Arguments:
- queries: bfloat16 [2, 2, 4096, 4096], P('cfg', None, ('clip', 'patch')), parts along dimension 2, may hold values from -270 to 270
- keys_values: bfloat16 [2, 2, 2, 4096, 4096], P('cfg', None, None, ('clip', 'patch')), parts along dimension 3, may hold values from -8 to 8
- timesteps: int32 [8], P('clip'), parts along dimension 0, may hold values from 0 to 49
- gate_table: float32 [50, 4096], replicated, may hold values from 0.5 to 1.5
Outputs:
- guided: bfloat16 [2, 4096, 32, 128], P(None, ('clip', 'patch'), None, 'cfg'), parts along dimension 1
There are 4 independent parts, one for each index of `clip`. A program takes and returns all parts, laid end to end along the dimension named above; an argument that names none is the same for every part. Nothing has to cross between parts.
All inputs are finite; a program needn't handle non-finite values.
Results may differ from a plain program's by a relative error of at most 0.013.
Values may be sent and summed in bfloat16 or wider, within the bound.
No kernel may reach another device: no remote copies, remote signals or barrier semaphores. Data moves between devices by JAX's collectives and lax.ppermute only.
A program may use at most 64 MiB of HBM per device.

v0:
```python
import math

import jax
import jax.numpy as jnp
from jax import lax
from jax.sharding import PartitionSpec as P

HEADS = 32


def to_heads(field, heads, copies):
    tok, width = field.shape
    depth = width // heads
    return (
        field.reshape(copies, tok // copies, heads, depth)
        .transpose(2, 0, 1, 3)
        .reshape(heads * copies, tok // copies, depth)
    )


def pairs_to_heads(pair, heads, copies):
    tok, width = (pair.shape[1], pair.shape[2])
    depth = width // heads
    split_pair = pair.reshape(2, tok, heads, depth).transpose(2, 0, 1, 3)
    return jnp.broadcast_to(split_pair[:, None], (heads, copies, 2, tok, depth)).reshape(
        heads * copies, 2, tok, depth
    )


def heads_to_tokens(moved, heads):
    return moved.reshape((heads, -1) + moved.shape[2:])


def attend(query_heads, keys_all, local_keys, mode, tok, qrows, n_patch):
    per_dev, n_query, depth = query_heads.shape
    scale = 1.0 / math.sqrt(depth)
    group_cap = max(1, 1024 // qrows)
    group_block = math.gcd(n_patch, 1 << group_cap.bit_length() - 1)
    blocks = n_patch // group_block
    rows = group_block * qrows
    query_blocks = query_heads.reshape(per_dev, blocks, rows, depth).transpose(1, 0, 2, 3)
    key_patch = jnp.arange(n_patch * tok) // tok

    def one_block(args):
        index, block = args
        scores = (
            jnp.einsum("hqd,hkd->hqk", block, keys_all[:, 0], preferred_element_type=jnp.float32)
            * scale
        )
        if mode != "whole":
            query_patch = index * group_block + jnp.arange(rows) // qrows
            same = query_patch[:, None] == key_patch[None, :]
            scores = jnp.where(same[None], -jnp.inf, scores)
        top = jnp.max(scores, axis=2)
        if mode == "mixed":
            shaped = local_keys.reshape(per_dev, 2, n_patch, tok, depth)
            near = shaped
            grouped = block.reshape(per_dev, group_block, qrows, depth)
            local_scores = (
                jnp.einsum(
                    "hgqd,hgkd->hgqk", grouped, near[:, 0], preferred_element_type=jnp.float32
                )
                * scale
            )
            top = jnp.maximum(top, jnp.max(local_scores, axis=3).reshape(per_dev, rows))
        weight = jnp.exp(scores - top[:, :, None])
        total = jnp.sum(weight, axis=2)
        summed = jnp.einsum(
            "hqk,hkd->hqd",
            weight.astype(jnp.bfloat16),
            keys_all[:, 1],
            preferred_element_type=jnp.float32,
        )
        if mode == "mixed":
            local_weight = jnp.exp(
                local_scores - top.reshape(per_dev, group_block, qrows)[:, :, :, None]
            )
            total = total + jnp.sum(local_weight, axis=3).reshape(per_dev, rows)
            local_sum = jnp.einsum(
                "hgqk,hgkd->hgqd",
                local_weight.astype(jnp.bfloat16),
                near[:, 1],
                preferred_element_type=jnp.float32,
            )
            summed = summed + local_sum.reshape(per_dev, rows, depth)
        return (summed / total[:, :, None]).astype(jnp.bfloat16)

    results = lax.map(one_block, (jnp.arange(blocks), query_blocks))
    return results.transpose(1, 0, 2, 3).reshape(per_dev, n_query, depth)


def combine(both, own_gate):
    cond = both[..., 0, :].astype(jnp.float32)
    uncond = both[..., 1, :].astype(jnp.float32)
    return (own_gate * (uncond + 5.0 * (cond - uncond))).astype(jnp.bfloat16)


def half_gate(gate, heads):
    depth = gate.shape[0] // heads
    return lax.dynamic_slice_in_dim(
        gate.reshape(heads, 2, depth // 2), lax.axis_index("cfg"), 1, 1
    )[:, 0]


def guide(attn_tok, gate, heads):
    depth = attn_tok.shape[2]
    tok = attn_tok.shape[1]
    halves = attn_tok.reshape(heads, tok, 2, depth // 2)
    both = lax.all_to_all(halves, "cfg", split_axis=2, concat_axis=2, tiled=True)
    mixed = combine(both, half_gate(gate, heads)[:, None, :])
    return mixed.transpose(1, 0, 2)


def body(queries, keys_values, timesteps, gate_table):
    n_patch = lax.axis_size("patch")
    tok = queries.shape[2]
    width = queries.shape[3]
    heads = HEADS
    depth = width // heads
    copies = max(1, n_patch // heads)
    qrows = tok // copies
    one_hot = (timesteps[:, None] == jnp.arange(gate_table.shape[0])[None, :]).astype(jnp.float32)
    gates = jnp.dot(one_hot, gate_table, precision=lax.Precision.HIGHEST)
    stale = lax.all_to_all(
        pairs_to_heads(keys_values[0, 0], heads, copies),
        "patch",
        split_axis=0,
        concat_axis=2,
        tiled=True,
    )

    def send_queries(field):
        return lax.all_to_all(
            to_heads(field, heads, copies), "patch", split_axis=0, concat_axis=1, tiled=True
        )

    first_query = send_queries(queries[0, 0])
    second_query = send_queries(queries[0, 1])
    first = attend(first_query, stale, None, "whole", tok, qrows, n_patch)
    first_tok = heads_to_tokens(
        lax.all_to_all(first, "patch", split_axis=1, concat_axis=0, tiled=True), heads
    )
    halves = first_tok.reshape(heads, tok, 2, depth // 2)
    both = lax.all_to_all(halves, "cfg", split_axis=2, concat_axis=2, tiled=True)
    out_first = combine(both, half_gate(gates[0], heads)[:, None, :]).transpose(1, 0, 2)
    fresh = lax.all_to_all(
        pairs_to_heads(keys_values[0, 1], heads, copies),
        "patch",
        split_axis=0,
        concat_axis=2,
        tiled=True,
    )
    second = attend(second_query, stale, fresh, "mixed", tok, qrows, n_patch)
    second_tok = heads_to_tokens(
        lax.all_to_all(second, "patch", split_axis=1, concat_axis=0, tiled=True), heads
    )
    out_second = guide(second_tok, gates[1], heads)
    return jnp.stack([out_first, out_second])


def solution(mesh):
    placed = (
        P("cfg", None, ("clip", "patch"), None),
        P("cfg", None, None, ("clip", "patch"), None),
        P("clip"),
        P(),
    )
    return jax.shard_map(
        body,
        mesh=mesh,
        in_specs=placed,
        out_specs=P(None, ("clip", "patch"), None, "cfg"),
        check_vma=False,
    )
```

profile of v0, /device:TPU:1, one launch (start us, length us, event | category | flops | bytes accessed | tf_op | source)
XLA Modules:
  0.0 162.7 jit_solution(3580090349313223904)
XLA Ops:
  0.0 1.1 slice_bitcast_fusion.15
  1.1 0.7 copy.58
  1.8 19.6 %all-to-all-start.4 = ((bf16[64,8,128]{2,1,0:T(8,128)(2,1)}), bf16[64,8,128]{2,1,0:T(8,128)(2,1)S(1)}, u32[]{:S(2)}, u32[]{:S(2)}) async-start(bf16[64,8,128]{2,1,0:T(8,128)(2,1)} %bitcast.22), calls=%async_computation.4 | async-start | bytes 262144 | tf_op jit(solution)/shard_map/all_to_all | solution.py:133
  21.4 1.1 fusion.42
  22.6 12.3 %all-to-all-done.4 = bf16[64,8,128]{2,1,0:T(8,128)(2,1)S(1)} async-done(((bf16[64,8,128]{2,1,0:T(8,128)(2,1)}), bf16[64,8,128]{2,1,0:T(8,128)(2,1)S(1)}, u32[]{:S(2)}, u32[]{:S(2)}) %all-to-all-start.4) | async-done | bytes 131104 | tf_op jit(solution)/shard_map/all_to_all | solution.py:133
  35.0 0.9 broadcast_in_dim.40
  35.8 4.8 %all-to-all-start.5 = ((bf16[64,2,16,128]{3,2,1,0:T(8,128)(2,1)}), bf16[64,2,16,128]{3,2,1,0:T(8,128)(2,1)S(1)}, u32[]{:S(2)}, u32[]{:S(2)}) async-start(bf16[64,2,16,128]{3,2,1,0:T(8,128)(2,1)} %bitcast.25), calls=%async_computation.5 | async-start | bytes 1048576 | tf_op jit(solution)/shard_map/all_to_all | solution.py:146
  40.8 15.3 %all-to-all-done.5 = bf16[64,2,16,128]{3,2,1,0:T(8,128)(2,1)S(1)} async-done(((bf16[64,2,16,128]{3,2,1,0:T(8,128)(2,1)}), bf16[64,2,16,128]{3,2,1,0:T(8,128)(2,1)S(1)}, u32[]{:S(2)}, u32[]{:S(2)}) %all-to-all-start.5) | async-done | bytes 524320 | tf_op jit(solution)/shard_map/all_to_all | solution.py:146
  56.1 0.9 broadcast_in_dim.38
  57.0 11.6 %all-to-all-start.1 = ((bf16[64,2,16,128]{3,2,1,0:T(8,128)(2,1)}), bf16[64,2,16,128]{3,2,1,0:T(8,128)(2,1)S(1)}, u32[]{:S(2)}, u32[]{:S(2)}) async-start(bf16[64,2,16,128]{3,2,1,0:T(8,128)(2,1)} %bitcast.5), calls=%async_computation.1 | async-start | bytes 1048576 | tf_op jit(solution)/shard_map/all_to_all | solution.py:124
  68.6 0.4 fusion.37
  69.2 0.7 copy.53
  70.0 0.3 fusion.44
  70.4 17.3 %all-to-all-done.1 = bf16[64,2,16,128]{3,2,1,0:T(8,128)(2,1)S(1)} async-done(((bf16[64,2,16,128]{3,2,1,0:T(8,128)(2,1)}), bf16[64,2,16,128]{3,2,1,0:T(8,128)(2,1)S(1)}, u32[]{:S(2)}, u32[]{:S(2)}) %all-to-all-start.1) | async-done | bytes 524320 | tf_op jit(solution)/shard_map/all_to_all | solution.py:124
  87.7 6.7 %all-to-all-start = ((bf16[64,8,128]{2,1,0:T(8,128)(2,1)}), bf16[64,8,128]{2,1,0:T(8,128)(2,1)S(1)}, u32[]{:S(2)}, u32[]{:S(2)}) async-start(bf16[64,8,128]{2,1,0:T(8,128)(2,1)} %bitcast.2), calls=%async_computation | async-start | bytes 262144 | tf_op jit(solution)/shard_map/all_to_all | solution.py:133
  94.4 0.5 fusion.43
  94.9 0.5 fusion
  95.4 0.5 fusion.11
  96.1 0.2 fusion.22
  96.4 0.3 fusion.8
  96.7 0.2 copy.76
  96.9 0.6 broadcast.113
  97.5 1.5 reduce.24
  98.9 0.7 reshape.237
  99.7 8.3 %all-to-all-done = bf16[64,8,128]{2,1,0:T(8,128)(2,1)S(1)} async-done(((bf16[64,8,128]{2,1,0:T(8,128)(2,1)}), bf16[64,8,128]{2,1,0:T(8,128)(2,1)S(1)}, u32[]{:S(2)}, u32[]{:S(2)}) %all-to-all-start) | async-done | bytes 131104 | tf_op jit(solution)/shard_map/all_to_all | solution.py:133
  108.0 6.4 %all-to-all-start.6 = ((bf16[64,2,512]{2,1,0:T(2,128)(2,1)}), bf16[64,2,512]{2,1,0:T(2,128)(2,1)S(1)}, u32[]{:S(2)}, u32[]{:S(2)}) async-start(bf16[64,2,512]{2,1,0:T(2,128)(2,1)} %reshape.237), calls=%async_computation.6 | async-start | bytes 262144 | tf_op jit(solution)/shard_map/all_to_all | solution.py:155
  114.4 0.5 multiply_reduce_fusion
  114.9 0.5 fusion.2
  115.4 0.5 fusion.9
  116.0 0.2 copy.78
  116.2 1.5 reduce.25
  117.7 0.7 reshape.241
  118.4 9.4 %all-to-all-done.6 = bf16[64,2,512]{2,1,0:T(2,128)(2,1)S(1)} async-done(((bf16[64,2,512]{2,1,0:T(2,128)(2,1)}), bf16[64,2,512]{2,1,0:T(2,128)(2,1)S(1)}, u32[]{:S(2)}, u32[]{:S(2)}) %all-to-all-start.6) | async-done | bytes 131104 | tf_op jit(solution)/shard_map/all_to_all | solution.py:155
  127.7 5.0 %all-to-all-start.2 = ((bf16[64,2,512]{2,1,0:T(2,128)(2,1)}), bf16[64,2,512]{2,1,0:T(2,128)(2,1)S(1)}, u32[]{:S(2)}, u32[]{:S(2)}) async-start(bf16[64,2,512]{2,1,0:T(2,128)(2,1)} %reshape.241), calls=%async_computation.2 | async-start | bytes 262144 | tf_op jit(solution)/shard_map/all_to_all | solution.py:141
  133.0 0.7 bitcast_reduce_fusion.1
  133.7 0.1 reshape_reshape.7
  133.9 0.9 reshape.239
  134.8 11.5 %all-to-all-done.2 = bf16[64,2,512]{2,1,0:T(2,128)(2,1)S(1)} async-done(((bf16[64,2,512]{2,1,0:T(2,128)(2,1)}), bf16[64,2,512]{2,1,0:T(2,128)(2,1)S(1)}, u32[]{:S(2)}, u32[]{:S(2)}) %all-to-all-start.2) | async-done | bytes 131104 | tf_op jit(solution)/shard_map/all_to_all | solution.py:141
  146.3 8.8 %all-to-all-start.7 = ((bf16[2,2,16384]{2,1,0:T(2,128)(2,1)}), bf16[2,2,16384]{2,1,0:T(2,128)(2,1)S(1)}, u32[]{:S(2)}, u32[]{:S(2)}) async-start(bf16[2,2,16384]{2,1,0:T(2,128)(2,1)} %reshape.239), calls=%async_computation.7 | async-start | bytes 262144 | tf_op jit(solution)/shard_map/all_to_all | solution.py:109
  155.2 0.7 bitcast_reduce_fusion
  155.9 0.1 reshape_reshape.6
  156.1 0.9 reshape.243
  157.0 3.4 %all-to-all-start.3 = ((bf16[2,2,16384]{2,1,0:T(2,128)(2,1)}), bf16[2,2,16384]{2,1,0:T(2,128)(2,1)S(1)}, u32[]{:S(2)}, u32[]{:S(2)}) async-start(bf16[2,2,16384]{2,1,0:T(2,128)(2,1)} %reshape.243), calls=%async_computation.3 | async-start | bytes 262144 | tf_op jit(solution)/shard_map/all_to_all | solution.py:144
  160.4 0.2 reshape.240
  160.6 0.9 all-to-all-done.3
  161.5 0.2 reshape.244
  161.7 0.1 fusion.26
  161.9 0.8 copy.63
  (32 shorter events, 1.3 us)
Async XLA Ops:
  0.0 68.6 %copy-start = (f32[50,4096]{1,0:T(8,128)S(1)}, f32[50,4096]{1,0:T(8,128)}, u32[]{:S(2)}) copy-start(f32[50,4096]{1,0:T(8,128)} %param.7) | copy-start | bytes 2457604
  1.8 33.2 %all-to-all-start.4 = ((bf16[64,8,128]{2,1,0:T(8,128)(2,1)}), bf16[64,8,128]{2,1,0:T(8,128)(2,1)S(1)}, u32[]{:S(2)}, u32[]{:S(2)}) async-start(bf16[64,8,128]{2,1,0:T(8,128)(2,1)} %bitcast.22), calls=%async_computation.4 | async-start | bytes 262144 | tf_op jit(solution)/shard_map/all_to_all | solution.py:133
  35.8 32.7 %copy-start.1 = (s32[2]{0:T(128)S(1)}, s32[2]{0:T(128)}, u32[]{:S(2)}) copy-start(s32[2]{0:T(128)} %param.6) | copy-start | bytes 28
  35.8 20.2 %all-to-all-start.5 = ((bf16[64,2,16,128]{3,2,1,0:T(8,128)(2,1)}), bf16[64,2,16,128]{3,2,1,0:T(8,128)(2,1)S(1)}, u32[]{:S(2)}, u32[]{:S(2)}) async-start(bf16[64,2,16,128]{3,2,1,0:T(8,128)(2,1)} %bitcast.25), calls=%async_computation.5 | async-start | bytes 1048576 | tf_op jit(solution)/shard_map/all_to_all | solution.py:146
  57.0 30.7 %all-to-all-start.1 = ((bf16[64,2,16,128]{3,2,1,0:T(8,128)(2,1)}), bf16[64,2,16,128]{3,2,1,0:T(8,128)(2,1)S(1)}, u32[]{:S(2)}, u32[]{:S(2)}) async-start(bf16[64,2,16,128]{3,2,1,0:T(8,128)(2,1)} %bitcast.5), calls=%async_computation.1 | async-start | bytes 1048576 | tf_op jit(solution)/shard_map/all_to_all | solution.py:124
  87.7 20.3 %all-to-all-start = ((bf16[64,8,128]{2,1,0:T(8,128)(2,1)}), bf16[64,8,128]{2,1,0:T(8,128)(2,1)S(1)}, u32[]{:S(2)}, u32[]{:S(2)}) async-start(bf16[64,8,128]{2,1,0:T(8,128)(2,1)} %bitcast.2), calls=%async_computation | async-start | bytes 262144 | tf_op jit(solution)/shard_map/all_to_all | solution.py:133
  108.0 19.8 %all-to-all-start.6 = ((bf16[64,2,512]{2,1,0:T(2,128)(2,1)}), bf16[64,2,512]{2,1,0:T(2,128)(2,1)S(1)}, u32[]{:S(2)}, u32[]{:S(2)}) async-start(bf16[64,2,512]{2,1,0:T(2,128)(2,1)} %reshape.237), calls=%async_computation.6 | async-start | bytes 262144 | tf_op jit(solution)/shard_map/all_to_all | solution.py:155
  127.7 18.6 %all-to-all-start.2 = ((bf16[64,2,512]{2,1,0:T(2,128)(2,1)}), bf16[64,2,512]{2,1,0:T(2,128)(2,1)S(1)}, u32[]{:S(2)}, u32[]{:S(2)}) async-start(bf16[64,2,512]{2,1,0:T(2,128)(2,1)} %reshape.241), calls=%async_computation.2 | async-start | bytes 262144 | tf_op jit(solution)/shard_map/all_to_all | solution.py:141
  146.3 10.7 %all-to-all-start.7 = ((bf16[2,2,16384]{2,1,0:T(2,128)(2,1)}), bf16[2,2,16384]{2,1,0:T(2,128)(2,1)S(1)}, u32[]{:S(2)}, u32[]{:S(2)}) async-start(bf16[2,2,16384]{2,1,0:T(2,128)(2,1)} %reshape.239), calls=%async_computation.7 | async-start | bytes 262144 | tf_op jit(solution)/shard_map/all_to_all | solution.py:109
  157.0 4.5 %all-to-all-start.3 = ((bf16[2,2,16384]{2,1,0:T(2,128)(2,1)}), bf16[2,2,16384]{2,1,0:T(2,128)(2,1)S(1)}, u32[]{:S(2)}, u32[]{:S(2)}) async-start(bf16[2,2,16384]{2,1,0:T(2,128)(2,1)} %reshape.243), calls=%async_computation.3 | async-start | bytes 262144 | tf_op jit(solution)/shard_map/all_to_all | solution.py:144
where the time goes:
time: 163 us
  waiting for transfers between devices  74.9 us (46%)
  starting transfers between devices  66.2 us (41%)
  local copies, waits for them, and re-layouts  13.7 us (8%)
  other arithmetic  4.38 us (3%)
  matrix products  3.12 us (2%)
    all_to_all x2, starting transfers between devices, send_queries(): lax.all_to_all(to_heads(field, heads, copies), 'patch', split_axis=0, con...  26.3 us
    all_to_all x2, waiting for transfers between devices, send_queries(): lax.all_to_all(to_heads(field, heads, copies), 'patch', split_axis=0, con...  20.6 us
    all_to_all x1, waiting for transfers between devices, body(): lax.all_to_all(pairs_to_heads(keys_values[0, 0], heads, copies), 'patch',...  17.3 us
    all_to_all x1, waiting for transfers between devices, body(): lax.all_to_all(pairs_to_heads(keys_values[0, 1], heads, copies), 'patch',...  15.3 us
    all_to_all x1, starting transfers between devices, body(): lax.all_to_all(pairs_to_heads(keys_values[0, 0], heads, copies), 'patch',...  11.6 us
    all_to_all x1, waiting for transfers between devices, body(): lax.all_to_all(first, 'patch', split_axis=1, concat_axis=0, tiled=True)  11.5 us
    all_to_all x1, waiting for transfers between devices, body(): lax.all_to_all(second, 'patch', split_axis=1, concat_axis=0, tiled=True)  9.37 us
    all_to_all x1, starting transfers between devices, guide(): lax.all_to_all(halves, 'cfg', split_axis=2, concat_axis=2, tiled=True)  8.75 us
  transfers between devices with their start and end apart: 8, of which 7 were waited for; matrix products, arithmetic and copies ran while one was open for 10% of the time, Pallas kernels for 0%

commit v1 on v0

v1 whole, which is shorter than its diff:
```python
import math

import jax
import jax.numpy as jnp
from jax import lax
from jax.experimental import pallas as pl
from jax.experimental.pallas import tpu as pltpu
from jax.sharding import PartitionSpec as P

HEADS = 32
DEPTH = 128
COPIES = 2
TOK = 16
HALF = TOK // COPIES
N_PATCH = 64
TOKENS = N_PATCH * TOK
GROUP = 8
FACTOR = math.log2(math.e) / math.sqrt(DEPTH)
BF16 = jnp.bfloat16
F32 = jnp.float32


def head_of(ref, step, h):
    return ref[step, :, h * DEPTH : (h + 1) * DEPTH]


def pack_kernel(q_ref, kv_ref, out_ref):
    for h in range(HEADS):
        first = head_of(q_ref, 0, h)
        second = head_of(q_ref, 1, h)
        key = head_of(kv_ref, 0, h)
        value = head_of(kv_ref, 1, h)
        for copy in range(COPIES):
            rows = slice(copy * HALF, (copy + 1) * HALF)
            chunk = copy * HEADS + h
            out_ref[chunk, 0:16, :] = jnp.concatenate([first[rows], second[rows]], 0)
            out_ref[chunk, 16:32, :] = key
            out_ref[chunk, 32:48, :] = value


def pieces(value):
    high = value.astype(BF16).astype(F32)
    rest = value - high
    mid = rest.astype(BF16).astype(F32)
    return high, mid, rest - mid


def attend_kernel(x_ref, out_ref):
    keys = x_ref[:, 16:32, :].reshape(TOKENS, DEPTH)
    values = x_ref[:, 32:48, :].reshape(TOKENS, DEPTH)
    n = GROUP * TOK
    row = lax.broadcasted_iota(jnp.int32, (n, n), 0)
    col = lax.broadcasted_iota(jnp.int32, (n, n), 1)
    own = jnp.logical_and(row // TOK == col // TOK, row % TOK >= HALF)
    lane = lax.broadcasted_iota(jnp.int32, (GROUP, HALF, DEPTH), 2)
    for g in range(N_PATCH // GROUP):
        patches = slice(g * GROUP, (g + 1) * GROUP)
        query = x_ref[patches, 0:16, :].reshape(n, DEPTH)
        score = lax.dot_general(
            query, keys, (((1,), (1,)), ((), ())), preferred_element_type=F32
        )
        near = jnp.where(own, -jnp.inf, score[:, g * n : (g + 1) * n])
        parts = [score[:, : g * n], near, score[:, (g + 1) * n :]]
        score = jnp.concatenate([p for p in parts if p.shape[1]], axis=1)
        top = jnp.max(score, axis=1, keepdims=True)
        weight = jnp.exp2((score - top) * FACTOR)
        total = jnp.sum(weight, axis=1, keepdims=True)
        summed = jnp.dot(weight.astype(BF16), values, preferred_element_type=F32)
        attn = (summed / total).reshape(GROUP, 2, HALF, DEPTH)
        out_ref[patches, 0] = attn[:, 0].astype(BF16)
        out_ref[patches, 1] = attn[:, 1].astype(BF16)
        top = jnp.broadcast_to(top, (n, DEPTH)).reshape(GROUP, 2, HALF, DEPTH)[:, 1]
        total = jnp.broadcast_to(total, (n, DEPTH)).reshape(GROUP, 2, HALF, DEPTH)[:, 1]
        stats = jnp.zeros((GROUP, HALF, DEPTH), F32)
        for i, piece in enumerate(pieces(top) + pieces(total)):
            stats = jnp.where(lane == i, piece, stats)
        out_ref[patches, 2] = stats.astype(BF16)


def local_kernel(q_ref, kv_ref, sum_ref, top_ref, total_ref):
    n = GROUP * TOK
    row = lax.broadcasted_iota(jnp.int32, (n, n), 0)
    col = lax.broadcasted_iota(jnp.int32, (n, n), 1)
    same = row // TOK == col // TOK

    def rows(ref, step, g):
        return jnp.concatenate(
            [head_of(ref, step, h) for h in range(g * GROUP, (g + 1) * GROUP)], 0
        )

    for g in range(HEADS // GROUP):
        score = lax.dot_general(
            rows(q_ref, 1, g),
            rows(kv_ref, 0, g),
            (((1,), (1,)), ((), ())),
            preferred_element_type=F32,
        )
        score = jnp.where(same, score, -jnp.inf)
        top = jnp.max(score, axis=1, keepdims=True)
        weight = jnp.exp2((score - top) * FACTOR)
        total = jnp.sum(weight, axis=1, keepdims=True)
        summed = jnp.dot(
            weight.astype(BF16), rows(kv_ref, 1, g), preferred_element_type=F32
        )
        for ref, value in ((sum_ref, summed), (top_ref, top), (total_ref, total)):
            value = jnp.broadcast_to(value, (n, DEPTH)).reshape(GROUP, COPIES, HALF, DEPTH)
            for copy in range(COPIES):
                start = copy * HEADS + g * GROUP
                ref[start : start + GROUP] = value[:, copy]


def merge_kernel(y_ref, sum_ref, top_ref, total_ref, out_ref, held):
    n = N_PATCH * HALF
    held[0:n] = y_ref[:, 0].astype(F32).reshape(n, DEPTH)
    stats = y_ref[:, 2].astype(F32).reshape(n, DEPTH).astype(BF16)
    row = lax.broadcasted_iota(jnp.int32, (DEPTH, 2 * DEPTH), 0)
    col = lax.broadcasted_iota(jnp.int32, (DEPTH, 2 * DEPTH), 1)
    pick = jnp.where(
        jnp.logical_and(row < 6, row // 3 == col // DEPTH), 1.0, 0.0
    ).astype(BF16)
    far = jnp.dot(stats, pick, preferred_element_type=F32)
    far_top, far_total = far[:, :DEPTH], far[:, DEPTH:]
    near_top = top_ref[...].reshape(n, DEPTH)
    top = jnp.maximum(far_top, near_top)
    far_scale = jnp.exp2((far_top - top) * FACTOR) * far_total
    near_scale = jnp.exp2((near_top - top) * FACTOR)
    total = far_scale + near_scale * total_ref[...].reshape(n, DEPTH)
    far_attn = y_ref[:, 1].astype(F32).reshape(n, DEPTH)
    summed = far_scale * far_attn + near_scale * sum_ref[...].reshape(n, DEPTH)
    held[n : 2 * n] = summed / total
    for step in range(2):
        for copy in range(COPIES):
            for t in range(HALF):
                start = step * n + copy * HEADS * HALF + t
                out_ref[step, copy * HALF + t] = held[
                    pl.ds(start, HEADS, stride=HALF), :
                ].astype(BF16)


def guide_kernel(both_ref, gate_ref, out_ref):
    upper = lax.axis_index("cfg") == 1
    half = DEPTH // 2
    for step in range(2):
        gate = gate_ref[step]
        for t in range(TOK):
            cond = both_ref[0, step, t].astype(F32)
            uncond = both_ref[1, step, t].astype(F32)
            mixed = gate * (uncond + 5.0 * (cond - uncond))
            out_ref[step, t] = jnp.where(upper, mixed[:, half:], mixed[:, :half]).astype(BF16)


QUERIES = pl.BlockSpec((None, 2, TOK, HEADS * DEPTH), lambda i: (0, 0, 0, 0))


def pairs(step):
    return pl.BlockSpec((None, None, 2, TOK, HEADS * DEPTH), lambda i: (0, step, 0, 0, 0))


def call(kernel, out, args, specs=None, scratch=(), flops=0):
    many = isinstance(out, list)
    shapes = out if many else [out]
    moved = sum(a.size * a.dtype.itemsize for a in list(args) + list(shapes))
    vmem = pl.BlockSpec(memory_space=pltpu.VMEM)
    return pl.pallas_call(
        kernel,
        grid=(1,),
        out_shape=out,
        in_specs=specs or [vmem] * len(args),
        out_specs=[vmem] * len(shapes) if many else vmem,
        scratch_shapes=list(scratch),
        cost_estimate=pl.CostEstimate(flops=flops, bytes_accessed=moved, transcendentals=0),
        compiler_params=pltpu.CompilerParams(vmem_limit_bytes=32 << 20),
    )(*args)


def body(queries, keys_values, timesteps, gate_table):
    shape = jax.ShapeDtypeStruct
    fields = (queries, keys_values)
    sent = call(pack_kernel, shape((N_PATCH, 48, DEPTH), BF16), fields, [QUERIES, pairs(0)])
    held = lax.all_to_all(sent, "patch", split_axis=0, concat_axis=0, tiled=True)
    part = shape((N_PATCH, HALF, DEPTH), F32)
    near = call(local_kernel, [part] * 3, fields, [QUERIES, pairs(1)])
    gates = jnp.take(gate_table, timesteps, axis=0, mode="clip").reshape(2, HEADS, DEPTH)
    far = call(attend_kernel, shape((N_PATCH, 3, HALF, DEPTH), BF16), (held,))
    back = lax.all_to_all(far, "patch", split_axis=0, concat_axis=0, tiled=True)
    attn = call(
        merge_kernel,
        shape((2, TOK, HEADS, DEPTH), BF16),
        (back, *near),
        scratch=[pltpu.VMEM((2 * N_PATCH * HALF, DEPTH), F32)],
    )
    both = lax.all_gather(attn, "cfg", axis=0, tiled=False)
    return call(guide_kernel, shape((2, TOK, HEADS, DEPTH // 2), BF16), (both, gates))


def solution(mesh):
    placed = (
        P("cfg", None, ("clip", "patch"), None),
        P("cfg", None, None, ("clip", "patch"), None),
        P("clip"),
        P(),
    )
    return jax.shard_map(
        body,
        mesh=mesh,
        in_specs=placed,
        out_specs=P(None, ("clip", "patch"), None, "cfg"),
        check_vma=False,
    )
```

time: 163 us -> 82.2 us (0.50)
  waiting for transfers between devices: 74.9 us -> 12.9 us
  starting transfers between devices: 66.2 us -> 9.92 us
  blocking collectives: 0 us -> 48.7 us
  local copies, waits for them, and re-layouts: 13.7 us -> 2.67 us
  Pallas kernels: 0 us -> 7.13 us
  other arithmetic: 4.38 us -> 0.01 us
  matrix products: 3.12 us -> 0 us
    all_to_all x8 -> x1, waiting for transfers between devices: 74.9 us -> 12.9 us  [body(): back = lax.all_to_all(far, 'patch', split_axis=0, concat_axis=0, tiled=True)]
    all_to_all x8 -> x1, starting transfers between devices: 66.2 us -> 9.92 us  [body(): back = lax.all_to_all(far, 'patch', split_axis=0, concat_axis=0, tiled=True)]
    all_to_all x0 -> x1, blocking collectives: none -> 42.3 us  [body(): lax.all_to_all(sent, 'patch', split_axis=0, concat_axis=0, tiled=True)]
    pallas_call x0 -> x5, Pallas kernels: none -> 7.13 us  [call(): pl.pallas_call(kernel, grid=(1,), out_shape=out, in_specs=specs or [vmem]...]
    all_gather x0 -> x1, blocking collectives: none -> 6.46 us  [body(): both = lax.all_gather(attn, 'cfg', axis=0, tiled=False)]
    unnamed x17 -> x13, local copies, waits for them, and re-layouts: 5.59 us -> 2.09 us
    dot_general x7 -> x0, matrix products: 3.12 us -> none  [the longest x2 1.05 us: one_block(): jnp.einsum('hqd,hkd->hqk', block, keys_all[:, 0], preferred_element_type=...]
    unnamed x2 -> x0, other arithmetic: 2.9 us -> none
  transfers between devices with their start and end apart: 8 -> 1, of which waited for: 7 -> 1; matrix products, arithmetic and copies ran while one was open for 10% -> 1% of each run, Pallas kernels for 0% -> 1%
where the time goes in v1:
time: 82.2 us; the launch traced here: 81.5 us
  blocking collectives  48.7 us (59%)
  waiting for transfers between devices  12.9 us (16%)
  starting transfers between devices  9.92 us (12%)
  Pallas kernels  7.13 us (9%)
  local copies, waits for them, and re-layouts  2.67 us (3%)
    all_to_all x1, blocking collectives, body(): lax.all_to_all(sent, 'patch', split_axis=0, concat_axis=0, tiled=True)  42.3 us
    all_to_all x1, waiting for transfers between devices, body(): back = lax.all_to_all(far, 'patch', split_axis=0, concat_axis=0, tiled=True)  12.9 us
    all_to_all x1, starting transfers between devices, body(): back = lax.all_to_all(far, 'patch', split_axis=0, concat_axis=0, tiled=True)  9.92 us
    pallas_call x5, Pallas kernels, call(): pl.pallas_call(kernel, grid=(1,), out_shape=out, in_specs=specs or [vmem]...  7.13 us
    all_gather x1, blocking collectives, body(): both = lax.all_gather(attn, 'cfg', axis=0, tiled=False)  6.46 us
    unnamed x13, local copies, waits for them, and re-layouts  2.09 us
  transfers between devices with their start and end apart: 1, of which 1 were waited for; matrix products, arithmetic and copies ran while one was open for 1% of the time, Pallas kernels for 1%

profile of v1, /device:TPU:1, one launch (start us, length us, event | category | flops | bytes accessed | tf_op | source)
XLA Modules:
  0.0 81.5 jit_solution(9738561281568351670)
XLA Ops:
  0.0 0.0 copy-start
  0.0 0.0 copy-start.1
  0.0 1.1 %copy-done.1 = bf16[1,2,2,16,4096]{4,3,2,1,0:T(8,128)(2,1)S(1)} copy-done((bf16[1,2,2,16,4096]{4,3,2,1,0:T(8,128)(2,1)S(1)}, bf16[1,2,2,16,4096]{4,3,2,1,0:T(8,128)(2,1)}, u32[]{:S(2)}) %copy-start.1) | copy-done | bytes 524312
  1.1 0.0 copy-start.3
  1.1 0.9 %copy-done.3 = bf16[1,2,16,4096]{3,2,1,0:T(8,128)(2,1)S(1)} copy-done((bf16[1,2,16,4096]{3,2,1,0:T(8,128)(2,1)S(1)}, bf16[1,2,16,4096]{3,2,1,0:T(8,128)(2,1)}, u32[]{:S(2)}) %copy-start.3) | copy-done | bytes 262168
  2.1 0.1 shard_map.46
  2.2 42.3 %all_to_all.10.x_ref = bf16[64,48,128]{2,1,0:T(8,128)(2,1)S(1)} all-to-all(bf16[64,48,128]{2,1,0:T(8,128)(2,1)S(1)} %shard_map.46), channel_id=1, replica_groups=mesh['clip'=4,'cfg'=2,'patch'=64] {'patch'}, dimensions={0} | all-to-all | bytes 1572864 | tf_op jit(solution)/shard_map/all_to_all | solution.py:180
  44.5 3.7 %shard_map.47 = bf16[64,3,8,128]{3,2,1,0:T(8,128)(2,1)} custom-call(bf16[64,48,128]{2,1,0:T(8,128)(2,1)S(1)} %all_to_all.10.x_ref), custom_call_target="tpu_custom_call" | custom-call | bytes 1179648 | tf_op jit(solution)/shard_map/pallas_call | solution.py:164
  48.2 0.0 copy-start.2
  48.2 0.0 copy-start.4
  48.2 9.9 %all-to-all-start.1 = ((bf16[64,3,8,128]{3,2,1,0:T(8,128)(2,1)}), bf16[64,3,8,128]{3,2,1,0:T(8,128)(2,1)S(1)}, u32[]{:S(2)}, u32[]{:S(2)}) async-start(bf16[64,3,8,128]{3,2,1,0:T(8,128)(2,1)} %shard_map.47), calls=%async_computation.1 | async-start | bytes 786432 | tf_op jit(solution)/shard_map/all_to_all | solution.py:185
  58.1 0.0 copy-done.2
  58.1 0.0 copy-done.4
  58.1 0.0 copy-start.5
  58.1 1.1 %shard_map.48 = (f32[64,8,128]{2,1,0:T(8,128)S(1)}, f32[64,8,128]{2,1,0:T(8,128)S(1)}, f32[64,8,128]{2,1,0:T(8,128)S(1)}) custom-call(bf16[1,2,16,4096]{3,2,1,0:T(8,128)(2,1)S(1)} %copy-done.4, bf16[1,2,2,16,4096]{4,3,2,1,0:T(8,128)(2,1)S(1)} %copy-done.2), custom_call_target="tpu_custom_call" | custom-call | bytes 1572864 | tf_op jit(solution)/shard_map/pallas_call | solution.py:164
  59.2 0.0 copy-done.5
  59.2 0.0 copy-done
  59.2 0.6 gather_fusion
  59.8 12.9 %all-to-all-done.1.y_ref = bf16[64,3,8,128]{3,2,1,0:T(8,128)(2,1)S(1)} async-done(((bf16[64,3,8,128]{3,2,1,0:T(8,128)(2,1)}), bf16[64,3,8,128]{3,2,1,0:T(8,128)(2,1)S(1)}, u32[]{:S(2)}, u32[]{:S(2)}) %all-to-all-start.1) | async-done | bytes 393248 | tf_op jit(solution)/shard_map/all_to_all | solution.py:185
  72.8 0.3 shard_map.49
  73.1 6.5 %all-gather = bf16[4,16,32,128]{3,2,1,0:T(8,128)(2,1)S(1)} all-gather(bf16[2,16,32,128]{3,2,1,0:T(8,128)(2,1)S(1)} %shard_map.49), channel_id=2, replica_groups=mesh['clip'=4,'cfg'=2,'patch'=64] {'cfg'}, dimensions={0}, use_global_device_ids=true | all-gather | bytes 786432 | tf_op jit(solution)/shard_map/all_gather | solution.py:192
  79.6 1.9 %shard_map.50 = bf16[2,16,32,64]{3,2,1,0:T(8,128)(2,1)} custom-call(bf16[2,2,16,32,128]{4,3,2,1,0:T(8,128)(2,1)S(1)} %bitcast.5, f32[2,32,128]{2,1,0:T(8,128)S(1)} %bitcast.6), custom_call_target="tpu_custom_call" | custom-call | bytes 688128 | tf_op jit(solution)/shard_map/pallas_call | solution.py:164
  (2 shorter events, 0.0 us)
Async XLA Ops:
  0.0 59.2 %copy-start = (f32[50,4096]{1,0:T(8,128)S(1)}, f32[50,4096]{1,0:T(8,128)}, u32[]{:S(2)}) copy-start(f32[50,4096]{1,0:T(8,128)} %param.7) | copy-start | bytes 2457604
  0.0 1.1 %copy-start.1 = (bf16[1,2,2,16,4096]{4,3,2,1,0:T(8,128)(2,1)S(1)}, bf16[1,2,2,16,4096]{4,3,2,1,0:T(8,128)(2,1)}, u32[]{:S(2)}) copy-start(bf16[1,2,2,16,4096]{4,3,2,1,0:T(8,128)(2,1)} %kv_ref.3) | copy-start | bytes 1572868
  1.1 0.9 %copy-start.3 = (bf16[1,2,16,4096]{3,2,1,0:T(8,128)(2,1)S(1)}, bf16[1,2,16,4096]{3,2,1,0:T(8,128)(2,1)}, u32[]{:S(2)}) copy-start(bf16[1,2,16,4096]{3,2,1,0:T(8,128)(2,1)} %q_ref.3) | copy-start | bytes 786436
  48.2 9.9 %copy-start.2 = (bf16[1,2,2,16,4096]{4,3,2,1,0:T(8,128)(2,1)S(1)}, bf16[1,2,2,16,4096]{4,3,2,1,0:T(8,128)(2,1)}, u32[]{:S(2)}) copy-start(bf16[1,2,2,16,4096]{4,3,2,1,0:T(8,128)(2,1)} %kv_ref.3) | copy-start | bytes 1572868
  48.2 9.9 %copy-start.4 = (bf16[1,2,16,4096]{3,2,1,0:T(8,128)(2,1)S(1)}, bf16[1,2,16,4096]{3,2,1,0:T(8,128)(2,1)}, u32[]{:S(2)}) copy-start(bf16[1,2,16,4096]{3,2,1,0:T(8,128)(2,1)} %q_ref.3) | copy-start | bytes 786436
  48.2 24.6 %all-to-all-start.1 = ((bf16[64,3,8,128]{3,2,1,0:T(8,128)(2,1)}), bf16[64,3,8,128]{3,2,1,0:T(8,128)(2,1)S(1)}, u32[]{:S(2)}, u32[]{:S(2)}) async-start(bf16[64,3,8,128]{3,2,1,0:T(8,128)(2,1)} %shard_map.47), calls=%async_computation.1 | async-start | bytes 786432 | tf_op jit(solution)/shard_map/all_to_all | solution.py:185
  58.1 1.1 %copy-start.5 = (s32[2]{0:T(128)S(1)}, s32[2]{0:T(128)}, u32[]{:S(2)}) copy-start(s32[2]{0:T(128)} %param.6) | copy-start | bytes 28

commit v2 on v1

v2 whole, which is shorter than its diff:
```python
import math

import jax
import jax.numpy as jnp
from jax import lax
from jax.experimental import pallas as pl
from jax.experimental.pallas import tpu as pltpu
from jax.sharding import PartitionSpec as P

HEADS = 32
DEPTH = 128
HALF = DEPTH // 2
TOK = 16
SIDES = 2
NEAR = HEADS * TOK
ROWS = 2 * NEAR
GROUP = 8
BLOCK = 256
FACTOR = math.log2(math.e) / math.sqrt(DEPTH)
BF16 = jnp.bfloat16
F32 = jnp.float32
SHAPE = jax.ShapeDtypeStruct


def dot_t(a, b):
    return lax.dot_general(a, b, (((1,), (1,)), ((), ())), preferred_element_type=F32)


def pack_kernel(q_ref, kv_ref, out_ref, held, sems):
    fields = [q_ref.at[0, 0], q_ref.at[0, 1], kv_ref.at[0, 0, 0], kv_ref.at[0, 0, 1]]
    copies = [
        pltpu.make_async_copy(field, held.at[i], sems.at[i]) for i, field in enumerate(fields)
    ]
    for copy in copies:
        copy.start()
    for i, copy in enumerate(copies):
        copy.wait()
        for h in range(HEADS):
            out_ref[h, i * TOK : (i + 1) * TOK, :] = held[i, :, h * DEPTH : (h + 1) * DEPTH]


def split_value(value):
    high = value.astype(BF16).astype(F32)
    rest = value - high
    mid = rest.astype(BF16).astype(F32)
    return high, mid, rest - mid


def write_stats(top, total):
    n = top.shape[0] // TOK
    lane = lax.broadcasted_iota(jnp.int32, (n, TOK // 2, DEPTH), 2)
    both = []
    for value in (top, total):
        wide = jnp.broadcast_to(value, (n * TOK, DEPTH)).reshape(n, 2, TOK // 2, DEPTH)
        both.extend(split_value(jnp.where(lane < HALF, wide[:, 0], wide[:, 1])))
    stats = jnp.zeros((n, TOK // 2, DEPTH), F32)
    for i, piece in enumerate(both):
        stats = jnp.where(lane % HALF == i, piece, stats)
    return stats.astype(BF16)


def read_stats(stats):
    n = stats.shape[0]
    row = lax.broadcasted_iota(jnp.int32, (DEPTH, 4 * DEPTH), 0)
    part = lax.broadcasted_iota(jnp.int32, (DEPTH, 4 * DEPTH), 1) // DEPTH
    first = part % 2 * HALF + part // 2 * 3
    pick = jnp.where(jnp.logical_and(row >= first, row < first + 3), 1.0, 0.0).astype(BF16)
    flat = stats.astype(F32).reshape(n * TOK // 2, DEPTH).astype(BF16)
    wide = jnp.dot(flat, pick, preferred_element_type=F32)
    parts = [
        wide[:, i * DEPTH : (i + 1) * DEPTH].reshape(n, 1, TOK // 2, DEPTH) for i in range(4)
    ]
    top = jnp.concatenate(parts[:2], 1).reshape(n * TOK, DEPTH)
    total = jnp.concatenate(parts[2:], 1).reshape(n * TOK, DEPTH)
    return top, total


def local_kernel(q_ref, kv_ref, out_ref):
    n = GROUP * TOK
    row = lax.broadcasted_iota(jnp.int32, (n, n), 0)
    col = lax.broadcasted_iota(jnp.int32, (n, n), 1)
    same = row // TOK == col // TOK

    for g in range(HEADS // GROUP):
        heads = range(g * GROUP, (g + 1) * GROUP)
        query, key, value = (
            jnp.concatenate([ref[i, :, h * DEPTH : (h + 1) * DEPTH] for h in heads], 0)
            for ref, i in ((q_ref, 0), (kv_ref, 0), (kv_ref, 1))
        )
        score = jnp.where(same, dot_t(query, key), -jnp.inf)
        top = jnp.max(score, axis=1, keepdims=True)
        weight = jnp.exp2((score - top) * FACTOR)
        total = jnp.sum(weight, axis=1, keepdims=True)
        summed = jnp.dot(weight.astype(BF16), value, preferred_element_type=F32)
        here = slice(g * GROUP, (g + 1) * GROUP)
        out_ref[here, 0:TOK] = (summed / total).astype(BF16).reshape(GROUP, TOK, DEPTH)
        out_ref[here, TOK:] = write_stats(top, total)


def own_half_kernel(x_ref, sum_ref, top_ref, total_ref):
    keys = x_ref[:, 2 * TOK : 3 * TOK, :].reshape(NEAR, DEPTH)
    values = x_ref[:, 3 * TOK :, :].reshape(NEAR, DEPTH)
    row = lax.broadcasted_iota(jnp.int32, (BLOCK, BLOCK), 0)
    col = lax.broadcasted_iota(jnp.int32, (BLOCK, BLOCK), 1)
    same = row // TOK == col // TOK
    for step in range(2):
        for i in range(NEAR // BLOCK):
            patches = slice(i * BLOCK // TOK, (i + 1) * BLOCK // TOK)
            query = x_ref[patches, step * TOK : (step + 1) * TOK, :].reshape(BLOCK, DEPTH)
            score = dot_t(query, keys)
            if step == 1:
                near = jnp.where(same, -jnp.inf, score[:, i * BLOCK : (i + 1) * BLOCK])
                parts = [score[:, : i * BLOCK], near, score[:, (i + 1) * BLOCK :]]
                score = jnp.concatenate([p for p in parts if p.shape[1]], axis=1)
            top = jnp.max(score, axis=1, keepdims=True)
            weight = jnp.exp2((score - top) * FACTOR)
            here = slice(step * NEAR + i * BLOCK, step * NEAR + (i + 1) * BLOCK)
            sum_ref[here] = jnp.dot(weight.astype(BF16), values, preferred_element_type=F32)
            top_ref[here] = top
            total_ref[here] = jnp.sum(weight, axis=1, keepdims=True)


def other_half_kernel(x_ref, other_ref, sum_ref, top_ref, total_ref, out_ref):
    keys = other_ref[:, 0:TOK, :].reshape(NEAR, DEPTH)
    values = other_ref[:, TOK:, :].reshape(NEAR, DEPTH)
    lower = lax.broadcasted_iota(jnp.int32, (BLOCK, DEPTH), 1) < HALF
    n = BLOCK // TOK
    for i in range(NEAR // BLOCK):
        patches = slice(i * n, (i + 1) * n)
        attn = []
        for step in range(2):
            query = x_ref[patches, step * TOK : (step + 1) * TOK, :].reshape(BLOCK, DEPTH)
            score = dot_t(query, keys)
            here = slice(step * NEAR + i * BLOCK, step * NEAR + (i + 1) * BLOCK)
            old_top = top_ref[here]
            top = jnp.maximum(jnp.max(score, axis=1, keepdims=True), old_top)
            weight = jnp.exp2((score - top) * FACTOR)
            old = jnp.exp2((old_top - top) * FACTOR)
            total = jnp.sum(weight, axis=1, keepdims=True) + old * total_ref[here]
            summed = jnp.dot(weight.astype(BF16), values, preferred_element_type=F32)
            attn.append((summed + old * sum_ref[here]) / total)
        first, second = attn
        chunks = (
            jnp.where(lower, first, pltpu.roll(second, HALF, 1)),
            jnp.where(lower, pltpu.roll(first, HALF, 1), second),
        )
        stats = write_stats(top, total)
        for core, chunk in enumerate(chunks):
            at = slice(core * HEADS + i * n, core * HEADS + (i + 1) * n)
            out_ref[at, 0:TOK] = chunk.astype(BF16).reshape(n, TOK, DEPTH)
            out_ref[at, TOK:] = stats


def merge_kernel(y_ref, near_ref, gate_ref, out_ref, held):
    upper = lax.axis_index("cfg") == 1
    lower = lax.broadcasted_iota(jnp.int32, (NEAR, DEPTH), 1) < HALF

    def branch(b):
        heads = slice(b * HEADS, (b + 1) * HEADS)
        far = y_ref[heads, 0:TOK].astype(F32).reshape(NEAR, DEPTH)
        near = near_ref[b, :, 0:TOK].astype(F32).reshape(NEAR, DEPTH)
        near = jnp.where(upper, near, pltpu.roll(near, HALF, 1))
        far_top, far_total = read_stats(y_ref[heads, TOK:])
        near_top, near_total = read_stats(near_ref[b, :, TOK:])
        top = jnp.maximum(far_top, near_top)
        far_share = jnp.exp2((far_top - top) * FACTOR) * far_total
        near_share = jnp.exp2((near_top - top) * FACTOR) * near_total
        both = (far_share * far + near_share * near) / (far_share + near_share)
        return jnp.where(lower, far, both).astype(BF16).astype(F32)

    cond = branch(0)
    uncond = branch(1)
    mixed = (uncond + 5.0 * (cond - uncond)).reshape(HEADS, TOK, DEPTH)
    held[...] = (gate_ref[...].reshape(HEADS, 1, DEPTH) * mixed).reshape(NEAR, DEPTH)
    for t in range(TOK):
        rows = held[pl.ds(t, HEADS, stride=TOK), :]
        out_ref[0, t] = rows[:, :HALF].astype(BF16)
        out_ref[1, t] = rows[:, HALF:].astype(BF16)


def call(kernel, out, args, specs=None, scratch=(), flops=0):
    many = isinstance(out, list)
    shapes = out if many else [out]
    moved = sum(a.size * a.dtype.itemsize for a in list(args) + list(shapes))
    vmem = pl.BlockSpec(memory_space=pltpu.VMEM)
    return pl.pallas_call(
        kernel,
        grid=(1,),
        out_shape=out,
        in_specs=specs or [vmem] * len(args),
        out_specs=[vmem] * len(shapes) if many else vmem,
        scratch_shapes=list(scratch),
        cost_estimate=pl.CostEstimate(flops=flops, bytes_accessed=moved, transcendentals=0),
        compiler_params=pltpu.CompilerParams(vmem_limit_bytes=32 << 20),
    )(*args)


def body(queries, keys_values, timesteps, gate_table):
    width = HEADS * DEPTH
    sides = [[SIDES * i + side for i in range(HEADS)] for side in range(SIDES)]
    patches = SIDES * HEADS
    cores = [
        [core * patches + patch for core in range(2) for patch in side] for side in sides
    ]
    whole = pl.BlockSpec(memory_space=pltpu.HBM)
    sent = call(
        pack_kernel,
        SHAPE((HEADS, 4 * TOK, DEPTH), BF16),
        (queries, keys_values),
        [whole, whole],
        [pltpu.VMEM((4, TOK, width), BF16), pltpu.SemaphoreType.DMA((4,))],
    )
    held = lax.all_to_all(
        sent, "patch", split_axis=0, concat_axis=0, tiled=True, axis_index_groups=sides
    )
    near = call(
        local_kernel,
        SHAPE((HEADS, 3 * TOK // 2, DEPTH), BF16),
        (queries, keys_values),
        [
            pl.BlockSpec((None, 1, TOK, width), lambda i: (0, 1, 0, 0)),
            pl.BlockSpec((None, None, 2, TOK, width), lambda i: (0, 1, 0, 0, 0)),
        ],
    )
    near = lax.all_gather(near, "cfg", axis=0, tiled=False)
    gates = jnp.take(gate_table, timesteps, axis=0, mode="clip").reshape(2, HEADS, 2, HALF)
    gate = lax.dynamic_index_in_dim(gates, lax.axis_index("cfg"), 2, keepdims=False)
    gate = jnp.concatenate([gate[0], gate[1]], axis=1)
    other = lax.ppermute(
        held[:, 2 * TOK :, :], "patch", [(i, i ^ 1) for i in range(patches)]
    )
    column = SHAPE((ROWS, 1), F32)
    own = call(
        own_half_kernel,
        [SHAPE((ROWS, DEPTH), F32), column, column],
        (held,),
        flops=4 * ROWS * NEAR * DEPTH,
    )
    far = call(
        other_half_kernel,
        SHAPE((2 * HEADS, 3 * TOK // 2, DEPTH), BF16),
        (held, other, *own),
        flops=4 * ROWS * NEAR * DEPTH,
    )
    back = lax.all_to_all(
        far, ("cfg", "patch"), split_axis=0, concat_axis=0, tiled=True, axis_index_groups=cores
    )
    return call(
        merge_kernel,
        SHAPE((2, TOK, HEADS, HALF), BF16),
        (back, near, gate),
        scratch=[pltpu.VMEM((NEAR, DEPTH), F32)],
    )


def solution(mesh):
    placed = (
        P("cfg", None, ("clip", "patch"), None),
        P("cfg", None, None, ("clip", "patch"), None),
        P("clip"),
        P(),
    )
    return jax.shard_map(
        body,
        mesh=mesh,
        in_specs=placed,
        out_specs=P(None, ("clip", "patch"), None, "cfg"),
        check_vma=False,
    )
```

time: 82.2 us -> 77.2 us (0.939)
  blocking collectives: 48.7 us -> 31.9 us
  starting transfers between devices: 9.92 us -> 20.5 us
    all_to_all x1, blocking collectives: 42.3 us -> 29.8 us  [body(): lax.all_to_all(sent, 'patch', split_axis=0, concat_axis=0, tiled=True, ax...]
    ppermute x0 -> x1, starting transfers between devices: none -> 7.45 us  [body(): lax.ppermute(held[:, 2 * TOK:, :], 'patch', [(i, i ^ 1) for i in range(pa...]
    all_gather x1, blocking collectives: 6.46 us -> 2.09 us  [body(): near = lax.all_gather(near, 'cfg', axis=0, tiled=False)]
    all_to_all x1, starting transfers between devices: 9.92 us -> 13.1 us  [body(): lax.all_to_all(far, ('cfg', 'patch'), split_axis=0, concat_axis=0, tiled=...]
    all_to_all x1, waiting for transfers between devices: 12.9 us -> 9.92 us  [body(): lax.all_to_all(far, ('cfg', 'patch'), split_axis=0, concat_axis=0, tiled=...]
    ppermute x0 -> x1, waiting for transfers between devices: none -> 2.75 us  [body(): lax.ppermute(held[:, 2 * TOK:, :], 'patch', [(i, i ^ 1) for i in range(pa...]
    unnamed x13 -> x12, local copies, waits for them, and re-layouts: 2.09 us -> 2.73 us
  transfers between devices with their start and end apart: 1 -> 2, of which waited for: 1 -> 2; matrix products, arithmetic and copies ran while one was open for 1% -> 1% of each run, Pallas kernels for 1% -> 3%
where the time goes in v2:
time: 77.2 us; the launch traced here: 76.2 us
  blocking collectives  31.9 us (41%)
  starting transfers between devices  20.5 us (27%)
  waiting for transfers between devices  12.7 us (16%)
  Pallas kernels  7.47 us (10%)
  local copies, waits for them, and re-layouts  3.47 us (4%)
    all_to_all x1, blocking collectives, body(): lax.all_to_all(sent, 'patch', split_axis=0, concat_axis=0, tiled=True, ax...  29.8 us
    all_to_all x1, starting transfers between devices, body(): lax.all_to_all(far, ('cfg', 'patch'), split_axis=0, concat_axis=0, tiled=...  13.1 us
    all_to_all x1, waiting for transfers between devices, body(): lax.all_to_all(far, ('cfg', 'patch'), split_axis=0, concat_axis=0, tiled=...  9.92 us
    pallas_call x5, Pallas kernels, call(): pl.pallas_call(kernel, grid=(1,), out_shape=out, in_specs=specs or [vmem]...  7.47 us
    ppermute x1, starting transfers between devices, body(): lax.ppermute(held[:, 2 * TOK:, :], 'patch', [(i, i ^ 1) for i in range(pa...  7.45 us
    ppermute x1, waiting for transfers between devices, body(): lax.ppermute(held[:, 2 * TOK:, :], 'patch', [(i, i ^ 1) for i in range(pa...  2.75 us
    unnamed x12, local copies, waits for them, and re-layouts  2.73 us
    all_gather x1, blocking collectives, body(): near = lax.all_gather(near, 'cfg', axis=0, tiled=False)  2.09 us
  transfers between devices with their start and end apart: 2, of which 2 were waited for; matrix products, arithmetic and copies ran while one was open for 1% of the time, Pallas kernels for 3%

profile of v2, /device:TPU:1, one launch (start us, length us, event | category | flops | bytes accessed | tf_op | source)
XLA Modules:
  0.0 76.2 jit_solution(16074894394407556939)
XLA Ops:
  0.0 0.0 copy-start
  0.0 0.0 copy-start.1
  0.0 1.1 %copy-done.1 = bf16[1,2,2,16,4096]{4,3,2,1,0:T(8,128)(2,1)S(1)} copy-done((bf16[1,2,2,16,4096]{4,3,2,1,0:T(8,128)(2,1)S(1)}, bf16[1,2,2,16,4096]{4,3,2,1,0:T(8,128)(2,1)}, u32[]{:S(2)}) %copy-start.1) | copy-done | bytes 524312
  1.1 0.0 copy-start.3
  1.1 0.9 %copy-done.3 = bf16[1,2,16,4096]{3,2,1,0:T(8,128)(2,1)S(1)} copy-done((bf16[1,2,16,4096]{3,2,1,0:T(8,128)(2,1)S(1)}, bf16[1,2,16,4096]{3,2,1,0:T(8,128)(2,1)}, u32[]{:S(2)}) %copy-start.3) | copy-done | bytes 262168
  2.1 0.8 %shard_map.46 = bf16[32,64,128]{2,1,0:T(8,128)(2,1)S(1)} custom-call(bf16[1,2,16,4096]{3,2,1,0:T(8,128)(2,1)S(1)} %copy-done.3, bf16[1,2,2,16,4096]{4,3,2,1,0:T(8,128)(2,1)S(1)} %copy-done.1), custom_call_target="tpu_custom_call" | custom-call | bytes 1310720 | tf_op jit(solution)/shard_map/pallas_call | solution.py:186
  2.9 29.8 %all_to_all.10.x_ref = bf16[32,64,128]{2,1,0:T(8,128)(2,1)S(1)} all-to-all(bf16[32,64,128]{2,1,0:T(8,128)(2,1)S(1)} %shard_map.46), channel_id=1, replica_groups={{0,2,4,6,8,10,12,14,16,18,20,22,24,26,28,30,32,34,36,38,40,42,44,46,48,..., dimensions={0} | all-to-all | bytes 1048576 | tf_op jit(solution)/shard_map/all_to_all | solution.py:213
  32.7 7.5 %collective-permute-start = (bf16[32,32,128]{2,1,0:T(8,128)(2,1)S(1)}, bf16[32,32,128]{2,1,0:T(8,128)(2,1)S(1)}, u32[]{:S(2)}, u32[]{:S(2)}) collective-permute-start(bf16[32,32,128]{2,1,0:T(8,128)(2,1)S(1)} %slice.16), channel_id=1, source_target_pairs={{0,1},{1,0},{2,3},{3,2},{4,5},{5,4},{6,7},{7,6},{8,9},{9,8},{10,11... | collective-permute-start | bytes 786440 | tf_op jit(solution)/shard_map/ppermute | solution.py:229
  40.1 1.4 %shard_map.47 = (f32[1024,128]{1,0:T(8,128)S(1)}, f32[1024,1]{1,0:T(8,128)S(1)}, f32[1024,1]{1,0:T(8,128)S(1)}) custom-call(bf16[32,64,128]{2,1,0:T(8,128)(2,1)S(1)} %all_to_all.10.x_ref), custom_call_target="tpu_custom_call" | custom-call | flops 268435456 | bytes 1056768 | tf_op jit(solution)/shard_map/pallas_call | solution.py:186
  41.5 2.8 %collective-permute-done.other_ref = bf16[32,32,128]{2,1,0:T(8,128)(2,1)S(1)} collective-permute-done((bf16[32,32,128]{2,1,0:T(8,128)(2,1)S(1)}, bf16[32,32,128]{2,1,0:T(8,128)(2,1)S(1)}, u32[]{:S(2)}, u32[]{:S(2)}) %collective-permute-start) | collective-permute-done | bytes 262176 | tf_op jit(solution)/shard_map/ppermute | solution.py:229
  44.2 2.7 %shard_map.48 = bf16[64,24,128]{2,1,0:T(8,128)(2,1)} custom-call(bf16[32,64,128]{2,1,0:T(8,128)(2,1)S(1)} %all_to_all.10.x_ref, bf16[32,32,128]{2,1,0:T(8,128)(2,1)S(1)} %collective-permute-done.other_ref, f32[1024,128]{1,0:T(8,128)S(1)} %get-tuple-element.8.sum_ref, f32[1024,1]{1,0:T(8,128)S(1)} %get-tuple-element.9.top_ref, ...), custom_call_target="tpu_custom_call" | custom-call | flops 268435456 | bytes 1712128 | tf_op jit(solution)/shard_map/pallas_call | solution.py:186
  47.0 0.0 copy-start.2
  47.0 0.0 copy-start.4
  47.0 13.1 %all-to-all-start.1 = ((bf16[64,24,128]{2,1,0:T(8,128)(2,1)}), bf16[64,24,128]{2,1,0:T(8,128)(2,1)S(1)}, u32[]{:S(2)}, u32[]{:S(2)}) async-start(bf16[64,24,128]{2,1,0:T(8,128)(2,1)} %shard_map.48), calls=%async_computation.1 | async-start | bytes 786432 | tf_op jit(solution)/shard_map/all_to_all | solution.py:245
  60.1 0.0 copy-done.2
  60.1 0.0 copy-done.4
  60.1 1.1 %shard_map.49 = bf16[32,24,128]{2,1,0:T(8,128)(2,1)S(1)} custom-call(bf16[1,2,16,4096]{3,2,1,0:T(8,128)(2,1)S(1)} %copy-done.4, bf16[1,2,2,16,4096]{4,3,2,1,0:T(8,128)(2,1)S(1)} %copy-done.2), custom_call_target="tpu_custom_call" | custom-call | bytes 983040 | tf_op jit(solution)/shard_map/pallas_call | solution.py:186
  61.2 0.0 copy-start.5
  61.2 0.6 copy-done.5
  61.8 0.0 copy-done
  61.8 0.6 gather_fusion
  62.4 0.1 reshape.7
  62.5 2.1 %all-gather = bf16[64,24,128]{2,1,0:T(8,128)(2,1)S(1)} all-gather(bf16[32,24,128]{2,1,0:T(8,128)(2,1)S(1)} %shard_map.49), channel_id=2, replica_groups=mesh['clip'=4,'cfg'=2,'patch'=64] {'cfg'}, dimensions={0}, use_global_device_ids=true | all-gather | bytes 589824 | tf_op jit(solution)/shard_map/all_gather | solution.py:225
  64.7 0.1 pad_maximum_fusion.gate_ref
  64.7 9.9 %all-to-all-done.1.y_ref = bf16[64,24,128]{2,1,0:T(8,128)(2,1)S(1)} async-done(((bf16[64,24,128]{2,1,0:T(8,128)(2,1)}), bf16[64,24,128]{2,1,0:T(8,128)(2,1)S(1)}, u32[]{:S(2)}, u32[]{:S(2)}) %all-to-all-start.1) | async-done | bytes 393248 | tf_op jit(solution)/shard_map/all_to_all | solution.py:245
  74.7 1.5 %shard_map.50 = bf16[2,16,32,64]{3,2,1,0:T(8,128)(2,1)} custom-call(bf16[64,24,128]{2,1,0:T(8,128)(2,1)S(1)} %all-to-all-done.1.y_ref, bf16[2,32,24,128]{3,2,1,0:T(8,128)(2,1)S(1)} %bitcast.8, f32[32,128]{1,0:T(8,128)S(1)} %pad_maximum_fusion.gate_ref), custom_call_target="tpu_custom_call" | custom-call | bytes 933888 | tf_op jit(solution)/shard_map/pallas_call | solution.py:186
  (3 shorter events, 0.1 us)
Async XLA Ops:
  0.0 61.8 %copy-start = (f32[50,4096]{1,0:T(8,128)S(1)}, f32[50,4096]{1,0:T(8,128)}, u32[]{:S(2)}) copy-start(f32[50,4096]{1,0:T(8,128)} %param.7) | copy-start | bytes 2457604
  0.0 1.1 %copy-start.1 = (bf16[1,2,2,16,4096]{4,3,2,1,0:T(8,128)(2,1)S(1)}, bf16[1,2,2,16,4096]{4,3,2,1,0:T(8,128)(2,1)}, u32[]{:S(2)}) copy-start(bf16[1,2,2,16,4096]{4,3,2,1,0:T(8,128)(2,1)} %kv_ref.3) | copy-start | bytes 1572868
  1.1 0.9 %copy-start.3 = (bf16[1,2,16,4096]{3,2,1,0:T(8,128)(2,1)S(1)}, bf16[1,2,16,4096]{3,2,1,0:T(8,128)(2,1)}, u32[]{:S(2)}) copy-start(bf16[1,2,16,4096]{3,2,1,0:T(8,128)(2,1)} %q_ref.3) | copy-start | bytes 786436
  32.7 11.6 %collective-permute-start = (bf16[32,32,128]{2,1,0:T(8,128)(2,1)S(1)}, bf16[32,32,128]{2,1,0:T(8,128)(2,1)S(1)}, u32[]{:S(2)}, u32[]{:S(2)}) collective-permute-start(bf16[32,32,128]{2,1,0:T(8,128)(2,1)S(1)} %slice.16), channel_id=1, source_target_pairs={{0,1},{1,0},{2,3},{3,2},{4,5},{5,4},{6,7},{7,6},{8,9},{9,8},{10,11... | collective-permute-start | bytes 786440 | tf_op jit(solution)/shard_map/ppermute | solution.py:229
  47.0 13.1 %copy-start.2 = (bf16[1,2,2,16,4096]{4,3,2,1,0:T(8,128)(2,1)S(1)}, bf16[1,2,2,16,4096]{4,3,2,1,0:T(8,128)(2,1)}, u32[]{:S(2)}) copy-start(bf16[1,2,2,16,4096]{4,3,2,1,0:T(8,128)(2,1)} %kv_ref.3) | copy-start | bytes 1572868
  47.0 13.1 %copy-start.4 = (bf16[1,2,16,4096]{3,2,1,0:T(8,128)(2,1)S(1)}, bf16[1,2,16,4096]{3,2,1,0:T(8,128)(2,1)}, u32[]{:S(2)}) copy-start(bf16[1,2,16,4096]{3,2,1,0:T(8,128)(2,1)} %q_ref.3) | copy-start | bytes 786436
  47.0 27.7 %all-to-all-start.1 = ((bf16[64,24,128]{2,1,0:T(8,128)(2,1)}), bf16[64,24,128]{2,1,0:T(8,128)(2,1)S(1)}, u32[]{:S(2)}, u32[]{:S(2)}) async-start(bf16[64,24,128]{2,1,0:T(8,128)(2,1)} %shard_map.48), calls=%async_computation.1 | async-start | bytes 786432 | tf_op jit(solution)/shard_map/all_to_all | solution.py:245
  61.2 0.7 copy-start.5

commit v3 on v2

--- a/solution.py
+++ b/solution.py
@@ -14,6 +14,8 @@
 SIDES = 2
 NEAR = HEADS * TOK
 ROWS = 2 * NEAR
+PAIRS = TOK // 2
+SLOTS = DEPTH // TOK
 GROUP = 8
 BLOCK = 256
 FACTOR = math.log2(math.e) / math.sqrt(DEPTH)
@@ -47,32 +49,44 @@
 
 
 def write_stats(top, total):
-    n = top.shape[0] // TOK
-    lane = lax.broadcasted_iota(jnp.int32, (n, TOK // 2, DEPTH), 2)
-    both = []
-    for value in (top, total):
-        wide = jnp.broadcast_to(value, (n * TOK, DEPTH)).reshape(n, 2, TOK // 2, DEPTH)
-        both.extend(split_value(jnp.where(lane < HALF, wide[:, 0], wide[:, 1])))
-    stats = jnp.zeros((n, TOK // 2, DEPTH), F32)
-    for i, piece in enumerate(both):
-        stats = jnp.where(lane % HALF == i, piece, stats)
-    return stats.astype(BF16)
+    rows = top.shape[0]
+    n = rows // TOK
+    lane = lax.broadcasted_iota(jnp.int32, (rows, DEPTH), 1)
+    token = lax.broadcasted_iota(jnp.int32, (rows, DEPTH), 0) % TOK
+    slot = jnp.where(lane // SLOTS == token, lane % SLOTS, SLOTS)
+    value = jnp.where(slot < 3, top, total)
+    high, mid, low = split_value(value)
+    piece = jnp.where(slot % 3 == 0, high, jnp.where(slot % 3 == 1, mid, low))
+    piece = jnp.where(slot < 6, piece, 0.0).astype(BF16)
+    out_row = lax.broadcasted_iota(jnp.int32, (2 * n, rows), 0)
+    in_row = lax.broadcasted_iota(jnp.int32, (2 * n, rows), 1)
+    gather = jnp.where(out_row == in_row // TOK * 2, 1.0, 0.0).astype(BF16)
+    return jnp.dot(gather, piece, preferred_element_type=F32).reshape(n, 2, DEPTH).astype(BF16)
 
 
 def read_stats(stats):
     n = stats.shape[0]
-    row = lax.broadcasted_iota(jnp.int32, (DEPTH, 4 * DEPTH), 0)
-    part = lax.broadcasted_iota(jnp.int32, (DEPTH, 4 * DEPTH), 1) // DEPTH
-    first = part % 2 * HALF + part // 2 * 3
-    pick = jnp.where(jnp.logical_and(row >= first, row < first + 3), 1.0, 0.0).astype(BF16)
-    flat = stats.astype(F32).reshape(n * TOK // 2, DEPTH).astype(BF16)
-    wide = jnp.dot(flat, pick, preferred_element_type=F32)
-    parts = [
-        wide[:, i * DEPTH : (i + 1) * DEPTH].reshape(n, 1, TOK // 2, DEPTH) for i in range(4)
-    ]
-    top = jnp.concatenate(parts[:2], 1).reshape(n * TOK, DEPTH)
-    total = jnp.concatenate(parts[2:], 1).reshape(n * TOK, DEPTH)
-    return top, total
+    out_row = lax.broadcasted_iota(jnp.int32, (n * TOK, 2 * n), 0)
+    in_row = lax.broadcasted_iota(jnp.int32, (n * TOK, 2 * n), 1)
+    spread = jnp.where(in_row == out_row // TOK * 2, 1.0, 0.0).astype(BF16)
+    flat = stats.astype(F32).reshape(2 * n, DEPTH).astype(BF16)
+    wide = jnp.dot(spread, flat, preferred_element_type=F32)
+    lane = lax.broadcasted_iota(jnp.int32, (n * TOK, DEPTH), 1)
+    token = lax.broadcasted_iota(jnp.int32, (n * TOK, DEPTH), 0) % TOK
+    wide = jnp.where(lane // SLOTS == token, wide, 0.0).astype(BF16)
+    slot = lax.broadcasted_iota(jnp.int32, (DEPTH, 2 * DEPTH), 0) % SLOTS
+    part = lax.broadcasted_iota(jnp.int32, (DEPTH, 2 * DEPTH), 1) // DEPTH
+    pick = jnp.where(jnp.logical_and(slot < 6, slot // 3 == part), 1.0, 0.0).astype(BF16)
+    both = jnp.dot(wide, pick, preferred_element_type=F32)
+    return both[:, :DEPTH], both[:, DEPTH:]
+
+
+def write_rows(rows):
+    return rows.reshape(-1, TOK // 2, 2, DEPTH).astype(BF16)
+
+
+def read_rows(pairs):
+    return pairs.astype(F32).reshape(-1, DEPTH)
 
 
 def local_kernel(q_ref, kv_ref, out_ref):
@@ -93,36 +107,15 @@
         total = jnp.sum(weight, axis=1, keepdims=True)
         summed = jnp.dot(weight.astype(BF16), value, preferred_element_type=F32)
         here = slice(g * GROUP, (g + 1) * GROUP)
-        out_ref[here, 0:TOK] = (summed / total).astype(BF16).reshape(GROUP, TOK, DEPTH)
-        out_ref[here, TOK:] = write_stats(top, total)
-
-
-def own_half_kernel(x_ref, sum_ref, top_ref, total_ref):
-    keys = x_ref[:, 2 * TOK : 3 * TOK, :].reshape(NEAR, DEPTH)
-    values = x_ref[:, 3 * TOK :, :].reshape(NEAR, DEPTH)
+        out_ref[here, 0:PAIRS] = write_rows(summed / total)
+        out_ref[here, PAIRS] = write_stats(top, total)
+
+
+def attend_kernel(x_ref, kv_ref, out_ref):
+    side = lax.axis_index("patch") % SIDES
     row = lax.broadcasted_iota(jnp.int32, (BLOCK, BLOCK), 0)
     col = lax.broadcasted_iota(jnp.int32, (BLOCK, BLOCK), 1)
     same = row // TOK == col // TOK
-    for step in range(2):
-        for i in range(NEAR // BLOCK):
-            patches = slice(i * BLOCK // TOK, (i + 1) * BLOCK // TOK)
-            query = x_ref[patches, step * TOK : (step + 1) * TOK, :].reshape(BLOCK, DEPTH)
-            score = dot_t(query, keys)
-            if step == 1:
-                near = jnp.where(same, -jnp.inf, score[:, i * BLOCK : (i + 1) * BLOCK])
-                parts = [score[:, : i * BLOCK], near, score[:, (i + 1) * BLOCK :]]
-                score = jnp.concatenate([p for p in parts if p.shape[1]], axis=1)
-            top = jnp.max(score, axis=1, keepdims=True)
-            weight = jnp.exp2((score - top) * FACTOR)
-            here = slice(step * NEAR + i * BLOCK, step * NEAR + (i + 1) * BLOCK)
-            sum_ref[here] = jnp.dot(weight.astype(BF16), values, preferred_element_type=F32)
-            top_ref[here] = top
-            total_ref[here] = jnp.sum(weight, axis=1, keepdims=True)
-
-
-def other_half_kernel(x_ref, other_ref, sum_ref, top_ref, total_ref, out_ref):
-    keys = other_ref[:, 0:TOK, :].reshape(NEAR, DEPTH)
-    values = other_ref[:, TOK:, :].reshape(NEAR, DEPTH)
     lower = lax.broadcasted_iota(jnp.int32, (BLOCK, DEPTH), 1) < HALF
     n = BLOCK // TOK
     for i in range(NEAR // BLOCK):
@@ -130,15 +123,24 @@
         attn = []
         for step in range(2):
             query = x_ref[patches, step * TOK : (step + 1) * TOK, :].reshape(BLOCK, DEPTH)
-            score = dot_t(query, keys)
-            here = slice(step * NEAR + i * BLOCK, step * NEAR + (i + 1) * BLOCK)
-            old_top = top_ref[here]
-            top = jnp.maximum(jnp.max(score, axis=1, keepdims=True), old_top)
-            weight = jnp.exp2((score - top) * FACTOR)
-            old = jnp.exp2((old_top - top) * FACTOR)
-            total = jnp.sum(weight, axis=1, keepdims=True) + old * total_ref[here]
-            summed = jnp.dot(weight.astype(BF16), values, preferred_element_type=F32)
-            attn.append((summed + old * sum_ref[here]) / total)
+            scores = []
+            for half in range(SIDES):
+                score = dot_t(query, kv_ref[half, :, 0:TOK, :].reshape(NEAR, DEPTH))
+                if step == 1:
+                    own = jnp.logical_and(same, side == half)
+                    near = jnp.where(own, -jnp.inf, score[:, i * BLOCK : (i + 1) * BLOCK])
+                    parts = [score[:, : i * BLOCK], near, score[:, (i + 1) * BLOCK :]]
+                    score = jnp.concatenate([p for p in parts if p.shape[1]], axis=1)
+                scores.append(score)
+            tops = [jnp.max(score, axis=1, keepdims=True) for score in scores]
+            top = jnp.maximum(tops[0], tops[1])
+            total, summed = 0.0, 0.0
+            for half in range(SIDES):
+                weight = jnp.exp2((scores[half] - top) * FACTOR)
+                total += jnp.sum(weight, axis=1, keepdims=True)
+                values = kv_ref[half, :, TOK:, :].reshape(NEAR, DEPTH)
+                summed += jnp.dot(weight.astype(BF16), values, preferred_element_type=F32)
+            attn.append(summed / total)
         first, second = attn
         chunks = (
             jnp.where(lower, first, pltpu.roll(second, HALF, 1)),
@@ -147,8 +149,8 @@
         stats = write_stats(top, total)
         for core, chunk in enumerate(chunks):
             at = slice(core * HEADS + i * n, core * HEADS + (i + 1) * n)
-            out_ref[at, 0:TOK] = chunk.astype(BF16).reshape(n, TOK, DEPTH)
-            out_ref[at, TOK:] = stats
+            out_ref[at, 0:PAIRS] = write_rows(chunk)
+            out_ref[at, PAIRS] = stats
 
 
 def merge_kernel(y_ref, near_ref, gate_ref, out_ref, held):
@@ -157,11 +159,11 @@
 
     def branch(b):
         heads = slice(b * HEADS, (b + 1) * HEADS)
-        far = y_ref[heads, 0:TOK].astype(F32).reshape(NEAR, DEPTH)
-        near = near_ref[b, :, 0:TOK].astype(F32).reshape(NEAR, DEPTH)
+        far = read_rows(y_ref[heads, 0:PAIRS])
+        near = read_rows(near_ref[b, :, 0:PAIRS])
         near = jnp.where(upper, near, pltpu.roll(near, HALF, 1))
-        far_top, far_total = read_stats(y_ref[heads, TOK:])
-        near_top, near_total = read_stats(near_ref[b, :, TOK:])
+        far_top, far_total = read_stats(y_ref[heads, PAIRS])
+        near_top, near_total = read_stats(near_ref[b, :, PAIRS])
         top = jnp.maximum(far_top, near_top)
         far_share = jnp.exp2((far_top - top) * FACTOR) * far_total
         near_share = jnp.exp2((near_top - top) * FACTOR) * near_total
@@ -215,7 +217,7 @@
     )
     near = call(
         local_kernel,
-        SHAPE((HEADS, 3 * TOK // 2, DEPTH), BF16),
+        SHAPE((HEADS, PAIRS + 1, 2, DEPTH), BF16),
         (queries, keys_values),
         [
             pl.BlockSpec((None, 1, TOK, width), lambda i: (0, 1, 0, 0)),
@@ -226,21 +228,16 @@
     gates = jnp.take(gate_table, timesteps, axis=0, mode="clip").reshape(2, HEADS, 2, HALF)
     gate = lax.dynamic_index_in_dim(gates, lax.axis_index("cfg"), 2, keepdims=False)
     gate = jnp.concatenate([gate[0], gate[1]], axis=1)
-    other = lax.ppermute(
-        held[:, 2 * TOK :, :], "patch", [(i, i ^ 1) for i in range(patches)]
-    )
-    column = SHAPE((ROWS, 1), F32)
-    own = call(
-        own_half_kernel,
-        [SHAPE((ROWS, DEPTH), F32), column, column],
-        (held,),
-        flops=4 * ROWS * NEAR * DEPTH,
+    held, near, gate = lax.optimization_barrier((held, near, gate))
+    pairs = [[SIDES * i, SIDES * i + 1] for i in range(HEADS)]
+    stale = lax.all_gather(
+        held[:, 2 * TOK :, :], "patch", axis=0, tiled=False, axis_index_groups=pairs
     )
     far = call(
-        other_half_kernel,
-        SHAPE((2 * HEADS, 3 * TOK // 2, DEPTH), BF16),
-        (held, other, *own),
-        flops=4 * ROWS * NEAR * DEPTH,
+        attend_kernel,
+        SHAPE((2 * HEADS, PAIRS + 1, 2, DEPTH), BF16),
+        (held, stale),
+        flops=8 * ROWS * NEAR * DEPTH,
     )
     back = lax.all_to_all(
         far, ("cfg", "patch"), split_axis=0, concat_axis=0, tiled=True, axis_index_groups=cores

time: 77.2 us -> 75 us (0.972)
  starting transfers between devices: 20.5 us -> 13.9 us
  blocking collectives: 31.9 us -> 38.3 us
  waiting for transfers between devices: 12.7 us -> 11.5 us
  Pallas kernels: 7.47 us -> 6.69 us
    all_gather x0 -> x1, blocking collectives: none -> 10.3 us  [body(): lax.all_gather(held[:, 2 * TOK:, :], 'patch', axis=0, tiled=False, axis_i...]
    ppermute x1 -> x0, starting transfers between devices: 7.45 us -> none  [body(): lax.ppermute(held[:, 2 * TOK:, :], 'patch', [(i, i ^ 1) for i in range(pa...]
    all_to_all x1, blocking collectives: 29.8 us -> 25.4 us  [body(): lax.all_to_all(far, ('cfg', 'patch'), split_axis=0, concat_axis=0, tiled=...]
    ppermute x1 -> x0, waiting for transfers between devices: 2.75 us -> none  [body(): lax.ppermute(held[:, 2 * TOK:, :], 'patch', [(i, i ^ 1) for i in range(pa...]
    all_to_all x1, waiting for transfers between devices: 9.92 us -> 11.5 us  [body(): lax.all_to_all(sent, 'patch', split_axis=0, concat_axis=0, tiled=True, ax...]
    all_to_all x1, starting transfers between devices: 13.1 us -> 13.9 us  [body(): lax.all_to_all(sent, 'patch', split_axis=0, concat_axis=0, tiled=True, ax...]
    pallas_call x5 -> x4, Pallas kernels: 7.47 us -> 6.69 us  [call(): pl.pallas_call(kernel, grid=(1,), out_shape=out, in_specs=specs or [vmem]...]
  transfers between devices with their start and end apart: 2 -> 1, of which waited for: 2 -> 1; matrix products, arithmetic and copies ran while one was open for 1% -> 1% of each run, Pallas kernels for 3% -> 1%
where the time goes in v3:
time: 75 us; the launch traced here: 74 us
  blocking collectives  38.3 us (51%)
  starting transfers between devices  13.9 us (19%)
  waiting for transfers between devices  11.5 us (15%)
  Pallas kernels  6.69 us (9%)
  local copies, waits for them, and re-layouts  3.49 us (5%)
    all_to_all x1, blocking collectives, body(): lax.all_to_all(far, ('cfg', 'patch'), split_axis=0, concat_axis=0, tiled=...  25.4 us
    all_to_all x1, starting transfers between devices, body(): lax.all_to_all(sent, 'patch', split_axis=0, concat_axis=0, tiled=True, ax...  13.9 us
    all_to_all x1, waiting for transfers between devices, body(): lax.all_to_all(sent, 'patch', split_axis=0, concat_axis=0, tiled=True, ax...  11.5 us
    all_gather x1, blocking collectives, body(): lax.all_gather(held[:, 2 * TOK:, :], 'patch', axis=0, tiled=False, axis_i...  10.3 us
    pallas_call x4, Pallas kernels, call(): pl.pallas_call(kernel, grid=(1,), out_shape=out, in_specs=specs or [vmem]...  6.69 us
    unnamed x12, local copies, waits for them, and re-layouts  2.75 us
    all_gather x1, blocking collectives, body(): near = lax.all_gather(near, 'cfg', axis=0, tiled=False)  2.61 us
  transfers between devices with their start and end apart: 1, of which 1 were waited for; matrix products, arithmetic and copies ran while one was open for 1% of the time, Pallas kernels for 1%

profile of v3, /device:TPU:1, one launch (start us, length us, event | category | flops | bytes accessed | tf_op | source)
XLA Modules:
  0.0 74.0 jit_solution(14346334172470359000)
XLA Ops:
  0.0 0.0 copy-start
  0.0 0.0 copy-start.1
  0.0 1.1 %copy-done.1 = bf16[1,2,2,16,4096]{4,3,2,1,0:T(8,128)(2,1)S(1)} copy-done((bf16[1,2,2,16,4096]{4,3,2,1,0:T(8,128)(2,1)S(1)}, bf16[1,2,2,16,4096]{4,3,2,1,0:T(8,128)(2,1)}, u32[]{:S(2)}) %copy-start.1) | copy-done | bytes 524312
  1.1 0.0 copy-start.3
  1.1 0.9 %copy-done.3 = bf16[1,2,16,4096]{3,2,1,0:T(8,128)(2,1)S(1)} copy-done((bf16[1,2,16,4096]{3,2,1,0:T(8,128)(2,1)S(1)}, bf16[1,2,16,4096]{3,2,1,0:T(8,128)(2,1)}, u32[]{:S(2)}) %copy-start.3) | copy-done | bytes 262168
  2.1 1.6 %shard_map.46 = bf16[32,64,128]{2,1,0:T(8,128)(2,1)} custom-call(bf16[1,2,16,4096]{3,2,1,0:T(8,128)(2,1)S(1)} %copy-done.3, bf16[1,2,2,16,4096]{4,3,2,1,0:T(8,128)(2,1)S(1)} %copy-done.1), custom_call_target="tpu_custom_call" | custom-call | bytes 1310720 | tf_op jit(solution)/shard_map/pallas_call | solution.py:188
  3.7 0.0 copy-start.2
  3.7 0.0 copy-start.4
  3.7 13.9 %all-to-all-start = ((bf16[32,64,128]{2,1,0:T(8,128)(2,1)}), bf16[32,64,128]{2,1,0:T(8,128)(2,1)S(1)}, u32[]{:S(2)}, u32[]{:S(2)}) async-start(bf16[32,64,128]{2,1,0:T(8,128)(2,1)} %shard_map.46), calls=%async_computation | async-start | bytes 1048576 | tf_op jit(solution)/shard_map/all_to_all | solution.py:215
  17.6 0.0 copy-done.2
  17.6 0.0 copy-done.4
  17.6 0.7 shard_map.47
  18.2 0.0 copy-start.5
  18.2 0.7 copy-done.5
  18.9 0.0 copy-done
  18.9 0.6 gather_fusion
  19.5 0.1 reshape.7
  19.6 2.6 %all-gather = bf16[64,9,2,128]{3,2,1,0:T(2,128)(2,1)S(1)} all-gather(bf16[32,9,2,128]{3,2,1,0:T(2,128)(2,1)S(1)} %shard_map.47), channel_id=2, replica_groups=mesh['clip'=4,'cfg'=2,'patch'=64] {'cfg'}, dimensions={0}, use_global_device_ids=true | all-gather | bytes 442368 | tf_op jit(solution)/shard_map/all_gather | solution.py:227
  22.3 0.1 pad_maximum_fusion.gate_ref
  22.3 11.5 %all-to-all-done.x_ref = bf16[32,64,128]{2,1,0:T(8,128)(2,1)S(1)} async-done(((bf16[32,64,128]{2,1,0:T(8,128)(2,1)}), bf16[32,64,128]{2,1,0:T(8,128)(2,1)S(1)}, u32[]{:S(2)}, u32[]{:S(2)}) %all-to-all-start) | async-done | bytes 524320 | tf_op jit(solution)/shard_map/all_to_all | solution.py:215
  33.9 10.3 %all-gather.1 = bf16[64,32,128]{2,1,0:T(8,128)(2,1)S(1)} all-gather(bf16[32,32,128]{2,1,0:T(8,128)(2,1)S(1)} %slice.13), channel_id=3, replica_groups={{0,1},{2,3},{4,5},{6,7},{8,9},{10,11},{12,13},{14,15},{16,17},{18,19},{..., dimensions={0}, use_global_device_ids=true | all-gather | bytes 786432 | tf_op jit(solution)/shard_map/all_gather | solution.py:233
  44.2 2.4 %shard_map.48 = bf16[64,9,2,128]{3,2,1,0:T(2,128)(2,1)S(1)} custom-call(bf16[32,64,128]{2,1,0:T(8,128)(2,1)S(1)} %all-to-all-done.x_ref, bf16[2,32,32,128]{3,2,1,0:T(8,128)(2,1)S(1)} %bitcast.10), custom_call_target="tpu_custom_call" | custom-call | flops 536870912 | bytes 1343488 | tf_op jit(solution)/shard_map/pallas_call | solution.py:188
  46.5 25.4 %all_to_all.10.y_ref = bf16[64,9,2,128]{3,2,1,0:T(2,128)(2,1)S(1)} all-to-all(bf16[64,9,2,128]{3,2,1,0:T(2,128)(2,1)S(1)} %shard_map.48), channel_id=1, replica_groups={{0,2,4,6,8,10,12,14,16,18,20,22,24,26,28,30,32,34,36,38,40,42,44,46,48,..., dimensions={0} | all-to-all | bytes 589824 | tf_op jit(solution)/shard_map/all_to_all | solution.py:242
  71.9 2.1 %shard_map.49 = bf16[2,16,32,64]{3,2,1,0:T(8,128)(2,1)} custom-call(bf16[64,9,2,128]{3,2,1,0:T(2,128)(2,1)S(1)} %all_to_all.10.y_ref, bf16[2,32,9,2,128]{4,3,2,1,0:T(2,128)(2,1)S(1)} %bitcast.9, f32[32,128]{1,0:T(8,128)S(1)} %pad_maximum_fusion.gate_ref), custom_call_target="tpu_custom_call" | custom-call | bytes 737280 | tf_op jit(solution)/shard_map/pallas_call | solution.py:188
  (3 shorter events, 0.1 us)
Async XLA Ops:
  0.0 18.9 %copy-start = (f32[50,4096]{1,0:T(8,128)S(1)}, f32[50,4096]{1,0:T(8,128)}, u32[]{:S(2)}) copy-start(f32[50,4096]{1,0:T(8,128)} %param.7) | copy-start | bytes 2457604
  0.0 1.1 %copy-start.1 = (bf16[1,2,2,16,4096]{4,3,2,1,0:T(8,128)(2,1)S(1)}, bf16[1,2,2,16,4096]{4,3,2,1,0:T(8,128)(2,1)}, u32[]{:S(2)}) copy-start(bf16[1,2,2,16,4096]{4,3,2,1,0:T(8,128)(2,1)} %kv_ref.3) | copy-start | bytes 1572868
  1.1 0.9 %copy-start.3 = (bf16[1,2,16,4096]{3,2,1,0:T(8,128)(2,1)S(1)}, bf16[1,2,16,4096]{3,2,1,0:T(8,128)(2,1)}, u32[]{:S(2)}) copy-start(bf16[1,2,16,4096]{3,2,1,0:T(8,128)(2,1)} %q_ref.3) | copy-start | bytes 786436
  3.7 13.9 %copy-start.2 = (bf16[1,2,2,16,4096]{4,3,2,1,0:T(8,128)(2,1)S(1)}, bf16[1,2,2,16,4096]{4,3,2,1,0:T(8,128)(2,1)}, u32[]{:S(2)}) copy-start(bf16[1,2,2,16,4096]{4,3,2,1,0:T(8,128)(2,1)} %kv_ref.3) | copy-start | bytes 1572868
  3.7 13.9 %copy-start.4 = (bf16[1,2,16,4096]{3,2,1,0:T(8,128)(2,1)S(1)}, bf16[1,2,16,4096]{3,2,1,0:T(8,128)(2,1)}, u32[]{:S(2)}) copy-start(bf16[1,2,16,4096]{3,2,1,0:T(8,128)(2,1)} %q_ref.3) | copy-start | bytes 786436
  3.7 30.1 %all-to-all-start = ((bf16[32,64,128]{2,1,0:T(8,128)(2,1)}), bf16[32,64,128]{2,1,0:T(8,128)(2,1)S(1)}, u32[]{:S(2)}, u32[]{:S(2)}) async-start(bf16[32,64,128]{2,1,0:T(8,128)(2,1)} %shard_map.46), calls=%async_computation | async-start | bytes 1048576 | tf_op jit(solution)/shard_map/all_to_all | solution.py:215
  18.2 0.7 copy-start.5

commit v4 on v3

--- a/solution.py
+++ b/solution.py
@@ -17,7 +17,8 @@
 PAIRS = TOK // 2
 SLOTS = DEPTH // TOK
 GROUP = 8
-BLOCK = 256
+TOKENS = SIDES * NEAR
+BLOCK = 128
 FACTOR = math.log2(math.e) / math.sqrt(DEPTH)
 BF16 = jnp.bfloat16
 F32 = jnp.float32
@@ -28,17 +29,23 @@
     return lax.dot_general(a, b, (((1,), (1,)), ((), ())), preferred_element_type=F32)
 
 
-def pack_kernel(q_ref, kv_ref, out_ref, held, sems):
+def pack_kernel(q_ref, kv_ref, out_ref, held, packed, in_sems, out_sems):
     fields = [q_ref.at[0, 0], q_ref.at[0, 1], kv_ref.at[0, 0, 0], kv_ref.at[0, 0, 1]]
     copies = [
-        pltpu.make_async_copy(field, held.at[i], sems.at[i]) for i, field in enumerate(fields)
+        pltpu.make_async_copy(field, held.at[i], in_sems.at[i]) for i, field in enumerate(fields)
     ]
     for copy in copies:
         copy.start()
+    results = []
     for i, copy in enumerate(copies):
         copy.wait()
         for h in range(HEADS):
-            out_ref[h, i * TOK : (i + 1) * TOK, :] = held[i, :, h * DEPTH : (h + 1) * DEPTH]
+            packed[i, h] = held[i, :, h * DEPTH : (h + 1) * DEPTH]
+        rows = out_ref.at[:, i * TOK : (i + 1) * TOK, :]
+        results.append(pltpu.make_async_copy(packed.at[i], rows, out_sems.at[i]))
+        results[-1].start()
+    for result in results:
+        result.wait()
 
 
 def split_value(value):
@@ -111,63 +118,74 @@
         out_ref[here, PAIRS] = write_stats(top, total)
 
 
-def attend_kernel(x_ref, kv_ref, out_ref):
+def attend_kernel(x_ref, kv_ref, out_ref, score, weight, top, total):
     side = lax.axis_index("patch") % SIDES
     row = lax.broadcasted_iota(jnp.int32, (BLOCK, BLOCK), 0)
     col = lax.broadcasted_iota(jnp.int32, (BLOCK, BLOCK), 1)
     same = row // TOK == col // TOK
     lower = lax.broadcasted_iota(jnp.int32, (BLOCK, DEPTH), 1) < HALF
     n = BLOCK // TOK
+    steps = [slice(step * NEAR, (step + 1) * NEAR) for step in range(2)]
+    for step in range(2):
+        query = x_ref[:, step * TOK : (step + 1) * TOK, :].reshape(NEAR, DEPTH)
+        for half in range(SIDES):
+            keys = kv_ref[half, :, 0:TOK, :].reshape(NEAR, DEPTH)
+            score[steps[step], half * NEAR : (half + 1) * NEAR] = dot_t(query, keys)
+    for step in range(2):
+        for i in range(NEAR // BLOCK):
+            here = slice(step * NEAR + i * BLOCK, step * NEAR + (i + 1) * BLOCK)
+            if step == 1:
+                for half in range(SIDES):
+                    cols = slice(half * NEAR + i * BLOCK, half * NEAR + (i + 1) * BLOCK)
+                    own = jnp.logical_and(same, side == half)
+                    score[here, cols] = jnp.where(own, -jnp.inf, score[here, cols])
+            block = score[here]
+            most = jnp.max(block, axis=1, keepdims=True)
+            weights = jnp.exp2((block - most) * FACTOR)
+            added = jnp.sum(weights, axis=1, keepdims=True)
+            top[here] = jnp.broadcast_to(most, (BLOCK, DEPTH))
+            total[here] = jnp.broadcast_to(added, (BLOCK, DEPTH))
+            weight[here] = weights.astype(BF16)
+    values = kv_ref[:, :, TOK:, :].reshape(TOKENS, DEPTH)
+    attn = score.at[:, 0:DEPTH]
+    for step in range(2):
+        attn[steps[step]] = jnp.dot(weight[steps[step]], values, preferred_element_type=F32)
     for i in range(NEAR // BLOCK):
-        patches = slice(i * n, (i + 1) * n)
-        attn = []
-        for step in range(2):
-            query = x_ref[patches, step * TOK : (step + 1) * TOK, :].reshape(BLOCK, DEPTH)
-            scores = []
-            for half in range(SIDES):
-                score = dot_t(query, kv_ref[half, :, 0:TOK, :].reshape(NEAR, DEPTH))
-                if step == 1:
-                    own = jnp.logical_and(same, side == half)
-                    near = jnp.where(own, -jnp.inf, score[:, i * BLOCK : (i + 1) * BLOCK])
-                    parts = [score[:, : i * BLOCK], near, score[:, (i + 1) * BLOCK :]]
-                    score = jnp.concatenate([p for p in parts if p.shape[1]], axis=1)
-                scores.append(score)
-            tops = [jnp.max(score, axis=1, keepdims=True) for score in scores]
-            top = jnp.maximum(tops[0], tops[1])
-            total, summed = 0.0, 0.0
-            for half in range(SIDES):
-                weight = jnp.exp2((scores[half] - top) * FACTOR)
-                total += jnp.sum(weight, axis=1, keepdims=True)
-                values = kv_ref[half, :, TOK:, :].reshape(NEAR, DEPTH)
-                summed += jnp.dot(weight.astype(BF16), values, preferred_element_type=F32)
-            attn.append(summed / total)
-        first, second = attn
+        zero = slice(i * BLOCK, (i + 1) * BLOCK)
+        one = slice(NEAR + i * BLOCK, NEAR + (i + 1) * BLOCK)
+        first = attn[zero] / total[zero]
+        second = attn[one] / total[one]
         chunks = (
             jnp.where(lower, first, pltpu.roll(second, HALF, 1)),
             jnp.where(lower, pltpu.roll(first, HALF, 1), second),
         )
-        stats = write_stats(top, total)
+        stats = write_stats(top[one], total[one])
         for core, chunk in enumerate(chunks):
             at = slice(core * HEADS + i * n, core * HEADS + (i + 1) * n)
             out_ref[at, 0:PAIRS] = write_rows(chunk)
             out_ref[at, PAIRS] = stats
 
 
-def merge_kernel(y_ref, near_ref, gate_ref, out_ref, held):
+def near_kernel(near_ref, attn_ref, top_ref, total_ref):
     upper = lax.axis_index("cfg") == 1
+    for b in range(2):
+        near = read_rows(near_ref[b, :, 0:PAIRS])
+        attn_ref[b] = jnp.where(upper, near, pltpu.roll(near, HALF, 1))
+        top_ref[b], total_ref[b] = read_stats(near_ref[b, :, PAIRS])
+
+
+def merge_kernel(y_ref, near_ref, top_ref, total_ref, gate_ref, out_ref, held):
     lower = lax.broadcasted_iota(jnp.int32, (NEAR, DEPTH), 1) < HALF
 
     def branch(b):
         heads = slice(b * HEADS, (b + 1) * HEADS)
         far = read_rows(y_ref[heads, 0:PAIRS])
-        near = read_rows(near_ref[b, :, 0:PAIRS])
-        near = jnp.where(upper, near, pltpu.roll(near, HALF, 1))
         far_top, far_total = read_stats(y_ref[heads, PAIRS])
-        near_top, near_total = read_stats(near_ref[b, :, PAIRS])
+        near_top = top_ref[b]
         top = jnp.maximum(far_top, near_top)
         far_share = jnp.exp2((far_top - top) * FACTOR) * far_total
-        near_share = jnp.exp2((near_top - top) * FACTOR) * near_total
-        both = (far_share * far + near_share * near) / (far_share + near_share)
+        near_share = jnp.exp2((near_top - top) * FACTOR) * total_ref[b]
+        both = (far_share * far + near_share * near_ref[b]) / (far_share + near_share)
         return jnp.where(lower, far, both).astype(BF16).astype(F32)
 
     cond = branch(0)
@@ -180,20 +198,21 @@
         out_ref[1, t] = rows[:, HALF:].astype(BF16)
 
 
-def call(kernel, out, args, specs=None, scratch=(), flops=0):
+def call(kernel, out, args, specs=None, scratch=(), flops=0, out_space=pltpu.VMEM, limit=32):
     many = isinstance(out, list)
     shapes = out if many else [out]
     moved = sum(a.size * a.dtype.itemsize for a in list(args) + list(shapes))
     vmem = pl.BlockSpec(memory_space=pltpu.VMEM)
+    result = pl.BlockSpec(memory_space=out_space)
     return pl.pallas_call(
         kernel,
         grid=(1,),
         out_shape=out,
         in_specs=specs or [vmem] * len(args),
-        out_specs=[vmem] * len(shapes) if many else vmem,
+        out_specs=[result] * len(shapes) if many else result,
         scratch_shapes=list(scratch),
         cost_estimate=pl.CostEstimate(flops=flops, bytes_accessed=moved, transcendentals=0),
-        compiler_params=pltpu.CompilerParams(vmem_limit_bytes=32 << 20),
+        compiler_params=pltpu.CompilerParams(vmem_limit_bytes=limit << 20),
     )(*args)
 
 
@@ -210,7 +229,14 @@
         SHAPE((HEADS, 4 * TOK, DEPTH), BF16),
         (queries, keys_values),
         [whole, whole],
-        [pltpu.VMEM((4, TOK, width), BF16), pltpu.SemaphoreType.DMA((4,))],
+        [
+            pltpu.VMEM((4, TOK, width), BF16),
+            pltpu.VMEM((4, HEADS, TOK, DEPTH), BF16),
+            pltpu.SemaphoreType.DMA((4,)),
+            pltpu.SemaphoreType.DMA((4,)),
+        ],
+        out_space=pltpu.HBM,
+        limit=60,
     )
     held = lax.all_to_all(
         sent, "patch", split_axis=0, concat_axis=0, tiled=True, axis_index_groups=sides
@@ -225,6 +251,7 @@
         ],
     )
     near = lax.all_gather(near, "cfg", axis=0, tiled=False)
+    near = call(near_kernel, [SHAPE((2, NEAR, DEPTH), F32)] * 3, (near,))
     gates = jnp.take(gate_table, timesteps, axis=0, mode="clip").reshape(2, HEADS, 2, HALF)
     gate = lax.dynamic_index_in_dim(gates, lax.axis_index("cfg"), 2, keepdims=False)
     gate = jnp.concatenate([gate[0], gate[1]], axis=1)
@@ -237,7 +264,13 @@
         attend_kernel,
         SHAPE((2 * HEADS, PAIRS + 1, 2, DEPTH), BF16),
         (held, stale),
-        flops=8 * ROWS * NEAR * DEPTH,
+        scratch=[
+            pltpu.VMEM((ROWS, TOKENS), F32),
+            pltpu.VMEM((ROWS, TOKENS), BF16),
+            pltpu.VMEM((ROWS, DEPTH), F32),
+            pltpu.VMEM((ROWS, DEPTH), F32),
+        ],
+        flops=4 * ROWS * TOKENS * DEPTH,
     )
     back = lax.all_to_all(
         far, ("cfg", "patch"), split_axis=0, concat_axis=0, tiled=True, axis_index_groups=cores
@@ -245,7 +278,7 @@
     return call(
         merge_kernel,
         SHAPE((2, TOK, HEADS, HALF), BF16),
-        (back, near, gate),
+        (back, *near, gate),
         scratch=[pltpu.VMEM((NEAR, DEPTH), F32)],
     )
 

time: 75 us -> 72.4 us (0.965)
  local copies, waits for them, and re-layouts: 3.49 us -> 1.42 us
    unnamed x12 -> x8, local copies, waits for them, and re-layouts: 2.75 us -> 0.68 us
    pallas_call x4 -> x5, Pallas kernels: 6.69 us -> 6.77 us  [call(): pl.pallas_call(kernel, grid=(1,), out_shape=out, in_specs=specs or [vmem]...]
  transfers between devices with their start and end apart: 1 -> 1, of which waited for: 1 -> 1; matrix products, arithmetic and copies ran while one was open for 1% -> 1% of each run, Pallas kernels for 1% -> 2%
where the time goes in v4:
time: 72.4 us; the launch traced here: 71.3 us
  blocking collectives  38.3 us (53%)
  starting transfers between devices  13.9 us (19%)
  waiting for transfers between devices  10.8 us (15%)
  Pallas kernels  6.77 us (9%)
  local copies, waits for them, and re-layouts  1.42 us (2%)
    all_to_all x1, blocking collectives, body(): lax.all_to_all(far, ('cfg', 'patch'), split_axis=0, concat_axis=0, tiled=...  25.3 us
    all_to_all x1, starting transfers between devices, body(): lax.all_to_all(sent, 'patch', split_axis=0, concat_axis=0, tiled=True, ax...  13.9 us
    all_to_all x1, waiting for transfers between devices, body(): lax.all_to_all(sent, 'patch', split_axis=0, concat_axis=0, tiled=True, ax...  10.8 us
    all_gather x1, blocking collectives, body(): lax.all_gather(held[:, 2 * TOK:, :], 'patch', axis=0, tiled=False, axis_i...  10.3 us
    pallas_call x5, Pallas kernels, call(): pl.pallas_call(kernel, grid=(1,), out_shape=out, in_specs=specs or [vmem]...  6.77 us
    all_gather x1, blocking collectives, body(): near = lax.all_gather(near, 'cfg', axis=0, tiled=False)  2.61 us
  transfers between devices with their start and end apart: 1, of which 1 were waited for; matrix products, arithmetic and copies ran while one was open for 1% of the time, Pallas kernels for 2%

profile of v4, /device:TPU:1, one launch (start us, length us, event | category | flops | bytes accessed | tf_op | source)
XLA Modules:
  0.0 71.3 jit_solution(10011158799065322459)
XLA Ops:
  0.0 0.0 copy-start
  0.0 1.9 %shard_map.46 = bf16[32,64,128]{2,1,0:T(8,128)(2,1)} custom-call(bf16[1,2,16,4096]{3,2,1,0:T(8,128)(2,1)} %q_ref.3, bf16[1,2,2,16,4096]{4,3,2,1,0:T(8,128)(2,1)} %kv_ref.3), custom_call_target="tpu_custom_call" | custom-call | bytes 1310720 | tf_op jit(solution)/shard_map/pallas_call | solution.py:207
  1.9 0.0 copy-start.1
  2.0 0.0 copy-start.2
  2.0 13.9 %all-to-all-start = ((bf16[32,64,128]{2,1,0:T(8,128)(2,1)}), bf16[32,64,128]{2,1,0:T(8,128)(2,1)S(1)}, u32[]{:S(2)}, u32[]{:S(2)}) async-start(bf16[32,64,128]{2,1,0:T(8,128)(2,1)} %shard_map.46), calls=%async_computation | async-start | bytes 1048576 | tf_op jit(solution)/shard_map/all_to_all | solution.py:241
  15.8 0.0 copy-done.1
  15.9 0.0 copy-done.2
  15.9 0.7 shard_map.47
  16.5 0.0 copy-start.3
  16.5 0.7 copy-done.3
  17.2 0.0 copy-done
  17.2 0.6 gather_fusion
  17.8 0.1 reshape.7
  17.9 2.6 %all-gather = bf16[64,9,2,128]{3,2,1,0:T(2,128)(2,1)S(1)} all-gather(bf16[32,9,2,128]{3,2,1,0:T(2,128)(2,1)S(1)} %shard_map.47), channel_id=2, replica_groups=mesh['clip'=4,'cfg'=2,'patch'=64] {'cfg'}, dimensions={0}, use_global_device_ids=true | all-gather | bytes 442368 | tf_op jit(solution)/shard_map/all_gather | solution.py:253
  20.5 0.7 shard_map.48
  21.2 0.1 pad_maximum_fusion.gate_ref
  21.3 10.8 %all-to-all-done.x_ref = bf16[32,64,128]{2,1,0:T(8,128)(2,1)S(1)} async-done(((bf16[32,64,128]{2,1,0:T(8,128)(2,1)}), bf16[32,64,128]{2,1,0:T(8,128)(2,1)S(1)}, u32[]{:S(2)}, u32[]{:S(2)}) %all-to-all-start) | async-done | bytes 524320 | tf_op jit(solution)/shard_map/all_to_all | solution.py:241
  32.1 10.3 %all-gather.1 = bf16[64,32,128]{2,1,0:T(8,128)(2,1)S(1)} all-gather(bf16[32,32,128]{2,1,0:T(8,128)(2,1)S(1)} %slice.13), channel_id=3, replica_groups={{0,1},{2,3},{4,5},{6,7},{8,9},{10,11},{12,13},{14,15},{16,17},{18,19},{..., dimensions={0}, use_global_device_ids=true | all-gather | bytes 786432 | tf_op jit(solution)/shard_map/all_gather | solution.py:260
  42.5 1.9 %shard_map.49 = bf16[64,9,2,128]{3,2,1,0:T(2,128)(2,1)S(1)} custom-call(bf16[32,64,128]{2,1,0:T(8,128)(2,1)S(1)} %all-to-all-done.x_ref, bf16[2,32,32,128]{3,2,1,0:T(8,128)(2,1)S(1)} %bitcast.10), custom_call_target="tpu_custom_call" | custom-call | flops 536870912 | bytes 1343488 | tf_op jit(solution)/shard_map/pallas_call | solution.py:207
  44.4 25.3 %all_to_all.10.y_ref = bf16[64,9,2,128]{3,2,1,0:T(2,128)(2,1)S(1)} all-to-all(bf16[64,9,2,128]{3,2,1,0:T(2,128)(2,1)S(1)} %shard_map.49), channel_id=1, replica_groups={{0,2,4,6,8,10,12,14,16,18,20,22,24,26,28,30,32,34,36,38,40,42,44,46,48,..., dimensions={0} | all-to-all | bytes 589824 | tf_op jit(solution)/shard_map/all_to_all | solution.py:275
  69.7 1.6 %shard_map.50 = bf16[2,16,32,64]{3,2,1,0:T(8,128)(2,1)} custom-call(bf16[64,9,2,128]{3,2,1,0:T(2,128)(2,1)S(1)} %all_to_all.10.y_ref, f32[2,512,128]{2,1,0:T(8,128)S(1)} %get-tuple-element.17.near_ref, f32[2,512,128]{2,1,0:T(8,128)S(1)} %get-tuple-element.18.top_ref, f32[2,512,128]{2,1,0:T(8,128)S(1)} %get-tuple-element.19.total_ref, ...), custom_call_target="tpu_custom_call" | custom-call | bytes 2015232 | tf_op jit(solution)/shard_map/pallas_call | solution.py:207
  (3 shorter events, 0.1 us)
Async XLA Ops:
  0.0 17.2 %copy-start = (f32[50,4096]{1,0:T(8,128)S(1)}, f32[50,4096]{1,0:T(8,128)}, u32[]{:S(2)}) copy-start(f32[50,4096]{1,0:T(8,128)} %param.7) | copy-start | bytes 2457604
  1.9 13.9 %copy-start.1 = (bf16[1,2,2,16,4096]{4,3,2,1,0:T(8,128)(2,1)S(1)}, bf16[1,2,2,16,4096]{4,3,2,1,0:T(8,128)(2,1)}, u32[]{:S(2)}) copy-start(bf16[1,2,2,16,4096]{4,3,2,1,0:T(8,128)(2,1)} %kv_ref.3) | copy-start | bytes 1572868
  2.0 13.9 %copy-start.2 = (bf16[1,2,16,4096]{3,2,1,0:T(8,128)(2,1)S(1)}, bf16[1,2,16,4096]{3,2,1,0:T(8,128)(2,1)}, u32[]{:S(2)}) copy-start(bf16[1,2,16,4096]{3,2,1,0:T(8,128)(2,1)} %q_ref.3) | copy-start | bytes 786436
  2.0 30.1 %all-to-all-start = ((bf16[32,64,128]{2,1,0:T(8,128)(2,1)}), bf16[32,64,128]{2,1,0:T(8,128)(2,1)S(1)}, u32[]{:S(2)}, u32[]{:S(2)}) async-start(bf16[32,64,128]{2,1,0:T(8,128)(2,1)} %shard_map.46), calls=%async_computation | async-start | bytes 1048576 | tf_op jit(solution)/shard_map/all_to_all | solution.py:241
  16.5 0.7 copy-start.3

commit v5 on v4

--- a/solution.py
+++ b/solution.py
@@ -123,7 +123,6 @@
     row = lax.broadcasted_iota(jnp.int32, (BLOCK, BLOCK), 0)
     col = lax.broadcasted_iota(jnp.int32, (BLOCK, BLOCK), 1)
     same = row // TOK == col // TOK
-    lower = lax.broadcasted_iota(jnp.int32, (BLOCK, DEPTH), 1) < HALF
     n = BLOCK // TOK
     steps = [slice(step * NEAR, (step + 1) * NEAR) for step in range(2)]
     for step in range(2):
@@ -147,23 +146,13 @@
             total[here] = jnp.broadcast_to(added, (BLOCK, DEPTH))
             weight[here] = weights.astype(BF16)
     values = kv_ref[:, :, TOK:, :].reshape(TOKENS, DEPTH)
-    attn = score.at[:, 0:DEPTH]
     for step in range(2):
-        attn[steps[step]] = jnp.dot(weight[steps[step]], values, preferred_element_type=F32)
+        rows = steps[step]
+        attn = jnp.dot(weight[rows], values, preferred_element_type=F32) / total[rows]
+        out_ref[:, step * PAIRS : (step + 1) * PAIRS] = write_rows(attn)
     for i in range(NEAR // BLOCK):
-        zero = slice(i * BLOCK, (i + 1) * BLOCK)
-        one = slice(NEAR + i * BLOCK, NEAR + (i + 1) * BLOCK)
-        first = attn[zero] / total[zero]
-        second = attn[one] / total[one]
-        chunks = (
-            jnp.where(lower, first, pltpu.roll(second, HALF, 1)),
-            jnp.where(lower, pltpu.roll(first, HALF, 1), second),
-        )
-        stats = write_stats(top[one], total[one])
-        for core, chunk in enumerate(chunks):
-            at = slice(core * HEADS + i * n, core * HEADS + (i + 1) * n)
-            out_ref[at, 0:PAIRS] = write_rows(chunk)
-            out_ref[at, PAIRS] = stats
+        rows = slice(NEAR + i * BLOCK, NEAR + (i + 1) * BLOCK)
+        out_ref[i * n : (i + 1) * n, 2 * PAIRS] = write_stats(top[rows], total[rows])
 
 
 def near_kernel(near_ref, attn_ref, top_ref, total_ref):
@@ -175,12 +164,15 @@
 
 
 def merge_kernel(y_ref, near_ref, top_ref, total_ref, gate_ref, out_ref, held):
+    upper = lax.axis_index("cfg") == 1
     lower = lax.broadcasted_iota(jnp.int32, (NEAR, DEPTH), 1) < HALF
 
     def branch(b):
-        heads = slice(b * HEADS, (b + 1) * HEADS)
-        far = read_rows(y_ref[heads, 0:PAIRS])
-        far_top, far_total = read_stats(y_ref[heads, PAIRS])
+        first = read_rows(y_ref[b, :, 0:PAIRS])
+        second = read_rows(y_ref[b, :, PAIRS : 2 * PAIRS])
+        turned = pltpu.roll(jnp.where(upper, first, second), HALF, 1)
+        far = jnp.where(lower, jnp.where(upper, turned, first), jnp.where(upper, second, turned))
+        far_top, far_total = read_stats(y_ref[b, :, 2 * PAIRS])
         near_top = top_ref[b]
         top = jnp.maximum(far_top, near_top)
         far_share = jnp.exp2((far_top - top) * FACTOR) * far_total
@@ -220,9 +212,6 @@
     width = HEADS * DEPTH
     sides = [[SIDES * i + side for i in range(HEADS)] for side in range(SIDES)]
     patches = SIDES * HEADS
-    cores = [
-        [core * patches + patch for core in range(2) for patch in side] for side in sides
-    ]
     whole = pl.BlockSpec(memory_space=pltpu.HBM)
     sent = call(
         pack_kernel,
@@ -262,7 +251,7 @@
     )
     far = call(
         attend_kernel,
-        SHAPE((2 * HEADS, PAIRS + 1, 2, DEPTH), BF16),
+        SHAPE((HEADS, 2 * PAIRS + 1, 2, DEPTH), BF16),
         (held, stale),
         scratch=[
             pltpu.VMEM((ROWS, TOKENS), F32),
@@ -273,8 +262,9 @@
         flops=4 * ROWS * TOKENS * DEPTH,
     )
     back = lax.all_to_all(
-        far, ("cfg", "patch"), split_axis=0, concat_axis=0, tiled=True, axis_index_groups=cores
-    )
+        far, "patch", split_axis=0, concat_axis=0, tiled=True, axis_index_groups=sides
+    )
+    back = lax.all_gather(back, "cfg", axis=0, tiled=False)
     return call(
         merge_kernel,
         SHAPE((2, TOK, HEADS, HALF), BF16),

time: 72.4 us -> 74.8 us (1.033)
  the two profiles are of different devices: /device:TPU:1 before, /device:TPU:17 now
where the time goes in v5:
time: 74.8 us; the launch traced here: 74.5 us
  blocking collectives  41.7 us (56%)
  starting transfers between devices  13 us (17%)
  waiting for transfers between devices  10.8 us (14%)
  Pallas kernels  7.34 us (10%)
  local copies, waits for them, and re-layouts  1.42 us (2%)
    all_gather x1, blocking collectives, body(): lax.all_gather(held[:, 2 * TOK:, :], 'patch', axis=0, tiled=False, axis_i...  18.4 us
    all_to_all x1, blocking collectives, body(): lax.all_to_all(far, 'patch', split_axis=0, concat_axis=0, tiled=True, axi...  16.9 us
    all_to_all x1, starting transfers between devices, body(): lax.all_to_all(sent, 'patch', split_axis=0, concat_axis=0, tiled=True, ax...  13 us
    all_to_all x1, waiting for transfers between devices, body(): lax.all_to_all(sent, 'patch', split_axis=0, concat_axis=0, tiled=True, ax...  10.8 us
    pallas_call x5, Pallas kernels, call(): pl.pallas_call(kernel, grid=(1,), out_shape=out, in_specs=specs or [vmem]...  7.34 us
    all_gather x1, blocking collectives, body(): back = lax.all_gather(back, 'cfg', axis=0, tiled=False)  3.89 us
    all_gather x1, blocking collectives, body(): near = lax.all_gather(near, 'cfg', axis=0, tiled=False)  2.61 us
  transfers between devices with their start and end apart: 1, of which 1 were waited for; matrix products, arithmetic and copies ran while one was open for 1% of the time, Pallas kernels for 2%

profile of v5, /device:TPU:17, one launch (start us, length us, event | category | flops | bytes accessed | tf_op | source)
XLA Modules:
  0.0 74.5 jit_solution(3628328841570031920)
XLA Ops:
  0.0 0.0 copy-start
  0.0 1.9 %shard_map.46 = bf16[32,64,128]{2,1,0:T(8,128)(2,1)} custom-call(bf16[1,2,16,4096]{3,2,1,0:T(8,128)(2,1)} %q_ref.3, bf16[1,2,2,16,4096]{4,3,2,1,0:T(8,128)(2,1)} %kv_ref.3), custom_call_target="tpu_custom_call" | custom-call | bytes 1310720 | tf_op jit(solution)/shard_map/pallas_call | solution.py:199
  1.9 0.0 copy-start.1
  2.0 0.0 copy-start.2
  2.0 13.0 %all-to-all-start = ((bf16[32,64,128]{2,1,0:T(8,128)(2,1)}), bf16[32,64,128]{2,1,0:T(8,128)(2,1)S(1)}, u32[]{:S(2)}, u32[]{:S(2)}) async-start(bf16[32,64,128]{2,1,0:T(8,128)(2,1)} %shard_map.46), calls=%async_computation | async-start | bytes 1048576 | tf_op jit(solution)/shard_map/all_to_all | solution.py:230
  15.0 0.0 copy-done.1
  15.0 0.0 copy-done.2
  15.0 0.7 shard_map.47
  15.7 0.0 copy-start.3
  15.7 0.7 copy-done.3
  16.4 0.0 copy-done
  16.4 0.6 gather_fusion
  16.9 0.1 reshape.7
  17.1 2.6 %all-gather = bf16[64,9,2,128]{3,2,1,0:T(2,128)(2,1)S(1)} all-gather(bf16[32,9,2,128]{3,2,1,0:T(2,128)(2,1)S(1)} %shard_map.47), channel_id=2, replica_groups=mesh['clip'=4,'cfg'=2,'patch'=64] {'cfg'}, dimensions={0}, use_global_device_ids=true | all-gather | bytes 442368 | tf_op jit(solution)/shard_map/all_gather | solution.py:242
  19.7 0.7 shard_map.48
  20.4 0.1 pad_maximum_fusion.gate_ref
  20.5 10.8 %all-to-all-done.x_ref = bf16[32,64,128]{2,1,0:T(8,128)(2,1)S(1)} async-done(((bf16[32,64,128]{2,1,0:T(8,128)(2,1)}), bf16[32,64,128]{2,1,0:T(8,128)(2,1)S(1)}, u32[]{:S(2)}, u32[]{:S(2)}) %all-to-all-start) | async-done | bytes 524320 | tf_op jit(solution)/shard_map/all_to_all | solution.py:230
  31.3 18.4 %all-gather.1 = bf16[64,32,128]{2,1,0:T(8,128)(2,1)S(1)} all-gather(bf16[32,32,128]{2,1,0:T(8,128)(2,1)S(1)} %slice.13), channel_id=3, replica_groups={{0,1},{2,3},{4,5},{6,7},{8,9},{10,11},{12,13},{14,15},{16,17},{18,19},{..., dimensions={0}, use_global_device_ids=true | all-gather | bytes 786432 | tf_op jit(solution)/shard_map/all_gather | solution.py:249
  49.7 1.8 %shard_map.49 = bf16[32,17,2,128]{3,2,1,0:T(2,128)(2,1)S(1)} custom-call(bf16[32,64,128]{2,1,0:T(8,128)(2,1)S(1)} %all-to-all-done.x_ref, bf16[2,32,32,128]{3,2,1,0:T(8,128)(2,1)S(1)} %bitcast.12), custom_call_target="tpu_custom_call" | custom-call | flops 536870912 | bytes 1327104 | tf_op jit(solution)/shard_map/pallas_call | solution.py:199
  51.5 16.9 %all_to_all.10 = bf16[32,17,2,128]{3,2,1,0:T(2,128)(2,1)S(1)} all-to-all(bf16[32,17,2,128]{3,2,1,0:T(2,128)(2,1)S(1)} %shard_map.49), channel_id=1, replica_groups={{0,2,4,6,8,10,12,14,16,18,20,22,24,26,28,30,32,34,36,38,40,42,44,46,48,..., dimensions={0} | all-to-all | bytes 557056 | tf_op jit(solution)/shard_map/all_to_all | solution.py:264
  68.4 3.9 %all-gather.2 = bf16[64,17,2,128]{3,2,1,0:T(2,128)(2,1)S(1)} all-gather(bf16[32,17,2,128]{3,2,1,0:T(2,128)(2,1)S(1)} %all_to_all.10), channel_id=4, replica_groups=mesh['clip'=4,'cfg'=2,'patch'=64] {'cfg'}, dimensions={0}, use_global_device_ids=true | all-gather | bytes 835584 | tf_op jit(solution)/shard_map/all_gather | solution.py:267
  72.3 2.2 %shard_map.50 = bf16[2,16,32,64]{3,2,1,0:T(8,128)(2,1)} custom-call(bf16[2,32,17,2,128]{4,3,2,1,0:T(2,128)(2,1)S(1)} %bitcast.10, f32[2,512,128]{2,1,0:T(8,128)S(1)} %get-tuple-element.17.near_ref, f32[2,512,128]{2,1,0:T(8,128)S(1)} %get-tuple-element.18.top_ref, f32[2,512,128]{2,1,0:T(8,128)S(1)} %get-tuple-element.19.total_ref, ...), custom_call_target="tpu_custom_call" | custom-call | bytes 2277376 | tf_op jit(solution)/shard_map/pallas_call | solution.py:199
  (3 shorter events, 0.1 us)
Async XLA Ops:
  0.0 16.4 %copy-start = (f32[50,4096]{1,0:T(8,128)S(1)}, f32[50,4096]{1,0:T(8,128)}, u32[]{:S(2)}) copy-start(f32[50,4096]{1,0:T(8,128)} %param.7) | copy-start | bytes 2457604
  1.9 13.1 %copy-start.1 = (bf16[1,2,2,16,4096]{4,3,2,1,0:T(8,128)(2,1)S(1)}, bf16[1,2,2,16,4096]{4,3,2,1,0:T(8,128)(2,1)}, u32[]{:S(2)}) copy-start(bf16[1,2,2,16,4096]{4,3,2,1,0:T(8,128)(2,1)} %kv_ref.3) | copy-start | bytes 1572868
  2.0 13.1 %copy-start.2 = (bf16[1,2,16,4096]{3,2,1,0:T(8,128)(2,1)S(1)}, bf16[1,2,16,4096]{3,2,1,0:T(8,128)(2,1)}, u32[]{:S(2)}) copy-start(bf16[1,2,16,4096]{3,2,1,0:T(8,128)(2,1)} %q_ref.3) | copy-start | bytes 786436
  2.0 29.3 %all-to-all-start = ((bf16[32,64,128]{2,1,0:T(8,128)(2,1)}), bf16[32,64,128]{2,1,0:T(8,128)(2,1)S(1)}, u32[]{:S(2)}, u32[]{:S(2)}) async-start(bf16[32,64,128]{2,1,0:T(8,128)(2,1)} %shard_map.46), calls=%async_computation | async-start | bytes 1048576 | tf_op jit(solution)/shard_map/all_to_all | solution.py:230
  15.7 0.7 copy-start.3

commit v6 on v4

--- a/solution.py
+++ b/solution.py
@@ -12,6 +12,7 @@
 HALF = DEPTH // 2
 TOK = 16
 SIDES = 2
+SIDE_STRIDE = 2
 NEAR = HEADS * TOK
 ROWS = 2 * NEAR
 PAIRS = TOK // 2
@@ -119,7 +120,7 @@
 
 
 def attend_kernel(x_ref, kv_ref, out_ref, score, weight, top, total):
-    side = lax.axis_index("patch") % SIDES
+    side = lax.axis_index("patch") // SIDE_STRIDE % SIDES
     row = lax.broadcasted_iota(jnp.int32, (BLOCK, BLOCK), 0)
     col = lax.broadcasted_iota(jnp.int32, (BLOCK, BLOCK), 1)
     same = row // TOK == col // TOK
@@ -218,8 +219,10 @@
 
 def body(queries, keys_values, timesteps, gate_table):
     width = HEADS * DEPTH
-    sides = [[SIDES * i + side for i in range(HEADS)] for side in range(SIDES)]
     patches = SIDES * HEADS
+    sides = [
+        [p for p in range(patches) if p // SIDE_STRIDE % SIDES == side] for side in range(SIDES)
+    ]
     cores = [
         [core * patches + patch for core in range(2) for patch in side] for side in sides
     ]
@@ -256,7 +259,7 @@
     gate = lax.dynamic_index_in_dim(gates, lax.axis_index("cfg"), 2, keepdims=False)
     gate = jnp.concatenate([gate[0], gate[1]], axis=1)
     held, near, gate = lax.optimization_barrier((held, near, gate))
-    pairs = [[SIDES * i, SIDES * i + 1] for i in range(HEADS)]
+    pairs = [[p, p + SIDE_STRIDE] for p in sides[0]]
     stale = lax.all_gather(
         held[:, 2 * TOK :, :], "patch", axis=0, tiled=False, axis_index_groups=pairs
     )

time: 72.4 us -> 78.3 us (1.081)
  the two profiles are of different devices: /device:TPU:1 before, /device:TPU:9 now
where the time goes in v6:
time: 78.3 us; the launch traced here: 78 us
  blocking collectives  33.6 us (43%)
  waiting for transfers between devices  18.7 us (24%)
  starting transfers between devices  17.4 us (22%)
  Pallas kernels  6.77 us (9%)
  local copies, waits for them, and re-layouts  1.42 us (2%)
    all_to_all x1, blocking collectives, body(): lax.all_to_all(far, ('cfg', 'patch'), split_axis=0, concat_axis=0, tiled=...  23.6 us
    all_to_all x1, waiting for transfers between devices, body(): lax.all_to_all(sent, 'patch', split_axis=0, concat_axis=0, tiled=True, ax...  18.7 us
    all_to_all x1, starting transfers between devices, body(): lax.all_to_all(sent, 'patch', split_axis=0, concat_axis=0, tiled=True, ax...  17.4 us
    all_gather x1, blocking collectives, body(): lax.all_gather(held[:, 2 * TOK:, :], 'patch', axis=0, tiled=False, axis_i...  7.39 us
    pallas_call x5, Pallas kernels, call(): pl.pallas_call(kernel, grid=(1,), out_shape=out, in_specs=specs or [vmem]...  6.77 us
    all_gather x1, blocking collectives, body(): near = lax.all_gather(near, 'cfg', axis=0, tiled=False)  2.61 us
  transfers between devices with their start and end apart: 1, of which 1 were waited for; matrix products, arithmetic and copies ran while one was open for 1% of the time, Pallas kernels for 2%

profile of v6, /device:TPU:9, one launch (start us, length us, event | category | flops | bytes accessed | tf_op | source)
XLA Modules:
  0.0 78.0 jit_solution(15649726225161558786)
XLA Ops:
  0.0 0.0 copy-start
  0.0 1.9 %shard_map.46 = bf16[32,64,128]{2,1,0:T(8,128)(2,1)} custom-call(bf16[1,2,16,4096]{3,2,1,0:T(8,128)(2,1)} %q_ref.3, bf16[1,2,2,16,4096]{4,3,2,1,0:T(8,128)(2,1)} %kv_ref.3), custom_call_target="tpu_custom_call" | custom-call | bytes 1310720 | tf_op jit(solution)/shard_map/pallas_call | solution.py:208
  1.9 0.0 copy-start.1
  2.0 0.0 copy-start.2
  2.0 17.4 %all-to-all-start = ((bf16[32,64,128]{2,1,0:T(8,128)(2,1)}), bf16[32,64,128]{2,1,0:T(8,128)(2,1)S(1)}, u32[]{:S(2)}, u32[]{:S(2)}) async-start(bf16[32,64,128]{2,1,0:T(8,128)(2,1)} %shard_map.46), calls=%async_computation | async-start | bytes 1048576 | tf_op jit(solution)/shard_map/all_to_all | solution.py:244
  19.4 0.0 copy-done.1
  19.4 0.0 copy-done.2
  19.4 0.7 shard_map.47
  20.1 0.0 copy-start.3
  20.1 0.7 copy-done.3
  20.7 0.0 copy-done
  20.7 0.6 gather_fusion
  21.3 0.1 reshape.7
  21.4 2.6 %all-gather = bf16[64,9,2,128]{3,2,1,0:T(2,128)(2,1)S(1)} all-gather(bf16[32,9,2,128]{3,2,1,0:T(2,128)(2,1)S(1)} %shard_map.47), channel_id=2, replica_groups=mesh['clip'=4,'cfg'=2,'patch'=64] {'cfg'}, dimensions={0}, use_global_device_ids=true | all-gather | bytes 442368 | tf_op jit(solution)/shard_map/all_gather | solution.py:256
  24.0 0.7 shard_map.48
  24.8 0.1 pad_maximum_fusion.gate_ref
  24.8 18.7 %all-to-all-done.x_ref = bf16[32,64,128]{2,1,0:T(8,128)(2,1)S(1)} async-done(((bf16[32,64,128]{2,1,0:T(8,128)(2,1)}), bf16[32,64,128]{2,1,0:T(8,128)(2,1)S(1)}, u32[]{:S(2)}, u32[]{:S(2)}) %all-to-all-start) | async-done | bytes 524320 | tf_op jit(solution)/shard_map/all_to_all | solution.py:244
  43.5 7.4 %all-gather.1 = bf16[64,32,128]{2,1,0:T(8,128)(2,1)S(1)} all-gather(bf16[32,32,128]{2,1,0:T(8,128)(2,1)S(1)} %slice.13), channel_id=3, replica_groups={{0,2},{1,3},{4,6},{5,7},{8,10},{9,11},{12,14},{13,15},{16,18},{17,19},{..., dimensions={0}, use_global_device_ids=true | all-gather | bytes 786432 | tf_op jit(solution)/shard_map/all_gather | solution.py:263
  50.9 1.9 %shard_map.49 = bf16[64,9,2,128]{3,2,1,0:T(2,128)(2,1)S(1)} custom-call(bf16[32,64,128]{2,1,0:T(8,128)(2,1)S(1)} %all-to-all-done.x_ref, bf16[2,32,32,128]{3,2,1,0:T(8,128)(2,1)S(1)} %bitcast.10), custom_call_target="tpu_custom_call" | custom-call | flops 536870912 | bytes 1343488 | tf_op jit(solution)/shard_map/pallas_call | solution.py:208
  52.8 23.6 %all_to_all.10.y_ref = bf16[64,9,2,128]{3,2,1,0:T(2,128)(2,1)S(1)} all-to-all(bf16[64,9,2,128]{3,2,1,0:T(2,128)(2,1)S(1)} %shard_map.49), channel_id=1, replica_groups={{0,1,4,5,8,9,12,13,16,17,20,21,24,25,28,29,32,33,36,37,40,41,44,45,48,4..., dimensions={0} | all-to-all | bytes 589824 | tf_op jit(solution)/shard_map/all_to_all | solution.py:278
  76.4 1.6 %shard_map.50 = bf16[2,16,32,64]{3,2,1,0:T(8,128)(2,1)} custom-call(bf16[64,9,2,128]{3,2,1,0:T(2,128)(2,1)S(1)} %all_to_all.10.y_ref, f32[2,512,128]{2,1,0:T(8,128)S(1)} %get-tuple-element.17.near_ref, f32[2,512,128]{2,1,0:T(8,128)S(1)} %get-tuple-element.18.top_ref, f32[2,512,128]{2,1,0:T(8,128)S(1)} %get-tuple-element.19.total_ref, ...), custom_call_target="tpu_custom_call" | custom-call | bytes 2015232 | tf_op jit(solution)/shard_map/pallas_call | solution.py:208
  (3 shorter events, 0.1 us)
Async XLA Ops:
  0.0 20.7 %copy-start = (f32[50,4096]{1,0:T(8,128)S(1)}, f32[50,4096]{1,0:T(8,128)}, u32[]{:S(2)}) copy-start(f32[50,4096]{1,0:T(8,128)} %param.7) | copy-start | bytes 2457604
  1.9 17.4 %copy-start.1 = (bf16[1,2,2,16,4096]{4,3,2,1,0:T(8,128)(2,1)S(1)}, bf16[1,2,2,16,4096]{4,3,2,1,0:T(8,128)(2,1)}, u32[]{:S(2)}) copy-start(bf16[1,2,2,16,4096]{4,3,2,1,0:T(8,128)(2,1)} %kv_ref.3) | copy-start | bytes 1572868
  2.0 17.4 %copy-start.2 = (bf16[1,2,16,4096]{3,2,1,0:T(8,128)(2,1)S(1)}, bf16[1,2,16,4096]{3,2,1,0:T(8,128)(2,1)}, u32[]{:S(2)}) copy-start(bf16[1,2,16,4096]{3,2,1,0:T(8,128)(2,1)} %q_ref.3) | copy-start | bytes 786436
  2.0 41.5 %all-to-all-start = ((bf16[32,64,128]{2,1,0:T(8,128)(2,1)}), bf16[32,64,128]{2,1,0:T(8,128)(2,1)S(1)}, u32[]{:S(2)}, u32[]{:S(2)}) async-start(bf16[32,64,128]{2,1,0:T(8,128)(2,1)} %shard_map.46), calls=%async_computation | async-start | bytes 1048576 | tf_op jit(solution)/shard_map/all_to_all | solution.py:244
  20.1 0.7 copy-start.3

commit v7 on v4

--- a/solution.py
+++ b/solution.py
@@ -31,21 +31,41 @@
 
 def pack_kernel(q_ref, kv_ref, out_ref, held, packed, in_sems, out_sems):
     fields = [q_ref.at[0, 0], q_ref.at[0, 1], kv_ref.at[0, 0, 0], kv_ref.at[0, 0, 1]]
-    copies = [
+    loads = [
         pltpu.make_async_copy(field, held.at[i], in_sems.at[i]) for i, field in enumerate(fields)
     ]
-    for copy in copies:
-        copy.start()
-    results = []
-    for i, copy in enumerate(copies):
-        copy.wait()
+    stores = [
+        pltpu.make_async_copy(
+            packed.at[i], out_ref.at[:, i * TOK : (i + 1) * TOK, :], out_sems.at[i]
+        )
+        for i in range(len(fields))
+    ]
+
+    def by_head(i):
         for h in range(HEADS):
             packed[i, h] = held[i, :, h * DEPTH : (h + 1) * DEPTH]
-        rows = out_ref.at[:, i * TOK : (i + 1) * TOK, :]
-        results.append(pltpu.make_async_copy(packed.at[i], rows, out_sems.at[i]))
-        results[-1].start()
-    for result in results:
-        result.wait()
+
+    odd = lax.axis_index("cfg") == 1
+
+    @pl.when(odd)
+    def _():
+        for load in loads:
+            load.start()
+        for i, load in enumerate(loads):
+            load.wait()
+            by_head(i)
+            stores[i].start()
+        for store in stores:
+            store.wait()
+
+    @pl.when(jnp.logical_not(odd))
+    def _():
+        for i, load in enumerate(loads):
+            load.start()
+            load.wait()
+            by_head(i)
+            stores[i].start()
+            stores[i].wait()
 
 
 def split_value(value):

time: 72.4 us -> 70.6 us (0.975); the launches traced: 71.3 us -> 70.2 us
  waiting for transfers between devices: 10.8 us -> 2.81 us
  blocking collectives: 38.3 us -> 45.2 us
    all_to_all x1, waiting for transfers between devices: 10.8 us -> 2.81 us  [body(): lax.all_to_all(sent, 'patch', split_axis=0, concat_axis=0, tiled=True, ax...]
    all_gather x1, blocking collectives: 2.61 us -> 7.19 us  [body(): near = lax.all_gather(near, 'cfg', axis=0, tiled=False)]
    all_to_all x1, blocking collectives: 25.3 us -> 28 us  [body(): lax.all_to_all(far, ('cfg', 'patch'), split_axis=0, concat_axis=0, tiled=...]
where the time goes in v7:
time: 70.6 us; the launch traced here: 70.2 us
  blocking collectives  45.2 us (64%)
  starting transfers between devices  13.9 us (20%)
  Pallas kernels  6.76 us (10%)
  waiting for transfers between devices  2.81 us (4%)
  local copies, waits for them, and re-layouts  1.42 us (2%)
    all_to_all x1, blocking collectives, body(): lax.all_to_all(far, ('cfg', 'patch'), split_axis=0, concat_axis=0, tiled=...  28 us
    all_to_all x1, starting transfers between devices, body(): lax.all_to_all(sent, 'patch', split_axis=0, concat_axis=0, tiled=True, ax...  13.9 us
    all_gather x1, blocking collectives, body(): lax.all_gather(held[:, 2 * TOK:, :], 'patch', axis=0, tiled=False, axis_i...  10.1 us
    all_gather x1, blocking collectives, body(): near = lax.all_gather(near, 'cfg', axis=0, tiled=False)  7.19 us
    pallas_call x5, Pallas kernels, call(): pl.pallas_call(kernel, grid=(1,), out_shape=out, in_specs=specs or [vmem]...  6.76 us
    all_to_all x1, waiting for transfers between devices, body(): lax.all_to_all(sent, 'patch', split_axis=0, concat_axis=0, tiled=True, ax...  2.81 us
  transfers between devices with their start and end apart: 1, of which 1 were waited for; matrix products, arithmetic and copies ran while one was open for 1% of the time, Pallas kernels for 2%

profile of v7, /device:TPU:1, one launch (start us, length us, event | category | flops | bytes accessed | tf_op | source)
XLA Modules:
  0.0 70.2 jit_solution(5691606591891024011)
XLA Ops:
  0.0 0.0 copy-start
  0.0 1.9 %shard_map.46 = bf16[32,64,128]{2,1,0:T(8,128)(2,1)} custom-call(bf16[1,2,16,4096]{3,2,1,0:T(8,128)(2,1)} %q_ref.3, bf16[1,2,2,16,4096]{4,3,2,1,0:T(8,128)(2,1)} %kv_ref.3), custom_call_target="tpu_custom_call" | custom-call | bytes 1310720 | tf_op jit(solution)/shard_map/pallas_call | solution.py:227
  1.9 0.0 copy-start.1
  2.0 0.0 copy-start.2
  2.0 13.9 %all-to-all-start = ((bf16[32,64,128]{2,1,0:T(8,128)(2,1)}), bf16[32,64,128]{2,1,0:T(8,128)(2,1)S(1)}, u32[]{:S(2)}, u32[]{:S(2)}) async-start(bf16[32,64,128]{2,1,0:T(8,128)(2,1)} %shard_map.46), calls=%async_computation | async-start | bytes 1048576 | tf_op jit(solution)/shard_map/all_to_all | solution.py:261
  15.8 0.0 copy-done.1
  15.9 0.0 copy-done.2
  15.9 0.7 shard_map.47
  16.5 0.0 copy-start.3
  16.5 0.7 copy-done.3
  17.2 0.0 copy-done
  17.2 0.6 gather_fusion
  17.8 0.1 reshape.7
  17.9 7.2 %all-gather = bf16[64,9,2,128]{3,2,1,0:T(2,128)(2,1)S(1)} all-gather(bf16[32,9,2,128]{3,2,1,0:T(2,128)(2,1)S(1)} %shard_map.47), channel_id=2, replica_groups=mesh['clip'=4,'cfg'=2,'patch'=64] {'cfg'}, dimensions={0}, use_global_device_ids=true | all-gather | bytes 442368 | tf_op jit(solution)/shard_map/all_gather | solution.py:273
  25.1 0.7 shard_map.48
  25.8 0.1 pad_maximum_fusion.gate_ref
  25.9 2.8 %all-to-all-done.x_ref = bf16[32,64,128]{2,1,0:T(8,128)(2,1)S(1)} async-done(((bf16[32,64,128]{2,1,0:T(8,128)(2,1)}), bf16[32,64,128]{2,1,0:T(8,128)(2,1)S(1)}, u32[]{:S(2)}, u32[]{:S(2)}) %all-to-all-start) | async-done | bytes 524320 | tf_op jit(solution)/shard_map/all_to_all | solution.py:261
  28.7 10.1 %all-gather.1 = bf16[64,32,128]{2,1,0:T(8,128)(2,1)S(1)} all-gather(bf16[32,32,128]{2,1,0:T(8,128)(2,1)S(1)} %slice.13), channel_id=3, replica_groups={{0,1},{2,3},{4,5},{6,7},{8,9},{10,11},{12,13},{14,15},{16,17},{18,19},{..., dimensions={0}, use_global_device_ids=true | all-gather | bytes 786432 | tf_op jit(solution)/shard_map/all_gather | solution.py:280
  38.8 1.9 %shard_map.49 = bf16[64,9,2,128]{3,2,1,0:T(2,128)(2,1)S(1)} custom-call(bf16[32,64,128]{2,1,0:T(8,128)(2,1)S(1)} %all-to-all-done.x_ref, bf16[2,32,32,128]{3,2,1,0:T(8,128)(2,1)S(1)} %bitcast.10), custom_call_target="tpu_custom_call" | custom-call | flops 536870912 | bytes 1343488 | tf_op jit(solution)/shard_map/pallas_call | solution.py:227
  40.7 28.0 %all_to_all.10.y_ref = bf16[64,9,2,128]{3,2,1,0:T(2,128)(2,1)S(1)} all-to-all(bf16[64,9,2,128]{3,2,1,0:T(2,128)(2,1)S(1)} %shard_map.49), channel_id=1, replica_groups={{0,2,4,6,8,10,12,14,16,18,20,22,24,26,28,30,32,34,36,38,40,42,44,46,48,..., dimensions={0} | all-to-all | bytes 589824 | tf_op jit(solution)/shard_map/all_to_all | solution.py:295
  68.7 1.6 %shard_map.50 = bf16[2,16,32,64]{3,2,1,0:T(8,128)(2,1)} custom-call(bf16[64,9,2,128]{3,2,1,0:T(2,128)(2,1)S(1)} %all_to_all.10.y_ref, f32[2,512,128]{2,1,0:T(8,128)S(1)} %get-tuple-element.17.near_ref, f32[2,512,128]{2,1,0:T(8,128)S(1)} %get-tuple-element.18.top_ref, f32[2,512,128]{2,1,0:T(8,128)S(1)} %get-tuple-element.19.total_ref, ...), custom_call_target="tpu_custom_call" | custom-call | bytes 2015232 | tf_op jit(solution)/shard_map/pallas_call | solution.py:227
  (3 shorter events, 0.1 us)
Async XLA Ops:
  0.0 17.2 %copy-start = (f32[50,4096]{1,0:T(8,128)S(1)}, f32[50,4096]{1,0:T(8,128)}, u32[]{:S(2)}) copy-start(f32[50,4096]{1,0:T(8,128)} %param.7) | copy-start | bytes 2457604
  1.9 13.9 %copy-start.1 = (bf16[1,2,2,16,4096]{4,3,2,1,0:T(8,128)(2,1)S(1)}, bf16[1,2,2,16,4096]{4,3,2,1,0:T(8,128)(2,1)}, u32[]{:S(2)}) copy-start(bf16[1,2,2,16,4096]{4,3,2,1,0:T(8,128)(2,1)} %kv_ref.3) | copy-start | bytes 1572868
  2.0 13.9 %copy-start.2 = (bf16[1,2,16,4096]{3,2,1,0:T(8,128)(2,1)S(1)}, bf16[1,2,16,4096]{3,2,1,0:T(8,128)(2,1)}, u32[]{:S(2)}) copy-start(bf16[1,2,16,4096]{3,2,1,0:T(8,128)(2,1)} %q_ref.3) | copy-start | bytes 786436
  2.0 26.7 %all-to-all-start = ((bf16[32,64,128]{2,1,0:T(8,128)(2,1)}), bf16[32,64,128]{2,1,0:T(8,128)(2,1)S(1)}, u32[]{:S(2)}, u32[]{:S(2)}) async-start(bf16[32,64,128]{2,1,0:T(8,128)(2,1)} %shard_map.46), calls=%async_computation | async-start | bytes 1048576 | tf_op jit(solution)/shard_map/all_to_all | solution.py:261
  16.5 0.7 copy-start.3

commit v8 on v7

--- a/solution.py
+++ b/solution.py
@@ -116,7 +116,7 @@
     return pairs.astype(F32).reshape(-1, DEPTH)
 
 
-def local_kernel(q_ref, kv_ref, out_ref):
+def local_kernel(q_ref, kv_ref, attn_ref, top_ref, total_ref):
     n = GROUP * TOK
     row = lax.broadcasted_iota(jnp.int32, (n, n), 0)
     col = lax.broadcasted_iota(jnp.int32, (n, n), 1)
@@ -133,9 +133,10 @@
         weight = jnp.exp2((score - top) * FACTOR)
         total = jnp.sum(weight, axis=1, keepdims=True)
         summed = jnp.dot(weight.astype(BF16), value, preferred_element_type=F32)
-        here = slice(g * GROUP, (g + 1) * GROUP)
-        out_ref[here, 0:PAIRS] = write_rows(summed / total)
-        out_ref[here, PAIRS] = write_stats(top, total)
+        here = slice(g * n, (g + 1) * n)
+        attn_ref[here] = summed / total
+        top_ref[here] = jnp.broadcast_to(top, (n, DEPTH))
+        total_ref[here] = jnp.broadcast_to(total, (n, DEPTH))
 
 
 def attend_kernel(x_ref, kv_ref, out_ref, score, weight, top, total):
@@ -143,7 +144,6 @@
     row = lax.broadcasted_iota(jnp.int32, (BLOCK, BLOCK), 0)
     col = lax.broadcasted_iota(jnp.int32, (BLOCK, BLOCK), 1)
     same = row // TOK == col // TOK
-    lower = lax.broadcasted_iota(jnp.int32, (BLOCK, DEPTH), 1) < HALF
     n = BLOCK // TOK
     steps = [slice(step * NEAR, (step + 1) * NEAR) for step in range(2)]
     for step in range(2):
@@ -167,49 +167,33 @@
             total[here] = jnp.broadcast_to(added, (BLOCK, DEPTH))
             weight[here] = weights.astype(BF16)
     values = kv_ref[:, :, TOK:, :].reshape(TOKENS, DEPTH)
-    attn = score.at[:, 0:DEPTH]
     for step in range(2):
-        attn[steps[step]] = jnp.dot(weight[steps[step]], values, preferred_element_type=F32)
+        rows = steps[step]
+        attn = jnp.dot(weight[rows], values, preferred_element_type=F32) / total[rows]
+        out_ref[:, step * PAIRS : (step + 1) * PAIRS] = write_rows(attn)
     for i in range(NEAR // BLOCK):
-        zero = slice(i * BLOCK, (i + 1) * BLOCK)
-        one = slice(NEAR + i * BLOCK, NEAR + (i + 1) * BLOCK)
-        first = attn[zero] / total[zero]
-        second = attn[one] / total[one]
-        chunks = (
-            jnp.where(lower, first, pltpu.roll(second, HALF, 1)),
-            jnp.where(lower, pltpu.roll(first, HALF, 1), second),
-        )
-        stats = write_stats(top[one], total[one])
-        for core, chunk in enumerate(chunks):
-            at = slice(core * HEADS + i * n, core * HEADS + (i + 1) * n)
-            out_ref[at, 0:PAIRS] = write_rows(chunk)
-            out_ref[at, PAIRS] = stats
-
-
-def near_kernel(near_ref, attn_ref, top_ref, total_ref):
-    upper = lax.axis_index("cfg") == 1
-    for b in range(2):
-        near = read_rows(near_ref[b, :, 0:PAIRS])
-        attn_ref[b] = jnp.where(upper, near, pltpu.roll(near, HALF, 1))
-        top_ref[b], total_ref[b] = read_stats(near_ref[b, :, PAIRS])
-
-
-def merge_kernel(y_ref, near_ref, top_ref, total_ref, gate_ref, out_ref, held):
+        rows = slice(NEAR + i * BLOCK, NEAR + (i + 1) * BLOCK)
+        out_ref[i * n : (i + 1) * n, 2 * PAIRS] = write_stats(top[rows], total[rows])
+
+
+def merge_kernel(y_ref, near_ref, top_ref, total_ref, out_ref):
     lower = lax.broadcasted_iota(jnp.int32, (NEAR, DEPTH), 1) < HALF
-
-    def branch(b):
-        heads = slice(b * HEADS, (b + 1) * HEADS)
-        far = read_rows(y_ref[heads, 0:PAIRS])
-        far_top, far_total = read_stats(y_ref[heads, PAIRS])
-        near_top = top_ref[b]
-        top = jnp.maximum(far_top, near_top)
-        far_share = jnp.exp2((far_top - top) * FACTOR) * far_total
-        near_share = jnp.exp2((near_top - top) * FACTOR) * total_ref[b]
-        both = (far_share * far + near_share * near_ref[b]) / (far_share + near_share)
-        return jnp.where(lower, far, both).astype(BF16).astype(F32)
-
-    cond = branch(0)
-    uncond = branch(1)
+    first = read_rows(y_ref[:, 0:PAIRS])
+    far = read_rows(y_ref[:, PAIRS : 2 * PAIRS])
+    far_top, far_total = read_stats(y_ref[:, 2 * PAIRS])
+    near_top = top_ref[...]
+    top = jnp.maximum(far_top, near_top)
+    far_share = jnp.exp2((far_top - top) * FACTOR) * far_total
+    near_share = jnp.exp2((near_top - top) * FACTOR) * total_ref[...]
+    second = (far_share * far + near_share * near_ref[...]) / (far_share + near_share)
+    out_ref[0] = jnp.where(lower, first, pltpu.roll(second, HALF, 1)).astype(BF16)
+    out_ref[1] = jnp.where(lower, pltpu.roll(first, HALF, 1), second).astype(BF16)
+
+
+def guide_kernel(both_ref, gate_ref, out_ref, held):
+    core = lax.axis_index("cfg")
+    cond = both_ref[0, core].astype(F32)
+    uncond = both_ref[1, core].astype(F32)
     mixed = (uncond + 5.0 * (cond - uncond)).reshape(HEADS, TOK, DEPTH)
     held[...] = (gate_ref[...].reshape(HEADS, 1, DEPTH) * mixed).reshape(NEAR, DEPTH)
     for t in range(TOK):
@@ -240,9 +224,6 @@
     width = HEADS * DEPTH
     sides = [[SIDES * i + side for i in range(HEADS)] for side in range(SIDES)]
     patches = SIDES * HEADS
-    cores = [
-        [core * patches + patch for core in range(2) for patch in side] for side in sides
-    ]
     whole = pl.BlockSpec(memory_space=pltpu.HBM)
     sent = call(
         pack_kernel,
@@ -263,15 +244,13 @@
     )
     near = call(
         local_kernel,
-        SHAPE((HEADS, PAIRS + 1, 2, DEPTH), BF16),
+        [SHAPE((NEAR, DEPTH), F32)] * 3,
         (queries, keys_values),
         [
             pl.BlockSpec((None, 1, TOK, width), lambda i: (0, 1, 0, 0)),
             pl.BlockSpec((None, None, 2, TOK, width), lambda i: (0, 1, 0, 0, 0)),
         ],
     )
-    near = lax.all_gather(near, "cfg", axis=0, tiled=False)
-    near = call(near_kernel, [SHAPE((2, NEAR, DEPTH), F32)] * 3, (near,))
     gates = jnp.take(gate_table, timesteps, axis=0, mode="clip").reshape(2, HEADS, 2, HALF)
     gate = lax.dynamic_index_in_dim(gates, lax.axis_index("cfg"), 2, keepdims=False)
     gate = jnp.concatenate([gate[0], gate[1]], axis=1)
@@ -282,7 +261,7 @@
     )
     far = call(
         attend_kernel,
-        SHAPE((2 * HEADS, PAIRS + 1, 2, DEPTH), BF16),
+        SHAPE((HEADS, 2 * PAIRS + 1, 2, DEPTH), BF16),
         (held, stale),
         scratch=[
             pltpu.VMEM((ROWS, TOKENS), F32),
@@ -293,12 +272,14 @@
         flops=4 * ROWS * TOKENS * DEPTH,
     )
     back = lax.all_to_all(
-        far, ("cfg", "patch"), split_axis=0, concat_axis=0, tiled=True, axis_index_groups=cores
-    )
+        far, "patch", split_axis=0, concat_axis=0, tiled=True, axis_index_groups=sides
+    )
+    attn = call(merge_kernel, SHAPE((2, NEAR, DEPTH), BF16), (back, *near))
+    both = lax.all_gather(attn, "cfg", axis=0, tiled=False)
     return call(
-        merge_kernel,
+        guide_kernel,
         SHAPE((2, TOK, HEADS, HALF), BF16),
-        (back, *near, gate),
+        (both, gate),
         scratch=[pltpu.VMEM((NEAR, DEPTH), F32)],
     )
 

time: 70.6 us -> 70.4 us (level)
  waiting for transfers between devices: 2.81 us -> 10.3 us
  blocking collectives: 45.2 us -> 38 us
    all_to_all x1, blocking collectives: 28 us -> 14.5 us  [body(): lax.all_to_all(far, 'patch', split_axis=0, concat_axis=0, tiled=True, axi...]
    all_to_all x1, waiting for transfers between devices: 2.81 us -> 10.3 us  [body(): lax.all_to_all(sent, 'patch', split_axis=0, concat_axis=0, tiled=True, ax...]
    all_gather x1, blocking collectives: 7.19 us -> 13.4 us  [body(): both = lax.all_gather(attn, 'cfg', axis=0, tiled=False)]
where the time goes in v8:
time: 70.4 us; the launch traced here: 70.1 us
  blocking collectives  38 us (54%)
  starting transfers between devices  13.9 us (20%)
  waiting for transfers between devices  10.3 us (15%)
  Pallas kernels  6.33 us (9%)
  local copies, waits for them, and re-layouts  1.41 us (2%)
    all_to_all x1, blocking collectives, body(): lax.all_to_all(far, 'patch', split_axis=0, concat_axis=0, tiled=True, axi...  14.5 us
    all_to_all x1, starting transfers between devices, body(): lax.all_to_all(sent, 'patch', split_axis=0, concat_axis=0, tiled=True, ax...  13.9 us
    all_gather x1, blocking collectives, body(): both = lax.all_gather(attn, 'cfg', axis=0, tiled=False)  13.4 us
    all_to_all x1, waiting for transfers between devices, body(): lax.all_to_all(sent, 'patch', split_axis=0, concat_axis=0, tiled=True, ax...  10.3 us
    all_gather x1, blocking collectives, body(): lax.all_gather(held[:, 2 * TOK:, :], 'patch', axis=0, tiled=False, axis_i...  10.1 us
    pallas_call x5, Pallas kernels, call(): pl.pallas_call(kernel, grid=(1,), out_shape=out, in_specs=specs or [vmem]...  6.33 us
  transfers between devices with their start and end apart: 1, of which 1 were waited for; matrix products, arithmetic and copies ran while one was open for 1% of the time, Pallas kernels for 2%

profile of v8, /device:TPU:1, one launch (start us, length us, event | category | flops | bytes accessed | tf_op | source)
XLA Modules:
  0.0 70.1 jit_solution(14761088977139603190)
XLA Ops:
  0.0 0.0 copy-start
  0.0 1.9 %shard_map.46 = bf16[32,64,128]{2,1,0:T(8,128)(2,1)} custom-call(bf16[1,2,16,4096]{3,2,1,0:T(8,128)(2,1)} %q_ref.3, bf16[1,2,2,16,4096]{4,3,2,1,0:T(8,128)(2,1)} %kv_ref.3), custom_call_target="tpu_custom_call" | custom-call | bytes 1310720 | tf_op jit(solution)/shard_map/pallas_call | solution.py:211
  1.9 0.0 copy-start.1
  2.0 0.0 copy-start.2
  2.0 13.9 %all-to-all-start = ((bf16[32,64,128]{2,1,0:T(8,128)(2,1)}), bf16[32,64,128]{2,1,0:T(8,128)(2,1)S(1)}, u32[]{:S(2)}, u32[]{:S(2)}) async-start(bf16[32,64,128]{2,1,0:T(8,128)(2,1)} %shard_map.46), calls=%async_computation | async-start | bytes 1048576 | tf_op jit(solution)/shard_map/all_to_all | solution.py:242
  15.8 0.0 copy-done.1
  15.9 0.0 copy-done.2
  15.9 1.1 %shard_map.47 = (f32[512,128]{1,0:T(8,128)S(1)}, f32[512,128]{1,0:T(8,128)S(1)}, f32[512,128]{1,0:T(8,128)S(1)}) custom-call(bf16[1,2,16,4096]{3,2,1,0:T(8,128)(2,1)S(1)} %copy-done.2, bf16[1,2,2,16,4096]{4,3,2,1,0:T(8,128)(2,1)S(1)} %copy-done.1), custom_call_target="tpu_custom_call" | custom-call | bytes 1572864 | tf_op jit(solution)/shard_map/pallas_call | solution.py:211
  17.0 0.0 copy-start.3
  17.0 0.6 copy-done.3
  17.6 0.0 copy-done
  17.6 0.6 gather_fusion
  18.2 0.1 reshape.7
  18.4 0.1 pad_maximum_fusion.gate_ref
  18.4 10.3 %all-to-all-done.x_ref = bf16[32,64,128]{2,1,0:T(8,128)(2,1)S(1)} async-done(((bf16[32,64,128]{2,1,0:T(8,128)(2,1)}), bf16[32,64,128]{2,1,0:T(8,128)(2,1)S(1)}, u32[]{:S(2)}, u32[]{:S(2)}) %all-to-all-start) | async-done | bytes 524320 | tf_op jit(solution)/shard_map/all_to_all | solution.py:242
  28.7 10.1 %all-gather = bf16[64,32,128]{2,1,0:T(8,128)(2,1)S(1)} all-gather(bf16[32,32,128]{2,1,0:T(8,128)(2,1)S(1)} %slice.13), channel_id=2, replica_groups={{0,1},{2,3},{4,5},{6,7},{8,9},{10,11},{12,13},{14,15},{16,17},{18,19},{..., dimensions={0}, use_global_device_ids=true | all-gather | bytes 786432 | tf_op jit(solution)/shard_map/all_gather | solution.py:259
  38.8 1.8 %shard_map.48 = bf16[32,17,2,128]{3,2,1,0:T(2,128)(2,1)S(1)} custom-call(bf16[32,64,128]{2,1,0:T(8,128)(2,1)S(1)} %all-to-all-done.x_ref, bf16[2,32,32,128]{3,2,1,0:T(8,128)(2,1)S(1)} %bitcast.10), custom_call_target="tpu_custom_call" | custom-call | flops 536870912 | bytes 1327104 | tf_op jit(solution)/shard_map/pallas_call | solution.py:211
  40.6 14.5 %all_to_all.10.y_ref = bf16[32,17,2,128]{3,2,1,0:T(2,128)(2,1)S(1)} all-to-all(bf16[32,17,2,128]{3,2,1,0:T(2,128)(2,1)S(1)} %shard_map.48), channel_id=1, replica_groups={{0,2,4,6,8,10,12,14,16,18,20,22,24,26,28,30,32,34,36,38,40,42,44,46,48,..., dimensions={0} | all-to-all | bytes 557056 | tf_op jit(solution)/shard_map/all_to_all | solution.py:274
  55.2 0.5 shard_map.49
  55.7 13.4 %all-gather.1 = bf16[4,512,128]{2,1,0:T(8,128)(2,1)S(1)} all-gather(bf16[2,512,128]{2,1,0:T(8,128)(2,1)S(1)} %shard_map.49), channel_id=3, replica_groups=mesh['clip'=4,'cfg'=2,'patch'=64] {'cfg'}, dimensions={0}, use_global_device_ids=true | all-gather | bytes 786432 | tf_op jit(solution)/shard_map/all_gather | solution.py:278
  69.1 0.9 %shard_map.50 = bf16[2,16,32,64]{3,2,1,0:T(8,128)(2,1)} custom-call(bf16[2,2,512,128]{3,2,1,0:T(8,128)(2,1)S(1)} %bitcast.9, f32[32,128]{1,0:T(8,128)S(1)} %pad_maximum_fusion.gate_ref), custom_call_target="tpu_custom_call" | custom-call | bytes 671744 | tf_op jit(solution)/shard_map/pallas_call | solution.py:211
  (3 shorter events, 0.1 us)
Async XLA Ops:
  0.0 17.6 %copy-start = (f32[50,4096]{1,0:T(8,128)S(1)}, f32[50,4096]{1,0:T(8,128)}, u32[]{:S(2)}) copy-start(f32[50,4096]{1,0:T(8,128)} %param.7) | copy-start | bytes 2457604
  1.9 13.9 %copy-start.1 = (bf16[1,2,2,16,4096]{4,3,2,1,0:T(8,128)(2,1)S(1)}, bf16[1,2,2,16,4096]{4,3,2,1,0:T(8,128)(2,1)}, u32[]{:S(2)}) copy-start(bf16[1,2,2,16,4096]{4,3,2,1,0:T(8,128)(2,1)} %kv_ref.3) | copy-start | bytes 1572868
  2.0 13.9 %copy-start.2 = (bf16[1,2,16,4096]{3,2,1,0:T(8,128)(2,1)S(1)}, bf16[1,2,16,4096]{3,2,1,0:T(8,128)(2,1)}, u32[]{:S(2)}) copy-start(bf16[1,2,16,4096]{3,2,1,0:T(8,128)(2,1)} %q_ref.3) | copy-start | bytes 786436
  2.0 26.7 %all-to-all-start = ((bf16[32,64,128]{2,1,0:T(8,128)(2,1)}), bf16[32,64,128]{2,1,0:T(8,128)(2,1)S(1)}, u32[]{:S(2)}, u32[]{:S(2)}) async-start(bf16[32,64,128]{2,1,0:T(8,128)(2,1)} %shard_map.46), calls=%async_computation | async-start | bytes 1048576 | tf_op jit(solution)/shard_map/all_to_all | solution.py:242
  17.0 0.7 copy-start.3

commit v9 on v8

--- a/solution.py
+++ b/solution.py
@@ -60,12 +60,15 @@
 
     @pl.when(jnp.logical_not(odd))
     def _():
-        for i, load in enumerate(loads):
-            load.start()
-            load.wait()
-            by_head(i)
-            stores[i].start()
-            stores[i].wait()
+        for both in ((0, 1), (2, 3)):
+            for i in both:
+                loads[i].start()
+            for i in both:
+                loads[i].wait()
+                by_head(i)
+                stores[i].start()
+            for i in both:
+                stores[i].wait()
 
 
 def split_value(value):

time: 70.4 us -> 73.3 us (1.041)
  the two profiles are of different devices: /device:TPU:1 before, /device:TPU:17 now
where the time goes in v9:
time: 73.3 us; the launch traced here: 73 us
  blocking collectives  40.1 us (55%)
  starting transfers between devices  13 us (18%)
  waiting for transfers between devices  11.9 us (16%)
  Pallas kernels  6.34 us (9%)
  local copies, waits for them, and re-layouts  1.41 us (2%)
    all_to_all x1, blocking collectives, body(): lax.all_to_all(far, 'patch', split_axis=0, concat_axis=0, tiled=True, axi...  20.1 us
    all_gather x1, blocking collectives, body(): lax.all_gather(held[:, 2 * TOK:, :], 'patch', axis=0, tiled=False, axis_i...  16.1 us
    all_to_all x1, starting transfers between devices, body(): lax.all_to_all(sent, 'patch', split_axis=0, concat_axis=0, tiled=True, ax...  13 us
    all_to_all x1, waiting for transfers between devices, body(): lax.all_to_all(sent, 'patch', split_axis=0, concat_axis=0, tiled=True, ax...  11.9 us
    pallas_call x5, Pallas kernels, call(): pl.pallas_call(kernel, grid=(1,), out_shape=out, in_specs=specs or [vmem]...  6.34 us
    all_gather x1, blocking collectives, body(): both = lax.all_gather(attn, 'cfg', axis=0, tiled=False)  3.89 us
  transfers between devices with their start and end apart: 1, of which 1 were waited for; matrix products, arithmetic and copies ran while one was open for 1% of the time, Pallas kernels for 1%

profile of v9, /device:TPU:17, one launch (start us, length us, event | category | flops | bytes accessed | tf_op | source)
XLA Modules:
  0.0 73.0 jit_solution(2701573583728196660)
XLA Ops:
  0.0 0.0 copy-start
  0.0 1.9 %shard_map.46 = bf16[32,64,128]{2,1,0:T(8,128)(2,1)} custom-call(bf16[1,2,16,4096]{3,2,1,0:T(8,128)(2,1)} %q_ref.3, bf16[1,2,2,16,4096]{4,3,2,1,0:T(8,128)(2,1)} %kv_ref.3), custom_call_target="tpu_custom_call" | custom-call | bytes 1310720 | tf_op jit(solution)/shard_map/pallas_call | solution.py:214
  1.9 0.0 copy-start.1
  2.0 0.0 copy-start.2
  2.0 13.0 %all-to-all-start = ((bf16[32,64,128]{2,1,0:T(8,128)(2,1)}), bf16[32,64,128]{2,1,0:T(8,128)(2,1)S(1)}, u32[]{:S(2)}, u32[]{:S(2)}) async-start(bf16[32,64,128]{2,1,0:T(8,128)(2,1)} %shard_map.46), calls=%async_computation | async-start | bytes 1048576 | tf_op jit(solution)/shard_map/all_to_all | solution.py:245
  15.0 0.0 copy-done.1
  15.0 0.0 copy-done.2
  15.0 1.1 %shard_map.47 = (f32[512,128]{1,0:T(8,128)S(1)}, f32[512,128]{1,0:T(8,128)S(1)}, f32[512,128]{1,0:T(8,128)S(1)}) custom-call(bf16[1,2,16,4096]{3,2,1,0:T(8,128)(2,1)S(1)} %copy-done.2, bf16[1,2,2,16,4096]{4,3,2,1,0:T(8,128)(2,1)S(1)} %copy-done.1), custom_call_target="tpu_custom_call" | custom-call | bytes 1572864 | tf_op jit(solution)/shard_map/pallas_call | solution.py:214
  16.1 0.0 copy-start.3
  16.1 0.6 copy-done.3
  16.8 0.0 copy-done
  16.8 0.6 gather_fusion
  17.4 0.1 reshape.7
  17.5 0.1 pad_maximum_fusion.gate_ref
  17.6 11.9 %all-to-all-done.x_ref = bf16[32,64,128]{2,1,0:T(8,128)(2,1)S(1)} async-done(((bf16[32,64,128]{2,1,0:T(8,128)(2,1)}), bf16[32,64,128]{2,1,0:T(8,128)(2,1)S(1)}, u32[]{:S(2)}, u32[]{:S(2)}) %all-to-all-start) | async-done | bytes 524320 | tf_op jit(solution)/shard_map/all_to_all | solution.py:245
  29.5 16.1 %all-gather = bf16[64,32,128]{2,1,0:T(8,128)(2,1)S(1)} all-gather(bf16[32,32,128]{2,1,0:T(8,128)(2,1)S(1)} %slice.13), channel_id=2, replica_groups={{0,1},{2,3},{4,5},{6,7},{8,9},{10,11},{12,13},{14,15},{16,17},{18,19},{..., dimensions={0}, use_global_device_ids=true | all-gather | bytes 786432 | tf_op jit(solution)/shard_map/all_gather | solution.py:262
  45.7 1.8 %shard_map.48 = bf16[32,17,2,128]{3,2,1,0:T(2,128)(2,1)S(1)} custom-call(bf16[32,64,128]{2,1,0:T(8,128)(2,1)S(1)} %all-to-all-done.x_ref, bf16[2,32,32,128]{3,2,1,0:T(8,128)(2,1)S(1)} %bitcast.10), custom_call_target="tpu_custom_call" | custom-call | flops 536870912 | bytes 1327104 | tf_op jit(solution)/shard_map/pallas_call | solution.py:214
  47.5 20.1 %all_to_all.10.y_ref = bf16[32,17,2,128]{3,2,1,0:T(2,128)(2,1)S(1)} all-to-all(bf16[32,17,2,128]{3,2,1,0:T(2,128)(2,1)S(1)} %shard_map.48), channel_id=1, replica_groups={{0,2,4,6,8,10,12,14,16,18,20,22,24,26,28,30,32,34,36,38,40,42,44,46,48,..., dimensions={0} | all-to-all | bytes 557056 | tf_op jit(solution)/shard_map/all_to_all | solution.py:277
  67.6 0.5 shard_map.49
  68.2 3.9 %all-gather.1 = bf16[4,512,128]{2,1,0:T(8,128)(2,1)S(1)} all-gather(bf16[2,512,128]{2,1,0:T(8,128)(2,1)S(1)} %shard_map.49), channel_id=3, replica_groups=mesh['clip'=4,'cfg'=2,'patch'=64] {'cfg'}, dimensions={0}, use_global_device_ids=true | all-gather | bytes 786432 | tf_op jit(solution)/shard_map/all_gather | solution.py:281
  72.1 0.9 %shard_map.50 = bf16[2,16,32,64]{3,2,1,0:T(8,128)(2,1)} custom-call(bf16[2,2,512,128]{3,2,1,0:T(8,128)(2,1)S(1)} %bitcast.9, f32[32,128]{1,0:T(8,128)S(1)} %pad_maximum_fusion.gate_ref), custom_call_target="tpu_custom_call" | custom-call | bytes 671744 | tf_op jit(solution)/shard_map/pallas_call | solution.py:214
  (3 shorter events, 0.1 us)
Async XLA Ops:
  0.0 16.8 %copy-start = (f32[50,4096]{1,0:T(8,128)S(1)}, f32[50,4096]{1,0:T(8,128)}, u32[]{:S(2)}) copy-start(f32[50,4096]{1,0:T(8,128)} %param.7) | copy-start | bytes 2457604
  1.9 13.1 %copy-start.1 = (bf16[1,2,2,16,4096]{4,3,2,1,0:T(8,128)(2,1)S(1)}, bf16[1,2,2,16,4096]{4,3,2,1,0:T(8,128)(2,1)}, u32[]{:S(2)}) copy-start(bf16[1,2,2,16,4096]{4,3,2,1,0:T(8,128)(2,1)} %kv_ref.3) | copy-start | bytes 1572868
  2.0 13.1 %copy-start.2 = (bf16[1,2,16,4096]{3,2,1,0:T(8,128)(2,1)S(1)}, bf16[1,2,16,4096]{3,2,1,0:T(8,128)(2,1)}, u32[]{:S(2)}) copy-start(bf16[1,2,16,4096]{3,2,1,0:T(8,128)(2,1)} %q_ref.3) | copy-start | bytes 786436
  2.0 27.5 %all-to-all-start = ((bf16[32,64,128]{2,1,0:T(8,128)(2,1)}), bf16[32,64,128]{2,1,0:T(8,128)(2,1)S(1)}, u32[]{:S(2)}, u32[]{:S(2)}) async-start(bf16[32,64,128]{2,1,0:T(8,128)(2,1)} %shard_map.46), calls=%async_computation | async-start | bytes 1048576 | tf_op jit(solution)/shard_map/all_to_all | solution.py:245
  16.1 0.7 copy-start.3

commit v10 on v8

--- a/solution.py
+++ b/solution.py
@@ -12,6 +12,7 @@
 HALF = DEPTH // 2
 TOK = 16
 SIDES = 2
+EVEN_CUTS = ((0, 16, 32), (0, 16, 32), (0, 32), (0, 32))
 NEAR = HEADS * TOK
 ROWS = 2 * NEAR
 PAIRS = TOK // 2
@@ -31,41 +32,45 @@
 
 def pack_kernel(q_ref, kv_ref, out_ref, held, packed, in_sems, out_sems):
     fields = [q_ref.at[0, 0], q_ref.at[0, 1], kv_ref.at[0, 0, 0], kv_ref.at[0, 0, 1]]
-    loads = [
-        pltpu.make_async_copy(field, held.at[i], in_sems.at[i]) for i, field in enumerate(fields)
-    ]
-    stores = [
-        pltpu.make_async_copy(
-            packed.at[i], out_ref.at[:, i * TOK : (i + 1) * TOK, :], out_sems.at[i]
+    def piece(i, first, last):
+        lanes = pl.ds(first * DEPTH, (last - first) * DEPTH)
+        load = pltpu.make_async_copy(
+            fields[i].at[:, lanes], held.at[i, :, lanes], in_sems.at[i]
         )
-        for i in range(len(fields))
-    ]
-
-    def by_head(i):
-        for h in range(HEADS):
+        heads = pl.ds(first, last - first)
+        store = pltpu.make_async_copy(
+            packed.at[i, heads], out_ref.at[heads, pl.ds(i * TOK, TOK), :], out_sems.at[i]
+        )
+        return load, store
+
+    def by_head(i, first, last):
+        for h in range(first, last):
             packed[i, h] = held[i, :, h * DEPTH : (h + 1) * DEPTH]
 
     odd = lax.axis_index("cfg") == 1
 
     @pl.when(odd)
     def _():
-        for load in loads:
+        pieces = [piece(i, 0, HEADS) for i in range(len(fields))]
+        for load, _ in pieces:
             load.start()
-        for i, load in enumerate(loads):
+        for i, (load, store) in enumerate(pieces):
             load.wait()
-            by_head(i)
-            stores[i].start()
-        for store in stores:
+            by_head(i, 0, HEADS)
+            store.start()
+        for _, store in pieces:
             store.wait()
 
     @pl.when(jnp.logical_not(odd))
     def _():
-        for i, load in enumerate(loads):
-            load.start()
-            load.wait()
-            by_head(i)
-            stores[i].start()
-            stores[i].wait()
+        for i, cuts in enumerate(EVEN_CUTS):
+            for first, last in zip(cuts[:-1], cuts[1:]):
+                load, store = piece(i, first, last)
+                load.start()
+                load.wait()
+                by_head(i, first, last)
+                store.start()
+                store.wait()
 
 
 def split_value(value):

time: 70.4 us -> 72.6 us (1.031)
  blocking collectives: 38 us -> 40.3 us
    all_gather x1, blocking collectives: 13.4 us -> 15.8 us  [body(): both = lax.all_gather(attn, 'cfg', axis=0, tiled=False)]
  transfers between devices with their start and end apart: 1 -> 1, of which waited for: 1 -> 1; matrix products, arithmetic and copies ran while one was open for 1% -> 1% of each run, Pallas kernels for 2% -> 1%
where the time goes in v10:
time: 72.6 us; the launch traced here: 72.2 us
  blocking collectives  40.3 us (56%)
  starting transfers between devices  13.9 us (19%)
  waiting for transfers between devices  10.1 us (14%)
  Pallas kernels  6.33 us (9%)
  local copies, waits for them, and re-layouts  1.41 us (2%)
    all_gather x1, blocking collectives, body(): both = lax.all_gather(attn, 'cfg', axis=0, tiled=False)  15.8 us
    all_to_all x1, blocking collectives, body(): lax.all_to_all(far, 'patch', split_axis=0, concat_axis=0, tiled=True, axi...  14.4 us
    all_to_all x1, starting transfers between devices, body(): lax.all_to_all(sent, 'patch', split_axis=0, concat_axis=0, tiled=True, ax...  13.9 us
    all_to_all x1, waiting for transfers between devices, body(): lax.all_to_all(sent, 'patch', split_axis=0, concat_axis=0, tiled=True, ax...  10.1 us
    all_gather x1, blocking collectives, body(): lax.all_gather(held[:, 2 * TOK:, :], 'patch', axis=0, tiled=False, axis_i...  10.1 us
    pallas_call x5, Pallas kernels, call(): pl.pallas_call(kernel, grid=(1,), out_shape=out, in_specs=specs or [vmem]...  6.33 us
  transfers between devices with their start and end apart: 1, of which 1 were waited for; matrix products, arithmetic and copies ran while one was open for 1% of the time, Pallas kernels for 1%

profile of v10, /device:TPU:1, one launch (start us, length us, event | category | flops | bytes accessed | tf_op | source)
XLA Modules:
  0.0 72.2 jit_solution(17337047441353526751)
XLA Ops:
  0.0 0.0 copy-start
  0.0 1.9 %shard_map.46 = bf16[32,64,128]{2,1,0:T(8,128)(2,1)} custom-call(bf16[1,2,16,4096]{3,2,1,0:T(8,128)(2,1)} %q_ref.3, bf16[1,2,2,16,4096]{4,3,2,1,0:T(8,128)(2,1)} %kv_ref.3), custom_call_target="tpu_custom_call" | custom-call | bytes 1310720 | tf_op jit(solution)/shard_map/pallas_call | solution.py:216
  1.9 0.0 copy-start.1
  2.0 0.0 copy-start.2
  2.0 13.9 %all-to-all-start = ((bf16[32,64,128]{2,1,0:T(8,128)(2,1)}), bf16[32,64,128]{2,1,0:T(8,128)(2,1)S(1)}, u32[]{:S(2)}, u32[]{:S(2)}) async-start(bf16[32,64,128]{2,1,0:T(8,128)(2,1)} %shard_map.46), calls=%async_computation | async-start | bytes 1048576 | tf_op jit(solution)/shard_map/all_to_all | solution.py:247
  15.8 0.0 copy-done.1
  15.9 0.0 copy-done.2
  15.9 1.1 %shard_map.47 = (f32[512,128]{1,0:T(8,128)S(1)}, f32[512,128]{1,0:T(8,128)S(1)}, f32[512,128]{1,0:T(8,128)S(1)}) custom-call(bf16[1,2,16,4096]{3,2,1,0:T(8,128)(2,1)S(1)} %copy-done.2, bf16[1,2,2,16,4096]{4,3,2,1,0:T(8,128)(2,1)S(1)} %copy-done.1), custom_call_target="tpu_custom_call" | custom-call | bytes 1572864 | tf_op jit(solution)/shard_map/pallas_call | solution.py:216
  17.0 0.0 copy-start.3
  17.0 0.6 copy-done.3
  17.6 0.0 copy-done
  17.6 0.6 gather_fusion
  18.2 0.1 reshape.7
  18.4 0.1 pad_maximum_fusion.gate_ref
  18.4 10.1 %all-to-all-done.x_ref = bf16[32,64,128]{2,1,0:T(8,128)(2,1)S(1)} async-done(((bf16[32,64,128]{2,1,0:T(8,128)(2,1)}), bf16[32,64,128]{2,1,0:T(8,128)(2,1)S(1)}, u32[]{:S(2)}, u32[]{:S(2)}) %all-to-all-start) | async-done | bytes 524320 | tf_op jit(solution)/shard_map/all_to_all | solution.py:247
  28.5 10.1 %all-gather = bf16[64,32,128]{2,1,0:T(8,128)(2,1)S(1)} all-gather(bf16[32,32,128]{2,1,0:T(8,128)(2,1)S(1)} %slice.13), channel_id=2, replica_groups={{0,1},{2,3},{4,5},{6,7},{8,9},{10,11},{12,13},{14,15},{16,17},{18,19},{..., dimensions={0}, use_global_device_ids=true | all-gather | bytes 786432 | tf_op jit(solution)/shard_map/all_gather | solution.py:264
  38.6 1.8 %shard_map.48 = bf16[32,17,2,128]{3,2,1,0:T(2,128)(2,1)S(1)} custom-call(bf16[32,64,128]{2,1,0:T(8,128)(2,1)S(1)} %all-to-all-done.x_ref, bf16[2,32,32,128]{3,2,1,0:T(8,128)(2,1)S(1)} %bitcast.10), custom_call_target="tpu_custom_call" | custom-call | flops 536870912 | bytes 1327104 | tf_op jit(solution)/shard_map/pallas_call | solution.py:216
  40.5 14.4 %all_to_all.10.y_ref = bf16[32,17,2,128]{3,2,1,0:T(2,128)(2,1)S(1)} all-to-all(bf16[32,17,2,128]{3,2,1,0:T(2,128)(2,1)S(1)} %shard_map.48), channel_id=1, replica_groups={{0,2,4,6,8,10,12,14,16,18,20,22,24,26,28,30,32,34,36,38,40,42,44,46,48,..., dimensions={0} | all-to-all | bytes 557056 | tf_op jit(solution)/shard_map/all_to_all | solution.py:279
  54.9 0.5 shard_map.49
  55.4 15.8 %all-gather.1 = bf16[4,512,128]{2,1,0:T(8,128)(2,1)S(1)} all-gather(bf16[2,512,128]{2,1,0:T(8,128)(2,1)S(1)} %shard_map.49), channel_id=3, replica_groups=mesh['clip'=4,'cfg'=2,'patch'=64] {'cfg'}, dimensions={0}, use_global_device_ids=true | all-gather | bytes 786432 | tf_op jit(solution)/shard_map/all_gather | solution.py:283
  71.3 0.9 %shard_map.50 = bf16[2,16,32,64]{3,2,1,0:T(8,128)(2,1)} custom-call(bf16[2,2,512,128]{3,2,1,0:T(8,128)(2,1)S(1)} %bitcast.9, f32[32,128]{1,0:T(8,128)S(1)} %pad_maximum_fusion.gate_ref), custom_call_target="tpu_custom_call" | custom-call | bytes 671744 | tf_op jit(solution)/shard_map/pallas_call | solution.py:216
  (3 shorter events, 0.1 us)
Async XLA Ops:
  0.0 17.6 %copy-start = (f32[50,4096]{1,0:T(8,128)S(1)}, f32[50,4096]{1,0:T(8,128)}, u32[]{:S(2)}) copy-start(f32[50,4096]{1,0:T(8,128)} %param.7) | copy-start | bytes 2457604
  1.9 13.9 %copy-start.1 = (bf16[1,2,2,16,4096]{4,3,2,1,0:T(8,128)(2,1)S(1)}, bf16[1,2,2,16,4096]{4,3,2,1,0:T(8,128)(2,1)}, u32[]{:S(2)}) copy-start(bf16[1,2,2,16,4096]{4,3,2,1,0:T(8,128)(2,1)} %kv_ref.3) | copy-start | bytes 1572868
  2.0 13.9 %copy-start.2 = (bf16[1,2,16,4096]{3,2,1,0:T(8,128)(2,1)S(1)}, bf16[1,2,16,4096]{3,2,1,0:T(8,128)(2,1)}, u32[]{:S(2)}) copy-start(bf16[1,2,16,4096]{3,2,1,0:T(8,128)(2,1)} %q_ref.3) | copy-start | bytes 786436
  2.0 26.6 %all-to-all-start = ((bf16[32,64,128]{2,1,0:T(8,128)(2,1)}), bf16[32,64,128]{2,1,0:T(8,128)(2,1)S(1)}, u32[]{:S(2)}, u32[]{:S(2)}) async-start(bf16[32,64,128]{2,1,0:T(8,128)(2,1)} %shard_map.46), calls=%async_computation | async-start | bytes 1048576 | tf_op jit(solution)/shard_map/all_to_all | solution.py:247
  17.0 0.7 copy-start.3

commit v11 on v8

--- a/solution.py
+++ b/solution.py
@@ -45,9 +45,9 @@
         for h in range(HEADS):
             packed[i, h] = held[i, :, h * DEPTH : (h + 1) * DEPTH]
 
-    odd = lax.axis_index("cfg") == 1
-
-    @pl.when(odd)
+    first = lax.axis_index("cfg") == 0
+
+    @pl.when(first)
     def _():
         for load in loads:
             load.start()
@@ -58,7 +58,7 @@
         for store in stores:
             store.wait()
 
-    @pl.when(jnp.logical_not(odd))
+    @pl.when(jnp.logical_not(first))
     def _():
         for i, load in enumerate(loads):
             load.start()

time: 70.4 us -> 75.5 us (1.072)
  the two profiles are of different devices: /device:TPU:1 before, /device:TPU:33 now
where the time goes in v11:
time: 75.5 us; the launch traced here: 75.2 us
  blocking collectives  37.1 us (49%)
  starting transfers between devices  13 us (17%)
  waiting for transfers between devices  12.5 us (17%)
  Pallas kernels  10.9 us (14%)
  local copies, waits for them, and re-layouts  1.41 us (2%)
    all_to_all x1, blocking collectives, body(): lax.all_to_all(far, 'patch', split_axis=0, concat_axis=0, tiled=True, axi...  18 us
    all_gather x1, blocking collectives, body(): lax.all_gather(held[:, 2 * TOK:, :], 'patch', axis=0, tiled=False, axis_i...  15.2 us
    all_to_all x1, starting transfers between devices, body(): lax.all_to_all(sent, 'patch', split_axis=0, concat_axis=0, tiled=True, ax...  13 us
    all_to_all x1, waiting for transfers between devices, body(): lax.all_to_all(sent, 'patch', split_axis=0, concat_axis=0, tiled=True, ax...  12.5 us
    pallas_call x5, Pallas kernels, call(): pl.pallas_call(kernel, grid=(1,), out_shape=out, in_specs=specs or [vmem]...  10.9 us
    all_gather x1, blocking collectives, body(): both = lax.all_gather(attn, 'cfg', axis=0, tiled=False)  4 us
  transfers between devices with their start and end apart: 1, of which 1 were waited for; matrix products, arithmetic and copies ran while one was open for 1% of the time, Pallas kernels for 1%

profile of v11, /device:TPU:33, one launch (start us, length us, event | category | flops | bytes accessed | tf_op | source)
XLA Modules:
  0.0 75.2 jit_solution(1891487735294931859)
XLA Ops:
  0.0 0.0 copy-start
  0.0 6.5 %shard_map.46 = bf16[32,64,128]{2,1,0:T(8,128)(2,1)} custom-call(bf16[1,2,16,4096]{3,2,1,0:T(8,128)(2,1)} %q_ref.3, bf16[1,2,2,16,4096]{4,3,2,1,0:T(8,128)(2,1)} %kv_ref.3), custom_call_target="tpu_custom_call" | custom-call | bytes 1310720 | tf_op jit(solution)/shard_map/pallas_call | solution.py:211
  6.5 0.0 copy-start.1
  6.5 0.0 copy-start.2
  6.5 13.0 %all-to-all-start = ((bf16[32,64,128]{2,1,0:T(8,128)(2,1)}), bf16[32,64,128]{2,1,0:T(8,128)(2,1)S(1)}, u32[]{:S(2)}, u32[]{:S(2)}) async-start(bf16[32,64,128]{2,1,0:T(8,128)(2,1)} %shard_map.46), calls=%async_computation | async-start | bytes 1048576 | tf_op jit(solution)/shard_map/all_to_all | solution.py:242
  19.6 0.0 copy-done.1
  19.6 0.0 copy-done.2
  19.6 1.1 %shard_map.47 = (f32[512,128]{1,0:T(8,128)S(1)}, f32[512,128]{1,0:T(8,128)S(1)}, f32[512,128]{1,0:T(8,128)S(1)}) custom-call(bf16[1,2,16,4096]{3,2,1,0:T(8,128)(2,1)S(1)} %copy-done.2, bf16[1,2,2,16,4096]{4,3,2,1,0:T(8,128)(2,1)S(1)} %copy-done.1), custom_call_target="tpu_custom_call" | custom-call | bytes 1572864 | tf_op jit(solution)/shard_map/pallas_call | solution.py:211
  20.7 0.0 copy-start.3
  20.7 0.6 copy-done.3
  21.4 0.0 copy-done
  21.4 0.6 gather_fusion
  21.9 0.1 reshape.7
  22.1 0.1 pad_maximum_fusion.gate_ref
  22.2 12.5 %all-to-all-done.x_ref = bf16[32,64,128]{2,1,0:T(8,128)(2,1)S(1)} async-done(((bf16[32,64,128]{2,1,0:T(8,128)(2,1)}), bf16[32,64,128]{2,1,0:T(8,128)(2,1)S(1)}, u32[]{:S(2)}, u32[]{:S(2)}) %all-to-all-start) | async-done | bytes 524320 | tf_op jit(solution)/shard_map/all_to_all | solution.py:242
  34.7 15.2 %all-gather = bf16[64,32,128]{2,1,0:T(8,128)(2,1)S(1)} all-gather(bf16[32,32,128]{2,1,0:T(8,128)(2,1)S(1)} %slice.13), channel_id=2, replica_groups={{0,1},{2,3},{4,5},{6,7},{8,9},{10,11},{12,13},{14,15},{16,17},{18,19},{..., dimensions={0}, use_global_device_ids=true | all-gather | bytes 786432 | tf_op jit(solution)/shard_map/all_gather | solution.py:259
  49.9 1.8 %shard_map.48 = bf16[32,17,2,128]{3,2,1,0:T(2,128)(2,1)S(1)} custom-call(bf16[32,64,128]{2,1,0:T(8,128)(2,1)S(1)} %all-to-all-done.x_ref, bf16[2,32,32,128]{3,2,1,0:T(8,128)(2,1)S(1)} %bitcast.10), custom_call_target="tpu_custom_call" | custom-call | flops 536870912 | bytes 1327104 | tf_op jit(solution)/shard_map/pallas_call | solution.py:211
  51.8 18.0 %all_to_all.10.y_ref = bf16[32,17,2,128]{3,2,1,0:T(2,128)(2,1)S(1)} all-to-all(bf16[32,17,2,128]{3,2,1,0:T(2,128)(2,1)S(1)} %shard_map.48), channel_id=1, replica_groups={{0,2,4,6,8,10,12,14,16,18,20,22,24,26,28,30,32,34,36,38,40,42,44,46,48,..., dimensions={0} | all-to-all | bytes 557056 | tf_op jit(solution)/shard_map/all_to_all | solution.py:274
  69.7 0.5 shard_map.49
  70.3 4.0 %all-gather.1 = bf16[4,512,128]{2,1,0:T(8,128)(2,1)S(1)} all-gather(bf16[2,512,128]{2,1,0:T(8,128)(2,1)S(1)} %shard_map.49), channel_id=3, replica_groups=mesh['clip'=4,'cfg'=2,'patch'=64] {'cfg'}, dimensions={0}, use_global_device_ids=true | all-gather | bytes 786432 | tf_op jit(solution)/shard_map/all_gather | solution.py:278
  74.3 0.9 %shard_map.50 = bf16[2,16,32,64]{3,2,1,0:T(8,128)(2,1)} custom-call(bf16[2,2,512,128]{3,2,1,0:T(8,128)(2,1)S(1)} %bitcast.9, f32[32,128]{1,0:T(8,128)S(1)} %pad_maximum_fusion.gate_ref), custom_call_target="tpu_custom_call" | custom-call | bytes 671744 | tf_op jit(solution)/shard_map/pallas_call | solution.py:211
  (3 shorter events, 0.1 us)
Async XLA Ops:
  0.0 21.4 %copy-start = (f32[50,4096]{1,0:T(8,128)S(1)}, f32[50,4096]{1,0:T(8,128)}, u32[]{:S(2)}) copy-start(f32[50,4096]{1,0:T(8,128)} %param.7) | copy-start | bytes 2457604
  6.5 13.1 %copy-start.1 = (bf16[1,2,2,16,4096]{4,3,2,1,0:T(8,128)(2,1)S(1)}, bf16[1,2,2,16,4096]{4,3,2,1,0:T(8,128)(2,1)}, u32[]{:S(2)}) copy-start(bf16[1,2,2,16,4096]{4,3,2,1,0:T(8,128)(2,1)} %kv_ref.3) | copy-start | bytes 1572868
  6.5 13.1 %copy-start.2 = (bf16[1,2,16,4096]{3,2,1,0:T(8,128)(2,1)S(1)}, bf16[1,2,16,4096]{3,2,1,0:T(8,128)(2,1)}, u32[]{:S(2)}) copy-start(bf16[1,2,16,4096]{3,2,1,0:T(8,128)(2,1)} %q_ref.3) | copy-start | bytes 786436
  6.5 28.2 %all-to-all-start = ((bf16[32,64,128]{2,1,0:T(8,128)(2,1)}), bf16[32,64,128]{2,1,0:T(8,128)(2,1)S(1)}, u32[]{:S(2)}, u32[]{:S(2)}) async-start(bf16[32,64,128]{2,1,0:T(8,128)(2,1)} %shard_map.46), calls=%async_computation | async-start | bytes 1048576 | tf_op jit(solution)/shard_map/all_to_all | solution.py:242
  20.7 0.7 copy-start.3

commit v12 on v9

--- a/solution.py
+++ b/solution.py
@@ -60,14 +60,14 @@
 
     @pl.when(jnp.logical_not(odd))
     def _():
-        for both in ((0, 1), (2, 3)):
-            for i in both:
+        for group in ((0,), (1,), (2, 3)):
+            for i in group:
                 loads[i].start()
-            for i in both:
+            for i in group:
                 loads[i].wait()
                 by_head(i)
                 stores[i].start()
-            for i in both:
+            for i in group:
                 stores[i].wait()
 
 

time: 73.3 us -> 70.7 us (0.965)
  the two profiles are of different devices: /device:TPU:17 before, /device:TPU:1 now
where the time goes in v12:
time: 70.7 us; the launch traced here: 70 us
  blocking collectives  38.1 us (54%)
  starting transfers between devices  13.9 us (20%)
  waiting for transfers between devices  10.2 us (14%)
  Pallas kernels  6.33 us (9%)
  local copies, waits for them, and re-layouts  1.41 us (2%)
    all_to_all x1, blocking collectives, body(): lax.all_to_all(far, 'patch', split_axis=0, concat_axis=0, tiled=True, axi...  16.4 us
    all_to_all x1, starting transfers between devices, body(): lax.all_to_all(sent, 'patch', split_axis=0, concat_axis=0, tiled=True, ax...  13.9 us
    all_gather x1, blocking collectives, body(): both = lax.all_gather(attn, 'cfg', axis=0, tiled=False)  11.6 us
    all_to_all x1, waiting for transfers between devices, body(): lax.all_to_all(sent, 'patch', split_axis=0, concat_axis=0, tiled=True, ax...  10.2 us
    all_gather x1, blocking collectives, body(): lax.all_gather(held[:, 2 * TOK:, :], 'patch', axis=0, tiled=False, axis_i...  10.1 us
    pallas_call x5, Pallas kernels, call(): pl.pallas_call(kernel, grid=(1,), out_shape=out, in_specs=specs or [vmem]...  6.33 us
  transfers between devices with their start and end apart: 1, of which 1 were waited for; matrix products, arithmetic and copies ran while one was open for 1% of the time, Pallas kernels for 2%

profile of v12, /device:TPU:1, one launch (start us, length us, event | category | flops | bytes accessed | tf_op | source)
XLA Modules:
  0.0 70.0 jit_solution(777803773307211647)
XLA Ops:
  0.0 0.0 copy-start
  0.0 1.9 %shard_map.46 = bf16[32,64,128]{2,1,0:T(8,128)(2,1)} custom-call(bf16[1,2,16,4096]{3,2,1,0:T(8,128)(2,1)} %q_ref.3, bf16[1,2,2,16,4096]{4,3,2,1,0:T(8,128)(2,1)} %kv_ref.3), custom_call_target="tpu_custom_call" | custom-call | bytes 1310720 | tf_op jit(solution)/shard_map/pallas_call | solution.py:214
  1.9 0.0 copy-start.1
  2.0 0.0 copy-start.2
  2.0 13.9 %all-to-all-start = ((bf16[32,64,128]{2,1,0:T(8,128)(2,1)}), bf16[32,64,128]{2,1,0:T(8,128)(2,1)S(1)}, u32[]{:S(2)}, u32[]{:S(2)}) async-start(bf16[32,64,128]{2,1,0:T(8,128)(2,1)} %shard_map.46), calls=%async_computation | async-start | bytes 1048576 | tf_op jit(solution)/shard_map/all_to_all | solution.py:245
  15.8 0.0 copy-done.1
  15.9 0.0 copy-done.2
  15.9 1.1 %shard_map.47 = (f32[512,128]{1,0:T(8,128)S(1)}, f32[512,128]{1,0:T(8,128)S(1)}, f32[512,128]{1,0:T(8,128)S(1)}) custom-call(bf16[1,2,16,4096]{3,2,1,0:T(8,128)(2,1)S(1)} %copy-done.2, bf16[1,2,2,16,4096]{4,3,2,1,0:T(8,128)(2,1)S(1)} %copy-done.1), custom_call_target="tpu_custom_call" | custom-call | bytes 1572864 | tf_op jit(solution)/shard_map/pallas_call | solution.py:214
  17.0 0.0 copy-start.3
  17.0 0.6 copy-done.3
  17.6 0.0 copy-done
  17.6 0.6 gather_fusion
  18.2 0.1 reshape.7
  18.4 0.1 pad_maximum_fusion.gate_ref
  18.4 10.2 %all-to-all-done.x_ref = bf16[32,64,128]{2,1,0:T(8,128)(2,1)S(1)} async-done(((bf16[32,64,128]{2,1,0:T(8,128)(2,1)}), bf16[32,64,128]{2,1,0:T(8,128)(2,1)S(1)}, u32[]{:S(2)}, u32[]{:S(2)}) %all-to-all-start) | async-done | bytes 524320 | tf_op jit(solution)/shard_map/all_to_all | solution.py:245
  28.6 10.1 %all-gather = bf16[64,32,128]{2,1,0:T(8,128)(2,1)S(1)} all-gather(bf16[32,32,128]{2,1,0:T(8,128)(2,1)S(1)} %slice.13), channel_id=2, replica_groups={{0,1},{2,3},{4,5},{6,7},{8,9},{10,11},{12,13},{14,15},{16,17},{18,19},{..., dimensions={0}, use_global_device_ids=true | all-gather | bytes 786432 | tf_op jit(solution)/shard_map/all_gather | solution.py:262
  38.7 1.8 %shard_map.48 = bf16[32,17,2,128]{3,2,1,0:T(2,128)(2,1)S(1)} custom-call(bf16[32,64,128]{2,1,0:T(8,128)(2,1)S(1)} %all-to-all-done.x_ref, bf16[2,32,32,128]{3,2,1,0:T(8,128)(2,1)S(1)} %bitcast.10), custom_call_target="tpu_custom_call" | custom-call | flops 536870912 | bytes 1327104 | tf_op jit(solution)/shard_map/pallas_call | solution.py:214
  40.6 16.4 %all_to_all.10.y_ref = bf16[32,17,2,128]{3,2,1,0:T(2,128)(2,1)S(1)} all-to-all(bf16[32,17,2,128]{3,2,1,0:T(2,128)(2,1)S(1)} %shard_map.48), channel_id=1, replica_groups={{0,2,4,6,8,10,12,14,16,18,20,22,24,26,28,30,32,34,36,38,40,42,44,46,48,..., dimensions={0} | all-to-all | bytes 557056 | tf_op jit(solution)/shard_map/all_to_all | solution.py:277
  57.0 0.5 shard_map.49
  57.5 11.6 %all-gather.1 = bf16[4,512,128]{2,1,0:T(8,128)(2,1)S(1)} all-gather(bf16[2,512,128]{2,1,0:T(8,128)(2,1)S(1)} %shard_map.49), channel_id=3, replica_groups=mesh['clip'=4,'cfg'=2,'patch'=64] {'cfg'}, dimensions={0}, use_global_device_ids=true | all-gather | bytes 786432 | tf_op jit(solution)/shard_map/all_gather | solution.py:281
  69.1 0.9 %shard_map.50 = bf16[2,16,32,64]{3,2,1,0:T(8,128)(2,1)} custom-call(bf16[2,2,512,128]{3,2,1,0:T(8,128)(2,1)S(1)} %bitcast.9, f32[32,128]{1,0:T(8,128)S(1)} %pad_maximum_fusion.gate_ref), custom_call_target="tpu_custom_call" | custom-call | bytes 671744 | tf_op jit(solution)/shard_map/pallas_call | solution.py:214
  (3 shorter events, 0.1 us)
Async XLA Ops:
  0.0 17.6 %copy-start = (f32[50,4096]{1,0:T(8,128)S(1)}, f32[50,4096]{1,0:T(8,128)}, u32[]{:S(2)}) copy-start(f32[50,4096]{1,0:T(8,128)} %param.7) | copy-start | bytes 2457604
  1.9 13.9 %copy-start.1 = (bf16[1,2,2,16,4096]{4,3,2,1,0:T(8,128)(2,1)S(1)}, bf16[1,2,2,16,4096]{4,3,2,1,0:T(8,128)(2,1)}, u32[]{:S(2)}) copy-start(bf16[1,2,2,16,4096]{4,3,2,1,0:T(8,128)(2,1)} %kv_ref.3) | copy-start | bytes 1572868
  2.0 13.9 %copy-start.2 = (bf16[1,2,16,4096]{3,2,1,0:T(8,128)(2,1)S(1)}, bf16[1,2,16,4096]{3,2,1,0:T(8,128)(2,1)}, u32[]{:S(2)}) copy-start(bf16[1,2,16,4096]{3,2,1,0:T(8,128)(2,1)} %q_ref.3) | copy-start | bytes 786436
  2.0 26.6 %all-to-all-start = ((bf16[32,64,128]{2,1,0:T(8,128)(2,1)}), bf16[32,64,128]{2,1,0:T(8,128)(2,1)S(1)}, u32[]{:S(2)}, u32[]{:S(2)}) async-start(bf16[32,64,128]{2,1,0:T(8,128)(2,1)} %shard_map.46), calls=%async_computation | async-start | bytes 1048576 | tf_op jit(solution)/shard_map/all_to_all | solution.py:245
  17.0 0.7 copy-start.3

commit v13 on v11

--- a/solution.py
+++ b/solution.py
@@ -12,6 +12,7 @@
 HALF = DEPTH // 2
 TOK = 16
 SIDES = 2
+Y_FIRST = 1
 NEAR = HEADS * TOK
 ROWS = 2 * NEAR
 PAIRS = TOK // 2
@@ -29,43 +30,32 @@
     return lax.dot_general(a, b, (((1,), (1,)), ((), ())), preferred_element_type=F32)
 
 
-def pack_kernel(q_ref, kv_ref, out_ref, held, packed, in_sems, out_sems):
-    fields = [q_ref.at[0, 0], q_ref.at[0, 1], kv_ref.at[0, 0, 0], kv_ref.at[0, 0, 1]]
+def pack_kernel(fields, out_ref, held, packed, in_sems, out_sems):
     loads = [
         pltpu.make_async_copy(field, held.at[i], in_sems.at[i]) for i, field in enumerate(fields)
     ]
-    stores = [
-        pltpu.make_async_copy(
-            packed.at[i], out_ref.at[:, i * TOK : (i + 1) * TOK, :], out_sems.at[i]
-        )
-        for i in range(len(fields))
-    ]
-
-    def by_head(i):
+    for load in loads:
+        load.start()
+    stores = []
+    for i, load in enumerate(loads):
+        load.wait()
         for h in range(HEADS):
             packed[i, h] = held[i, :, h * DEPTH : (h + 1) * DEPTH]
-
-    first = lax.axis_index("cfg") == 0
-
-    @pl.when(first)
-    def _():
-        for load in loads:
-            load.start()
-        for i, load in enumerate(loads):
-            load.wait()
-            by_head(i)
-            stores[i].start()
-        for store in stores:
-            store.wait()
-
-    @pl.when(jnp.logical_not(first))
-    def _():
-        for i, load in enumerate(loads):
-            load.start()
-            load.wait()
-            by_head(i)
-            stores[i].start()
-            stores[i].wait()
+        rows = out_ref.at[:, i * TOK : (i + 1) * TOK, :]
+        stores.append(pltpu.make_async_copy(packed.at[i], rows, out_sems.at[i]))
+        stores[-1].start()
+    for store in stores:
+        store.wait()
+
+
+def pack_own_kernel(q_ref, kv_ref, *refs):
+    pack_kernel([q_ref.at[0, i] for i in range(2)] + [kv_ref.at[0, 0, i] for i in range(2)], *refs)
+
+
+def pack_both_kernel(q_ref, stale_ref, *refs):
+    fields = [q_ref.at[0, i] for i in range(2)]
+    fields += [stale_ref.at[side, i] for side in range(SIDES) for i in range(2)]
+    pack_kernel(fields, *refs)
 
 
 def split_value(value):
@@ -139,7 +129,16 @@
         total_ref[here] = jnp.broadcast_to(total, (n, DEPTH))
 
 
-def attend_kernel(x_ref, kv_ref, out_ref, score, weight, top, total):
+def attend_own_kernel(x_ref, kv_ref, *refs):
+    attend(x_ref, [kv_ref.at[half] for half in range(SIDES)], *refs)
+
+
+def attend_both_kernel(x_ref, *refs):
+    pair = 2 * TOK
+    attend(x_ref, [x_ref.at[:, pair * (1 + half) : pair * (2 + half), :] for half in range(SIDES)], *refs)
+
+
+def attend(x_ref, pairs, out_ref, score, weight, top, total):
     side = lax.axis_index("patch") % SIDES
     row = lax.broadcasted_iota(jnp.int32, (BLOCK, BLOCK), 0)
     col = lax.broadcasted_iota(jnp.int32, (BLOCK, BLOCK), 1)
@@ -149,7 +148,7 @@
     for step in range(2):
         query = x_ref[:, step * TOK : (step + 1) * TOK, :].reshape(NEAR, DEPTH)
         for half in range(SIDES):
-            keys = kv_ref[half, :, 0:TOK, :].reshape(NEAR, DEPTH)
+            keys = pairs[half][:, 0:TOK, :].reshape(NEAR, DEPTH)
             score[steps[step], half * NEAR : (half + 1) * NEAR] = dot_t(query, keys)
     for step in range(2):
         for i in range(NEAR // BLOCK):
@@ -166,7 +165,7 @@
             top[here] = jnp.broadcast_to(most, (BLOCK, DEPTH))
             total[here] = jnp.broadcast_to(added, (BLOCK, DEPTH))
             weight[here] = weights.astype(BF16)
-    values = kv_ref[:, :, TOK:, :].reshape(TOKENS, DEPTH)
+    values = jnp.concatenate([pair[:, TOK:, :].reshape(NEAR, DEPTH) for pair in pairs], 0)
     for step in range(2):
         rows = steps[step]
         attn = jnp.dot(weight[rows], values, preferred_element_type=F32) / total[rows]
@@ -223,57 +222,73 @@
 def body(queries, keys_values, timesteps, gate_table):
     width = HEADS * DEPTH
     sides = [[SIDES * i + side for i in range(HEADS)] for side in range(SIDES)]
-    patches = SIDES * HEADS
+    pairs = [[SIDES * i, SIDES * i + 1] for i in range(HEADS)]
     whole = pl.BlockSpec(memory_space=pltpu.HBM)
-    sent = call(
-        pack_kernel,
-        SHAPE((HEADS, 4 * TOK, DEPTH), BF16),
-        (queries, keys_values),
-        [whole, whole],
-        [
-            pltpu.VMEM((4, TOK, width), BF16),
-            pltpu.VMEM((4, HEADS, TOK, DEPTH), BF16),
-            pltpu.SemaphoreType.DMA((4,)),
-            pltpu.SemaphoreType.DMA((4,)),
-        ],
-        out_space=pltpu.HBM,
-        limit=60,
-    )
-    held = lax.all_to_all(
-        sent, "patch", split_axis=0, concat_axis=0, tiled=True, axis_index_groups=sides
-    )
-    near = call(
-        local_kernel,
-        [SHAPE((NEAR, DEPTH), F32)] * 3,
-        (queries, keys_values),
-        [
-            pl.BlockSpec((None, 1, TOK, width), lambda i: (0, 1, 0, 0)),
-            pl.BlockSpec((None, None, 2, TOK, width), lambda i: (0, 1, 0, 0, 0)),
-        ],
-    )
-    gates = jnp.take(gate_table, timesteps, axis=0, mode="clip").reshape(2, HEADS, 2, HALF)
-    gate = lax.dynamic_index_in_dim(gates, lax.axis_index("cfg"), 2, keepdims=False)
-    gate = jnp.concatenate([gate[0], gate[1]], axis=1)
-    held, near, gate = lax.optimization_barrier((held, near, gate))
-    pairs = [[SIDES * i, SIDES * i + 1] for i in range(HEADS)]
-    stale = lax.all_gather(
-        held[:, 2 * TOK :, :], "patch", axis=0, tiled=False, axis_index_groups=pairs
-    )
-    far = call(
-        attend_kernel,
-        SHAPE((HEADS, 2 * PAIRS + 1, 2, DEPTH), BF16),
-        (held, stale),
-        scratch=[
-            pltpu.VMEM((ROWS, TOKENS), F32),
-            pltpu.VMEM((ROWS, TOKENS), BF16),
-            pltpu.VMEM((ROWS, DEPTH), F32),
-            pltpu.VMEM((ROWS, DEPTH), F32),
-        ],
-        flops=4 * ROWS * TOKENS * DEPTH,
-    )
-    back = lax.all_to_all(
-        far, "patch", split_axis=0, concat_axis=0, tiled=True, axis_index_groups=sides
-    )
+
+    def pack(kernel, stale, fields):
+        return call(
+            kernel,
+            SHAPE((HEADS, fields * TOK, DEPTH), BF16),
+            (queries, stale),
+            [whole, whole],
+            [
+                pltpu.VMEM((fields, TOK, width), BF16),
+                pltpu.VMEM((fields, HEADS, TOK, DEPTH), BF16),
+                pltpu.SemaphoreType.DMA((fields,)),
+                pltpu.SemaphoreType.DMA((fields,)),
+            ],
+            out_space=pltpu.HBM,
+            limit=60,
+        )
+
+    def to_heads(sent):
+        return lax.all_to_all(
+            sent, "patch", split_axis=0, concat_axis=0, tiled=True, axis_index_groups=sides
+        )
+
+    def over_y(field):
+        return lax.all_gather(field, "patch", axis=0, tiled=False, axis_index_groups=pairs)
+
+    def beside():
+        near = call(
+            local_kernel,
+            [SHAPE((NEAR, DEPTH), F32)] * 3,
+            (queries, keys_values),
+            [
+                pl.BlockSpec((None, 1, TOK, width), lambda i: (0, 1, 0, 0)),
+                pl.BlockSpec((None, None, 2, TOK, width), lambda i: (0, 1, 0, 0, 0)),
+            ],
+        )
+        gates = jnp.take(gate_table, timesteps, axis=0, mode="clip").reshape(2, HEADS, 2, HALF)
+        gate = lax.dynamic_index_in_dim(gates, lax.axis_index("cfg"), 2, keepdims=False)
+        return near, jnp.concatenate([gate[0], gate[1]], axis=1)
+
+    def attended(kernel, args):
+        return call(
+            kernel,
+            SHAPE((HEADS, 2 * PAIRS + 1, 2, DEPTH), BF16),
+            args,
+            scratch=[
+                pltpu.VMEM((ROWS, TOKENS), F32),
+                pltpu.VMEM((ROWS, TOKENS), BF16),
+                pltpu.VMEM((ROWS, DEPTH), F32),
+                pltpu.VMEM((ROWS, DEPTH), F32),
+            ],
+            flops=4 * ROWS * TOKENS * DEPTH,
+        )
+
+    def heads_first():
+        held = to_heads(pack(pack_own_kernel, keys_values, 4))
+        held, rest = lax.optimization_barrier((held, beside()))
+        return attended(attend_own_kernel, (held, over_y(held[:, 2 * TOK :, :]))), rest
+
+    def y_first():
+        held = to_heads(pack(pack_both_kernel, over_y(keys_values[0, 0]), 6))
+        held, rest = lax.optimization_barrier((held, beside()))
+        return attended(attend_both_kernel, (held,)), rest
+
+    far, (near, gate) = lax.cond(lax.axis_index("cfg") == Y_FIRST, y_first, heads_first)
+    back = to_heads(far)
     attn = call(merge_kernel, SHAPE((2, NEAR, DEPTH), BF16), (back, *near))
     both = lax.all_gather(attn, "cfg", axis=0, tiled=False)
     return call(

time: 75.5 us -> 68.3 us (0.905)
  the two profiles are of different devices: /device:TPU:33 before, /device:TPU:41 now
where the time goes in v13:
time: 68.3 us; the launch traced here: 67.9 us
  blocking collectives  32.5 us (48%)
  starting transfers between devices  13.2 us (19%)
  waiting for transfers between devices  11.8 us (17%)
  Pallas kernels  6.7 us (10%)
  local copies, waits for them, and re-layouts  3.55 us (5%)
    all_to_all x1, blocking collectives, to_heads(): lax.all_to_all(sent, 'patch', split_axis=0, concat_axis=0, tiled=True, ax...  17.5 us
    all_to_all x1, starting transfers between devices, to_heads(): lax.all_to_all(sent, 'patch', split_axis=0, concat_axis=0, tiled=True, ax...  13.2 us
    all_gather x1, blocking collectives, over_y(): lax.all_gather(field, 'patch', axis=0, tiled=False, axis_index_groups=pairs)  12.9 us
    all_to_all x1, waiting for transfers between devices, to_heads(): lax.all_to_all(sent, 'patch', split_axis=0, concat_axis=0, tiled=True, ax...  11.8 us
    pallas_call x5, Pallas kernels, call(): pl.pallas_call(kernel, grid=(1,), out_shape=out, in_specs=specs or [vmem]...  6.7 us
    all_gather x1, blocking collectives, body(): both = lax.all_gather(attn, 'cfg', axis=0, tiled=False)  2.18 us
    gather x1, local copies, waits for them, and re-layouts, beside(): jnp.take(gate_table, timesteps, axis=0, mode='clip')  1.77 us
  transfers between devices with their start and end apart: 1, of which 1 were waited for; matrix products, arithmetic and copies ran while one was open for 3% of the time, Pallas kernels for 2%

profile of v13, /device:TPU:41, one launch (start us, length us, event | category | flops | bytes accessed | tf_op | source)
XLA Modules:
  0.0 67.9 jit_solution(13765760446297735074)
XLA Ops:
  0.0 0.0 copy-start.4
  0.0 0.7 copy-done.4
  0.7 46.1 %conditional.1 = (bf16[32,17,2,128]{3,2,1,0:T(2,128)(2,1)S(1)}, f32[512,128]{1,0:T(8,128)S(1)}, f32[512,128]{1,0:T(8,128)S(1)}, f32[512,128]{1,0:T(8,128)S(1)}, f32[32,128]{1,0:T(8,128)S(1)}) conditional(s32[]{:T(128)} %convert_element_type.3, (bf16[1,2,16,4096]{3,2,1,0:T(8,128)(2,1)}, bf16[1,2,2,16,4096]{4,3,2,1,0:T(8,128)(2,1)}, s32[2]{0:T(128)S(1)}, ...), branch_computations={%region_0.1_spmd, %region_1.2_spmd} | conditional | flops 536876032 | bytes 11227366 | solution.py:290
  0.7 1.0 %slice.19 = bf16[1,1,2,16,4096]{4,3,2,1,0:T(8,128)(2,1)S(1)} slice(bf16[1,2,2,16,4096]{4,3,2,1,0:T(8,128)(2,1)} %get-tuple-element.34.kv_ref), slice={[0:1], [0:1], [0:2], [0:16], [0:4096]} | slice | bytes 524288 | tf_op jit(solution)/shard_map/cond/branch_1_fun/slice | solution.py:286
  1.6 0.0 copy-start.3
  1.6 12.9 %all-gather.1 = bf16[2,1,2,16,4096]{4,3,2,1,0:T(8,128)(2,1)} all-gather(bf16[1,1,2,16,4096]{4,3,2,1,0:T(8,128)(2,1)S(1)} %slice.19), channel_id=3, replica_groups={{0,1},{2,3},{4,5},{6,7},{8,9},{10,11},{12,13},{14,15},{16,17},{18,19},{..., dimensions={0}, use_global_device_ids=true | all-gather | bytes 786432 | tf_op jit(solution)/shard_map/cond/branch_1_fun/all_gather | solution.py:250
  14.5 0.0 copy-done.3
  14.5 2.3 %branch_1_fun.3 = bf16[32,96,128]{2,1,0:T(8,128)(2,1)} custom-call(bf16[1,2,16,4096]{3,2,1,0:T(8,128)(2,1)S(1)} %copy-done.3, bf16[2,2,16,4096]{3,2,1,0:T(8,128)(2,1)} %bitcast.19), custom_call_target="tpu_custom_call" | custom-call | bytes 1572864 | tf_op jit(solution)/shard_map/cond/branch_1_fun/pallas_call | solution.py:210
  16.8 0.0 copy-start.1
  16.8 13.2 %all-to-all-start.1 = ((bf16[32,96,128]{2,1,0:T(8,128)(2,1)}), bf16[32,96,128]{2,1,0:T(8,128)(2,1)S(1)}, u32[]{:S(2)}, u32[]{:S(2)}) async-start(bf16[32,96,128]{2,1,0:T(8,128)(2,1)} %branch_1_fun.3), calls=%async_computation.1 | async-start | bytes 1572864 | tf_op jit(solution)/shard_map/cond/branch_1_fun/all_to_all | solution.py:245
  30.0 0.0 copy-done.1
  30.1 1.1 %branch_1_fun.4 = (f32[512,128]{1,0:T(8,128)S(1)}, f32[512,128]{1,0:T(8,128)S(1)}, f32[512,128]{1,0:T(8,128)S(1)}) custom-call(bf16[1,2,16,4096]{3,2,1,0:T(8,128)(2,1)S(1)} %copy-done.3, bf16[1,2,2,16,4096]{4,3,2,1,0:T(8,128)(2,1)S(1)} %copy-done.1), custom_call_target="tpu_custom_call" | custom-call | bytes 1572864 | tf_op jit(solution)/shard_map/cond/branch_1_fun/pallas_call | solution.py:210
  31.2 1.8 %gather_fusion.1 = f32[2,4096]{1,0:T(2,128)S(1)} fusion(f32[50,4096]{1,0:T(8,128)} %get-tuple-element.38, s32[1024]{0:T(1024)S(1)} %pad_clamp_fusion.1), kind=kCustom, calls=%fused_computation.1 | custom fusion | bytes 65544 | tf_op jit(solution)/shard_map/cond/branch_1_fun/jit(_take)/gather | solution.py:262
  32.9 0.1 reshape.13
  33.1 0.1 pad_maximum_fusion.1
  33.2 11.8 %all-to-all-done.1.x_ref = bf16[32,96,128]{2,1,0:T(8,128)(2,1)S(1)} async-done(((bf16[32,96,128]{2,1,0:T(8,128)(2,1)}), bf16[32,96,128]{2,1,0:T(8,128)(2,1)S(1)}, u32[]{:S(2)}, u32[]{:S(2)}) %all-to-all-start.1) | async-done | bytes 786464 | tf_op jit(solution)/shard_map/cond/branch_1_fun/all_to_all | solution.py:245
  44.9 1.8 %branch_1_fun.5 = bf16[32,17,2,128]{3,2,1,0:T(2,128)(2,1)S(1)} custom-call(bf16[32,96,128]{2,1,0:T(8,128)(2,1)S(1)} %all-to-all-done.1.x_ref), custom_call_target="tpu_custom_call" | custom-call | flops 536870912 | bytes 1064960 | tf_op jit(solution)/shard_map/cond/branch_1_fun/pallas_call | solution.py:210
  46.8 17.5 %all_to_all.13.y_ref = bf16[32,17,2,128]{3,2,1,0:T(2,128)(2,1)S(1)} all-to-all(bf16[32,17,2,128]{3,2,1,0:T(2,128)(2,1)S(1)} %get-tuple-element.50), channel_id=1, replica_groups={{0,2,4,6,8,10,12,14,16,18,20,22,24,26,28,30,32,34,36,38,40,42,44,46,48,..., dimensions={0} | all-to-all | bytes 557056 | tf_op jit(solution)/shard_map/all_to_all | solution.py:245
  64.3 0.5 shard_map.46
  64.8 2.2 %all-gather.2 = bf16[4,512,128]{2,1,0:T(8,128)(2,1)S(1)} all-gather(bf16[2,512,128]{2,1,0:T(8,128)(2,1)S(1)} %shard_map.46), channel_id=4, replica_groups=mesh['clip'=4,'cfg'=2,'patch'=64] {'cfg'}, dimensions={0}, use_global_device_ids=true | all-gather | bytes 786432 | tf_op jit(solution)/shard_map/all_gather | solution.py:293
  67.0 0.9 %shard_map.47 = bf16[2,16,32,64]{3,2,1,0:T(8,128)(2,1)} custom-call(bf16[2,2,512,128]{3,2,1,0:T(8,128)(2,1)S(1)} %bitcast.17, f32[32,128]{1,0:T(8,128)S(1)} %get-tuple-element.54.gate_ref), custom_call_target="tpu_custom_call" | custom-call | bytes 671744 | tf_op jit(solution)/shard_map/pallas_call | solution.py:210
  (2 shorter events, 0.0 us)
Async XLA Ops:
  0.0 0.7 copy-start.4
  1.6 12.9 %copy-start.3 = (bf16[1,2,16,4096]{3,2,1,0:T(8,128)(2,1)S(1)}, bf16[1,2,16,4096]{3,2,1,0:T(8,128)(2,1)}, u32[]{:S(2)}) copy-start(bf16[1,2,16,4096]{3,2,1,0:T(8,128)(2,1)} %get-tuple-element.33.q_ref) | copy-start | bytes 786436 | tf_op jit(solution)/shard_map/cond
  16.8 13.2 %copy-start.1 = (bf16[1,2,2,16,4096]{4,3,2,1,0:T(8,128)(2,1)S(1)}, bf16[1,2,2,16,4096]{4,3,2,1,0:T(8,128)(2,1)}, u32[]{:S(2)}) copy-start(bf16[1,2,2,16,4096]{4,3,2,1,0:T(8,128)(2,1)} %get-tuple-element.34.kv_ref) | copy-start | bytes 1572868 | tf_op jit(solution)/shard_map/cond
  16.8 28.1 %all-to-all-start.1 = ((bf16[32,96,128]{2,1,0:T(8,128)(2,1)}), bf16[32,96,128]{2,1,0:T(8,128)(2,1)S(1)}, u32[]{:S(2)}, u32[]{:S(2)}) async-start(bf16[32,96,128]{2,1,0:T(8,128)(2,1)} %branch_1_fun.3), calls=%async_computation.1 | async-start | bytes 1572864 | tf_op jit(solution)/shard_map/cond/branch_1_fun/all_to_all | solution.py:245

commit v14 on v13

--- a/solution.py
+++ b/solution.py
@@ -30,7 +30,7 @@
     return lax.dot_general(a, b, (((1,), (1,)), ((), ())), preferred_element_type=F32)
 
 
-def pack_kernel(fields, out_ref, held, packed, in_sems, out_sems):
+def pack_kernel(fields, out_ref, held, in_sems, packed, out_sems):
     loads = [
         pltpu.make_async_copy(field, held.at[i], in_sems.at[i]) for i, field in enumerate(fields)
     ]
@@ -49,13 +49,22 @@
 
 
 def pack_own_kernel(q_ref, kv_ref, *refs):
-    pack_kernel([q_ref.at[0, i] for i in range(2)] + [kv_ref.at[0, 0, i] for i in range(2)], *refs)
-
-
-def pack_both_kernel(q_ref, stale_ref, *refs):
-    fields = [q_ref.at[0, i] for i in range(2)]
+    fields = [q_ref.at[0, i] for i in range(2)] + [kv_ref.at[0, 0, i] for i in range(2)]
+    pack_kernel(fields, *refs)
+
+
+def pack_both_kernel(q_ref, stale_ref, out_ref, packed, sems):
+    fields = [q_ref.at[i] for i in range(2)]
     fields += [stale_ref.at[side, i] for side in range(SIDES) for i in range(2)]
-    pack_kernel(fields, *refs)
+    stores = []
+    for i, field in enumerate(fields):
+        for h in range(HEADS):
+            packed[i, h] = field[:, h * DEPTH : (h + 1) * DEPTH]
+        rows = out_ref.at[:, i * TOK : (i + 1) * TOK, :]
+        stores.append(pltpu.make_async_copy(packed.at[i], rows, sems.at[i]))
+        stores[-1].start()
+    for store in stores:
+        store.wait()
 
 
 def split_value(value):
@@ -135,7 +144,8 @@
 
 def attend_both_kernel(x_ref, *refs):
     pair = 2 * TOK
-    attend(x_ref, [x_ref.at[:, pair * (1 + half) : pair * (2 + half), :] for half in range(SIDES)], *refs)
+    pairs = [x_ref.at[:, pair * (1 + half) : pair * (2 + half), :] for half in range(SIDES)]
+    attend(x_ref, pairs, *refs)
 
 
 def attend(x_ref, pairs, out_ref, score, weight, top, total):
@@ -225,21 +235,31 @@
     pairs = [[SIDES * i, SIDES * i + 1] for i in range(HEADS)]
     whole = pl.BlockSpec(memory_space=pltpu.HBM)
 
-    def pack(kernel, stale, fields):
+    def packed(kernel, stale, specs, fields, scratch, limit):
         return call(
             kernel,
             SHAPE((HEADS, fields * TOK, DEPTH), BF16),
             (queries, stale),
-            [whole, whole],
-            [
-                pltpu.VMEM((fields, TOK, width), BF16),
+            specs,
+            scratch
+            + [
                 pltpu.VMEM((fields, HEADS, TOK, DEPTH), BF16),
-                pltpu.SemaphoreType.DMA((fields,)),
                 pltpu.SemaphoreType.DMA((fields,)),
             ],
             out_space=pltpu.HBM,
-            limit=60,
-        )
+            limit=limit,
+        )
+
+    def pack_own():
+        loads = [pltpu.VMEM((4, TOK, width), BF16), pltpu.SemaphoreType.DMA((4,))]
+        return packed(pack_own_kernel, keys_values, [whole, whole], 4, loads, 60)
+
+    def pack_both(stale):
+        specs = [
+            pl.BlockSpec((None, 2, TOK, width), lambda i: (0, 0, 0, 0)),
+            pl.BlockSpec(memory_space=pltpu.VMEM),
+        ]
+        return packed(pack_both_kernel, stale, specs, 6, [], 32)
 
     def to_heads(sent):
         return lax.all_to_all(
@@ -278,12 +298,12 @@
         )
 
     def heads_first():
-        held = to_heads(pack(pack_own_kernel, keys_values, 4))
+        held = to_heads(pack_own())
         held, rest = lax.optimization_barrier((held, beside()))
         return attended(attend_own_kernel, (held, over_y(held[:, 2 * TOK :, :]))), rest
 
     def y_first():
-        held = to_heads(pack(pack_both_kernel, over_y(keys_values[0, 0]), 6))
+        held = to_heads(pack_both(over_y(keys_values[0, 0])))
         held, rest = lax.optimization_barrier((held, beside()))
         return attended(attend_both_kernel, (held,)), rest
 

time: 68.3 us -> 67.9 us (level)
  Pallas kernels: 6.7 us -> 5.38 us
  blocking collectives: 32.5 us -> 33.4 us
    all_gather x1, blocking collectives: 2.18 us -> 3.71 us  [body(): both = lax.all_gather(attn, 'cfg', axis=0, tiled=False)]
    pallas_call x5, Pallas kernels: 6.7 us -> 5.38 us  [call(): pl.pallas_call(kernel, grid=(1,), out_shape=out, in_specs=specs or [vmem]...]
where the time goes in v14:
time: 67.9 us; the launch traced here: 67.5 us
  blocking collectives  33.4 us (49%)
  starting transfers between devices  13.3 us (20%)
  waiting for transfers between devices  11.8 us (17%)
  Pallas kernels  5.38 us (8%)
  local copies, waits for them, and re-layouts  3.55 us (5%)
    all_to_all x1, blocking collectives, to_heads(): lax.all_to_all(sent, 'patch', split_axis=0, concat_axis=0, tiled=True, ax...  16.9 us
    all_to_all x1, starting transfers between devices, to_heads(): lax.all_to_all(sent, 'patch', split_axis=0, concat_axis=0, tiled=True, ax...  13.3 us
    all_gather x1, blocking collectives, over_y(): lax.all_gather(field, 'patch', axis=0, tiled=False, axis_index_groups=pairs)  12.7 us
    all_to_all x1, waiting for transfers between devices, to_heads(): lax.all_to_all(sent, 'patch', split_axis=0, concat_axis=0, tiled=True, ax...  11.8 us
    pallas_call x5, Pallas kernels, call(): pl.pallas_call(kernel, grid=(1,), out_shape=out, in_specs=specs or [vmem]...  5.38 us
    all_gather x1, blocking collectives, body(): both = lax.all_gather(attn, 'cfg', axis=0, tiled=False)  3.71 us
    gather x1, local copies, waits for them, and re-layouts, beside(): jnp.take(gate_table, timesteps, axis=0, mode='clip')  1.77 us
  transfers between devices with their start and end apart: 1, of which 1 were waited for; matrix products, arithmetic and copies ran while one was open for 3% of the time, Pallas kernels for 2%

profile of v14, /device:TPU:41, one launch (start us, length us, event | category | flops | bytes accessed | tf_op | source)
XLA Modules:
  0.0 67.5 jit_solution(6281554359030076099)
XLA Ops:
  0.0 0.0 copy-start.4
  0.0 0.7 copy-done.4
  0.7 44.8 %conditional.1 = (bf16[32,17,2,128]{3,2,1,0:T(2,128)(2,1)S(1)}, f32[512,128]{1,0:T(8,128)S(1)}, f32[512,128]{1,0:T(8,128)S(1)}, f32[512,128]{1,0:T(8,128)S(1)}, f32[32,128]{1,0:T(8,128)S(1)}) conditional(s32[]{:T(128)} %convert_element_type.3, (bf16[1,2,16,4096]{3,2,1,0:T(8,128)(2,1)}, bf16[1,2,2,16,4096]{4,3,2,1,0:T(8,128)(2,1)}, s32[2]{0:T(128)S(1)}, ...), branch_computations={%region_0.1_spmd, %region_1.2_spmd} | conditional | flops 536876032 | bytes 11227366 | solution.py:310
  0.7 1.0 %slice.19 = bf16[1,1,2,16,4096]{4,3,2,1,0:T(8,128)(2,1)S(1)} slice(bf16[1,2,2,16,4096]{4,3,2,1,0:T(8,128)(2,1)} %get-tuple-element.34.kv_ref), slice={[0:1], [0:1], [0:2], [0:16], [0:4096]} | slice | bytes 524288 | tf_op jit(solution)/shard_map/cond/branch_1_fun/slice | solution.py:306
  1.6 0.0 copy-start.3
  1.6 12.7 %all-gather.1 = bf16[2,1,2,16,4096]{4,3,2,1,0:T(8,128)(2,1)S(1)} all-gather(bf16[1,1,2,16,4096]{4,3,2,1,0:T(8,128)(2,1)S(1)} %slice.19), channel_id=3, replica_groups={{0,1},{2,3},{4,5},{6,7},{8,9},{10,11},{12,13},{14,15},{16,17},{18,19},{..., dimensions={0}, use_global_device_ids=true | all-gather | bytes 786432 | tf_op jit(solution)/shard_map/cond/branch_1_fun/all_gather | solution.py:270
  14.4 0.0 copy-done.3
  14.4 1.0 %branch_1_fun.3 = bf16[32,96,128]{2,1,0:T(8,128)(2,1)} custom-call(bf16[1,2,16,4096]{3,2,1,0:T(8,128)(2,1)S(1)} %copy-done.3, bf16[2,2,16,4096]{3,2,1,0:T(8,128)(2,1)S(1)} %bitcast.17), custom_call_target="tpu_custom_call" | custom-call | bytes 1572864 | tf_op jit(solution)/shard_map/cond/branch_1_fun/pallas_call | solution.py:220
  15.4 0.0 copy-start.1
  15.4 13.3 %all-to-all-start.1 = ((bf16[32,96,128]{2,1,0:T(8,128)(2,1)}), bf16[32,96,128]{2,1,0:T(8,128)(2,1)S(1)}, u32[]{:S(2)}, u32[]{:S(2)}) async-start(bf16[32,96,128]{2,1,0:T(8,128)(2,1)} %branch_1_fun.3), calls=%async_computation.1 | async-start | bytes 1572864 | tf_op jit(solution)/shard_map/cond/branch_1_fun/all_to_all | solution.py:265
  28.7 0.0 copy-done.1
  28.7 1.1 %branch_1_fun.4 = (f32[512,128]{1,0:T(8,128)S(1)}, f32[512,128]{1,0:T(8,128)S(1)}, f32[512,128]{1,0:T(8,128)S(1)}) custom-call(bf16[1,2,16,4096]{3,2,1,0:T(8,128)(2,1)S(1)} %copy-done.3, bf16[1,2,2,16,4096]{4,3,2,1,0:T(8,128)(2,1)S(1)} %copy-done.1), custom_call_target="tpu_custom_call" | custom-call | bytes 1572864 | tf_op jit(solution)/shard_map/cond/branch_1_fun/pallas_call | solution.py:220
  29.8 1.8 %gather_fusion.1 = f32[2,4096]{1,0:T(2,128)S(1)} fusion(f32[50,4096]{1,0:T(8,128)} %get-tuple-element.38, s32[1024]{0:T(1024)S(1)} %pad_clamp_fusion.1), kind=kCustom, calls=%fused_computation.1 | custom fusion | bytes 65544 | tf_op jit(solution)/shard_map/cond/branch_1_fun/jit(_take)/gather | solution.py:282
  31.6 0.1 reshape.13
  31.8 0.1 pad_maximum_fusion.1
  31.9 11.8 %all-to-all-done.1.x_ref = bf16[32,96,128]{2,1,0:T(8,128)(2,1)S(1)} async-done(((bf16[32,96,128]{2,1,0:T(8,128)(2,1)}), bf16[32,96,128]{2,1,0:T(8,128)(2,1)S(1)}, u32[]{:S(2)}, u32[]{:S(2)}) %all-to-all-start.1) | async-done | bytes 786464 | tf_op jit(solution)/shard_map/cond/branch_1_fun/all_to_all | solution.py:265
  43.6 1.8 %branch_1_fun.5 = bf16[32,17,2,128]{3,2,1,0:T(2,128)(2,1)S(1)} custom-call(bf16[32,96,128]{2,1,0:T(8,128)(2,1)S(1)} %all-to-all-done.1.x_ref), custom_call_target="tpu_custom_call" | custom-call | flops 536870912 | bytes 1064960 | tf_op jit(solution)/shard_map/cond/branch_1_fun/pallas_call | solution.py:220
  45.5 16.9 %all_to_all.13.y_ref = bf16[32,17,2,128]{3,2,1,0:T(2,128)(2,1)S(1)} all-to-all(bf16[32,17,2,128]{3,2,1,0:T(2,128)(2,1)S(1)} %get-tuple-element.50), channel_id=1, replica_groups={{0,2,4,6,8,10,12,14,16,18,20,22,24,26,28,30,32,34,36,38,40,42,44,46,48,..., dimensions={0} | all-to-all | bytes 557056 | tf_op jit(solution)/shard_map/all_to_all | solution.py:265
  62.4 0.5 shard_map.46
  62.9 3.7 %all-gather.2 = bf16[4,512,128]{2,1,0:T(8,128)(2,1)S(1)} all-gather(bf16[2,512,128]{2,1,0:T(8,128)(2,1)S(1)} %shard_map.46), channel_id=4, replica_groups=mesh['clip'=4,'cfg'=2,'patch'=64] {'cfg'}, dimensions={0}, use_global_device_ids=true | all-gather | bytes 786432 | tf_op jit(solution)/shard_map/all_gather | solution.py:313
  66.6 0.9 %shard_map.47 = bf16[2,16,32,64]{3,2,1,0:T(8,128)(2,1)} custom-call(bf16[2,2,512,128]{3,2,1,0:T(8,128)(2,1)S(1)} %bitcast.18, f32[32,128]{1,0:T(8,128)S(1)} %get-tuple-element.54.gate_ref), custom_call_target="tpu_custom_call" | custom-call | bytes 671744 | tf_op jit(solution)/shard_map/pallas_call | solution.py:220
  (2 shorter events, 0.0 us)
Async XLA Ops:
  0.0 0.7 copy-start.4
  1.6 12.8 %copy-start.3 = (bf16[1,2,16,4096]{3,2,1,0:T(8,128)(2,1)S(1)}, bf16[1,2,16,4096]{3,2,1,0:T(8,128)(2,1)}, u32[]{:S(2)}) copy-start(bf16[1,2,16,4096]{3,2,1,0:T(8,128)(2,1)} %get-tuple-element.33.q_ref) | copy-start | bytes 786436 | tf_op jit(solution)/shard_map/cond
  15.4 13.3 %copy-start.1 = (bf16[1,2,2,16,4096]{4,3,2,1,0:T(8,128)(2,1)S(1)}, bf16[1,2,2,16,4096]{4,3,2,1,0:T(8,128)(2,1)}, u32[]{:S(2)}) copy-start(bf16[1,2,2,16,4096]{4,3,2,1,0:T(8,128)(2,1)} %get-tuple-element.34.kv_ref) | copy-start | bytes 1572868 | tf_op jit(solution)/shard_map/cond
  15.4 28.2 %all-to-all-start.1 = ((bf16[32,96,128]{2,1,0:T(8,128)(2,1)}), bf16[32,96,128]{2,1,0:T(8,128)(2,1)S(1)}, u32[]{:S(2)}, u32[]{:S(2)}) async-start(bf16[32,96,128]{2,1,0:T(8,128)(2,1)} %branch_1_fun.3), calls=%async_computation.1 | async-start | bytes 1572864 | tf_op jit(solution)/shard_map/cond/branch_1_fun/all_to_all | solution.py:265

commit v15 on v14

--- a/solution.py
+++ b/solution.py
@@ -12,7 +12,7 @@
 HALF = DEPTH // 2
 TOK = 16
 SIDES = 2
-Y_FIRST = 1
+Y_FIRST = 0
 NEAR = HEADS * TOK
 ROWS = 2 * NEAR
 PAIRS = TOK // 2

time: 67.9 us -> 68.8 us (1.013)
  the two profiles are of different devices: /device:TPU:41 before, /device:TPU:1 now
where the time goes in v15:
time: 68.8 us; the launch traced here: 68.4 us
  blocking collectives  36 us (52%)
  starting transfers between devices  13.9 us (20%)
  waiting for transfers between devices  9.55 us (14%)
  Pallas kernels  6.26 us (9%)
  local copies, waits for them, and re-layouts  2.6 us (4%)
    all_to_all x1, blocking collectives, to_heads(): lax.all_to_all(sent, 'patch', split_axis=0, concat_axis=0, tiled=True, ax...  14.5 us
    all_to_all x1, starting transfers between devices, to_heads(): lax.all_to_all(sent, 'patch', split_axis=0, concat_axis=0, tiled=True, ax...  13.9 us
    all_gather x1, blocking collectives, body(): both = lax.all_gather(attn, 'cfg', axis=0, tiled=False)  11.3 us
    all_gather x1, blocking collectives, over_y(): lax.all_gather(field, 'patch', axis=0, tiled=False, axis_index_groups=pairs)  10.2 us
    all_to_all x1, waiting for transfers between devices, to_heads(): lax.all_to_all(sent, 'patch', split_axis=0, concat_axis=0, tiled=True, ax...  9.55 us
    pallas_call x5, Pallas kernels, call(): pl.pallas_call(kernel, grid=(1,), out_shape=out, in_specs=specs or [vmem]...  6.26 us
    gather x1, local copies, waits for them, and re-layouts, beside(): jnp.take(gate_table, timesteps, axis=0, mode='clip')  1.77 us
  transfers between devices with their start and end apart: 1, of which 1 were waited for; matrix products, arithmetic and copies ran while one was open for 3% of the time, Pallas kernels for 2%

profile of v15, /device:TPU:1, one launch (start us, length us, event | category | flops | bytes accessed | tf_op | source)
XLA Modules:
  0.0 68.4 jit_solution(6688098842444649805)
XLA Ops:
  0.0 0.0 copy-start.4
  0.0 0.7 copy-done.4
  0.7 40.5 %conditional.1 = (bf16[32,17,2,128]{3,2,1,0:T(2,128)(2,1)S(1)}, f32[512,128]{1,0:T(8,128)S(1)}, f32[512,128]{1,0:T(8,128)S(1)}, f32[512,128]{1,0:T(8,128)S(1)}, f32[32,128]{1,0:T(8,128)S(1)}) conditional(s32[]{:T(128)} %convert_element_type.3, (bf16[1,2,16,4096]{3,2,1,0:T(8,128)(2,1)}, bf16[1,2,2,16,4096]{4,3,2,1,0:T(8,128)(2,1)}, s32[2]{0:T(128)S(1)}, ...), branch_computations={%region_0.1_spmd, %region_1.2_spmd} | conditional | flops 536876032 | bytes 11227366 | solution.py:310
  0.7 1.9 %branch_0_fun.3 = bf16[32,64,128]{2,1,0:T(8,128)(2,1)} custom-call(bf16[1,2,16,4096]{3,2,1,0:T(8,128)(2,1)} %get-tuple-element.21.q_ref, bf16[1,2,2,16,4096]{4,3,2,1,0:T(8,128)(2,1)} %get-tuple-element.22.kv_ref), custom_call_target="tpu_custom_call" | custom-call | bytes 1310720 | tf_op jit(solution)/shard_map/cond/branch_0_fun/pallas_call | solution.py:220
  2.5 0.0 copy-start
  2.5 0.0 copy-start.2
  2.6 13.9 %all-to-all-start = ((bf16[32,64,128]{2,1,0:T(8,128)(2,1)}), bf16[32,64,128]{2,1,0:T(8,128)(2,1)S(1)}, u32[]{:S(2)}, u32[]{:S(2)}) async-start(bf16[32,64,128]{2,1,0:T(8,128)(2,1)} %branch_0_fun.3), calls=%async_computation | async-start | bytes 1048576 | tf_op jit(solution)/shard_map/cond/branch_0_fun/all_to_all | solution.py:265
  16.4 0.0 copy-done
  16.4 0.0 copy-done.2
  16.4 1.1 %branch_0_fun.4 = (f32[512,128]{1,0:T(8,128)S(1)}, f32[512,128]{1,0:T(8,128)S(1)}, f32[512,128]{1,0:T(8,128)S(1)}) custom-call(bf16[1,2,16,4096]{3,2,1,0:T(8,128)(2,1)S(1)} %copy-done.2, bf16[1,2,2,16,4096]{4,3,2,1,0:T(8,128)(2,1)S(1)} %copy-done), custom_call_target="tpu_custom_call" | custom-call | bytes 1572864 | tf_op jit(solution)/shard_map/cond/branch_0_fun/pallas_call | solution.py:220
  17.5 1.8 %gather_fusion = f32[2,4096]{1,0:T(2,128)S(1)} fusion(f32[50,4096]{1,0:T(8,128)} %get-tuple-element.26, s32[1024]{0:T(1024)S(1)} %pad_clamp_fusion), kind=kCustom, calls=%fused_computation | custom fusion | bytes 65544 | tf_op jit(solution)/shard_map/cond/branch_0_fun/jit(_take)/gather | solution.py:282
  19.3 0.1 reshape.12
  19.5 0.1 pad_maximum_fusion
  19.6 9.5 %all-to-all-done.x_ref = bf16[32,64,128]{2,1,0:T(8,128)(2,1)S(1)} async-done(((bf16[32,64,128]{2,1,0:T(8,128)(2,1)}), bf16[32,64,128]{2,1,0:T(8,128)(2,1)S(1)}, u32[]{:S(2)}, u32[]{:S(2)}) %all-to-all-start) | async-done | bytes 524320 | tf_op jit(solution)/shard_map/cond/branch_0_fun/all_to_all | solution.py:265
  29.1 10.2 %all-gather = bf16[64,32,128]{2,1,0:T(8,128)(2,1)S(1)} all-gather(bf16[32,32,128]{2,1,0:T(8,128)(2,1)S(1)} %slice.18), channel_id=2, replica_groups={{0,1},{2,3},{4,5},{6,7},{8,9},{10,11},{12,13},{14,15},{16,17},{18,19},{..., dimensions={0}, use_global_device_ids=true | all-gather | bytes 786432 | tf_op jit(solution)/shard_map/cond/branch_0_fun/all_gather | solution.py:270
  39.3 1.8 %branch_0_fun.5 = bf16[32,17,2,128]{3,2,1,0:T(2,128)(2,1)S(1)} custom-call(bf16[32,64,128]{2,1,0:T(8,128)(2,1)S(1)} %all-to-all-done.x_ref, bf16[2,32,32,128]{3,2,1,0:T(8,128)(2,1)S(1)} %bitcast.19), custom_call_target="tpu_custom_call" | custom-call | flops 536870912 | bytes 1327104 | tf_op jit(solution)/shard_map/cond/branch_0_fun/pallas_call | solution.py:220
  41.2 14.5 %all_to_all.13.y_ref = bf16[32,17,2,128]{3,2,1,0:T(2,128)(2,1)S(1)} all-to-all(bf16[32,17,2,128]{3,2,1,0:T(2,128)(2,1)S(1)} %get-tuple-element.50), channel_id=1, replica_groups={{0,2,4,6,8,10,12,14,16,18,20,22,24,26,28,30,32,34,36,38,40,42,44,46,48,..., dimensions={0} | all-to-all | bytes 557056 | tf_op jit(solution)/shard_map/all_to_all | solution.py:265
  55.7 0.5 shard_map.46
  56.2 11.3 %all-gather.2 = bf16[4,512,128]{2,1,0:T(8,128)(2,1)S(1)} all-gather(bf16[2,512,128]{2,1,0:T(8,128)(2,1)S(1)} %shard_map.46), channel_id=4, replica_groups=mesh['clip'=4,'cfg'=2,'patch'=64] {'cfg'}, dimensions={0}, use_global_device_ids=true | all-gather | bytes 786432 | tf_op jit(solution)/shard_map/all_gather | solution.py:313
  67.5 0.9 %shard_map.47 = bf16[2,16,32,64]{3,2,1,0:T(8,128)(2,1)} custom-call(bf16[2,2,512,128]{3,2,1,0:T(8,128)(2,1)S(1)} %bitcast.18, f32[32,128]{1,0:T(8,128)S(1)} %get-tuple-element.54.gate_ref), custom_call_target="tpu_custom_call" | custom-call | bytes 671744 | tf_op jit(solution)/shard_map/pallas_call | solution.py:220
  (3 shorter events, 0.1 us)
Async XLA Ops:
  0.0 0.7 copy-start.4
  2.5 13.9 %copy-start = (bf16[1,2,2,16,4096]{4,3,2,1,0:T(8,128)(2,1)S(1)}, bf16[1,2,2,16,4096]{4,3,2,1,0:T(8,128)(2,1)}, u32[]{:S(2)}) copy-start(bf16[1,2,2,16,4096]{4,3,2,1,0:T(8,128)(2,1)} %get-tuple-element.22.kv_ref) | copy-start | bytes 1572868 | tf_op jit(solution)/shard_map/cond
  2.5 13.9 %copy-start.2 = (bf16[1,2,16,4096]{3,2,1,0:T(8,128)(2,1)S(1)}, bf16[1,2,16,4096]{3,2,1,0:T(8,128)(2,1)}, u32[]{:S(2)}) copy-start(bf16[1,2,16,4096]{3,2,1,0:T(8,128)(2,1)} %get-tuple-element.21.q_ref) | copy-start | bytes 786436 | tf_op jit(solution)/shard_map/cond
  2.6 26.5 %all-to-all-start = ((bf16[32,64,128]{2,1,0:T(8,128)(2,1)}), bf16[32,64,128]{2,1,0:T(8,128)(2,1)S(1)}, u32[]{:S(2)}, u32[]{:S(2)}) async-start(bf16[32,64,128]{2,1,0:T(8,128)(2,1)} %branch_0_fun.3), calls=%async_computation | async-start | bytes 1048576 | tf_op jit(solution)/shard_map/cond/branch_0_fun/all_to_all | solution.py:265

commit v16 on v13

--- a/solution.py
+++ b/solution.py
@@ -30,30 +30,24 @@
     return lax.dot_general(a, b, (((1,), (1,)), ((), ())), preferred_element_type=F32)
 
 
-def pack_kernel(fields, out_ref, held, packed, in_sems, out_sems):
-    loads = [
-        pltpu.make_async_copy(field, held.at[i], in_sems.at[i]) for i, field in enumerate(fields)
-    ]
-    for load in loads:
-        load.start()
+def pack_kernel(fields, out_ref, packed, sems):
     stores = []
-    for i, load in enumerate(loads):
-        load.wait()
+    for i, field in enumerate(fields):
         for h in range(HEADS):
-            packed[i, h] = held[i, :, h * DEPTH : (h + 1) * DEPTH]
+            packed[i, h] = field[:, h * DEPTH : (h + 1) * DEPTH]
         rows = out_ref.at[:, i * TOK : (i + 1) * TOK, :]
-        stores.append(pltpu.make_async_copy(packed.at[i], rows, out_sems.at[i]))
+        stores.append(pltpu.make_async_copy(packed.at[i], rows, sems.at[i]))
         stores[-1].start()
     for store in stores:
         store.wait()
 
 
 def pack_own_kernel(q_ref, kv_ref, *refs):
-    pack_kernel([q_ref.at[0, i] for i in range(2)] + [kv_ref.at[0, 0, i] for i in range(2)], *refs)
+    pack_kernel([ref.at[i] for ref in (q_ref, kv_ref) for i in range(2)], *refs)
 
 
 def pack_both_kernel(q_ref, stale_ref, *refs):
-    fields = [q_ref.at[0, i] for i in range(2)]
+    fields = [q_ref.at[i] for i in range(2)]
     fields += [stale_ref.at[side, i] for side in range(SIDES) for i in range(2)]
     pack_kernel(fields, *refs)
 
@@ -135,7 +129,8 @@
 
 def attend_both_kernel(x_ref, *refs):
     pair = 2 * TOK
-    attend(x_ref, [x_ref.at[:, pair * (1 + half) : pair * (2 + half), :] for half in range(SIDES)], *refs)
+    pairs = [x_ref.at[:, pair * (1 + half) : pair * (2 + half), :] for half in range(SIDES)]
+    attend(x_ref, pairs, *refs)
 
 
 def attend(x_ref, pairs, out_ref, score, weight, top, total):
@@ -189,12 +184,23 @@
     out_ref[1] = jnp.where(lower, pltpu.roll(first, HALF, 1), second).astype(BF16)
 
 
-def guide_kernel(both_ref, gate_ref, out_ref, held):
+def guide_kernel(plan_ref, both_ref, table_ref, out_ref, held, gate):
     core = lax.axis_index("cfg")
+    upper = core == 1
+    lower = lax.broadcasted_iota(jnp.int32, (1, DEPTH), 1) < HALF
+    first, second = (table_ref[pl.ds(plan_ref[step], 1), :] for step in range(2))
+    for h in range(HEADS):
+        lanes = slice(h * DEPTH, (h + 1) * DEPTH)
+        turned = pltpu.roll(jnp.where(upper, first[:, lanes], second[:, lanes]), HALF, 1)
+        gate[h : h + 1] = jnp.where(
+            lower,
+            jnp.where(upper, turned, first[:, lanes]),
+            jnp.where(upper, second[:, lanes], turned),
+        )
     cond = both_ref[0, core].astype(F32)
     uncond = both_ref[1, core].astype(F32)
     mixed = (uncond + 5.0 * (cond - uncond)).reshape(HEADS, TOK, DEPTH)
-    held[...] = (gate_ref[...].reshape(HEADS, 1, DEPTH) * mixed).reshape(NEAR, DEPTH)
+    held[...] = (gate[...].reshape(HEADS, 1, DEPTH) * mixed).reshape(NEAR, DEPTH)
     for t in range(TOK):
         rows = held[pl.ds(t, HEADS, stride=TOK), :]
         out_ref[0, t] = rows[:, :HALF].astype(BF16)
@@ -223,22 +229,23 @@
     width = HEADS * DEPTH
     sides = [[SIDES * i + side for i in range(HEADS)] for side in range(SIDES)]
     pairs = [[SIDES * i, SIDES * i + 1] for i in range(HEADS)]
-    whole = pl.BlockSpec(memory_space=pltpu.HBM)
-
-    def pack(kernel, stale, fields):
+
+    first_pairs = keys_values[0, 0]
+
+    def packed(kernel, pairs, fields):
         return call(
             kernel,
             SHAPE((HEADS, fields * TOK, DEPTH), BF16),
-            (queries, stale),
-            [whole, whole],
+            (queries, pairs),
             [
-                pltpu.VMEM((fields, TOK, width), BF16),
+                pl.BlockSpec((None, 2, TOK, width), lambda i: (0, 0, 0, 0)),
+                pl.BlockSpec(memory_space=pltpu.VMEM),
+            ],
+            [
                 pltpu.VMEM((fields, HEADS, TOK, DEPTH), BF16),
-                pltpu.SemaphoreType.DMA((fields,)),
                 pltpu.SemaphoreType.DMA((fields,)),
             ],
             out_space=pltpu.HBM,
-            limit=60,
         )
 
     def to_heads(sent):
@@ -249,8 +256,8 @@
     def over_y(field):
         return lax.all_gather(field, "patch", axis=0, tiled=False, axis_index_groups=pairs)
 
-    def beside():
-        near = call(
+    def own_patch():
+        return call(
             local_kernel,
             [SHAPE((NEAR, DEPTH), F32)] * 3,
             (queries, keys_values),
@@ -259,9 +266,6 @@
                 pl.BlockSpec((None, None, 2, TOK, width), lambda i: (0, 1, 0, 0, 0)),
             ],
         )
-        gates = jnp.take(gate_table, timesteps, axis=0, mode="clip").reshape(2, HEADS, 2, HALF)
-        gate = lax.dynamic_index_in_dim(gates, lax.axis_index("cfg"), 2, keepdims=False)
-        return near, jnp.concatenate([gate[0], gate[1]], axis=1)
 
     def attended(kernel, args):
         return call(
@@ -278,24 +282,26 @@
         )
 
     def heads_first():
-        held = to_heads(pack(pack_own_kernel, keys_values, 4))
-        held, rest = lax.optimization_barrier((held, beside()))
-        return attended(attend_own_kernel, (held, over_y(held[:, 2 * TOK :, :]))), rest
+        held = to_heads(packed(pack_own_kernel, first_pairs, 4))
+        held, near = lax.optimization_barrier((held, own_patch()))
+        return attended(attend_own_kernel, (held, over_y(held[:, 2 * TOK :, :]))), near
 
     def y_first():
-        held = to_heads(pack(pack_both_kernel, over_y(keys_values[0, 0]), 6))
-        held, rest = lax.optimization_barrier((held, beside()))
-        return attended(attend_both_kernel, (held,)), rest
-
-    far, (near, gate) = lax.cond(lax.axis_index("cfg") == Y_FIRST, y_first, heads_first)
+        held = to_heads(packed(pack_both_kernel, over_y(first_pairs), 6))
+        held, near = lax.optimization_barrier((held, own_patch()))
+        return attended(attend_both_kernel, (held,)), near
+
+    far, near = lax.cond(lax.axis_index("cfg") == Y_FIRST, y_first, heads_first)
     back = to_heads(far)
     attn = call(merge_kernel, SHAPE((2, NEAR, DEPTH), BF16), (back, *near))
     both = lax.all_gather(attn, "cfg", axis=0, tiled=False)
+    vmem = pl.BlockSpec(memory_space=pltpu.VMEM)
     return call(
         guide_kernel,
         SHAPE((2, TOK, HEADS, HALF), BF16),
-        (both, gate),
-        scratch=[pltpu.VMEM((NEAR, DEPTH), F32)],
+        (timesteps, both, gate_table),
+        [pl.BlockSpec(memory_space=pltpu.SMEM), vmem, vmem],
+        scratch=[pltpu.VMEM((NEAR, DEPTH), F32), pltpu.VMEM((HEADS, DEPTH), F32)],
     )
 
 

time: 68.3 us -> 68.4 us (level)
  waiting for transfers between devices: 11.8 us -> 13.8 us
  local copies, waits for them, and re-layouts: 3.55 us -> 1.68 us
  Pallas kernels: 6.7 us -> 5.98 us
  blocking collectives: 32.5 us -> 33.2 us
    all_to_all x1, waiting for transfers between devices: 11.8 us -> 13.8 us  [to_heads(): lax.all_to_all(sent, 'patch', split_axis=0, concat_axis=0, tiled=True, ax...]
    gather x1 -> x0, local copies, waits for them, and re-layouts: 1.77 us -> none  [beside(): jnp.take(gate_table, timesteps, axis=0, mode='clip')]
    all_gather x1, blocking collectives: 2.18 us -> 3.91 us  [body(): both = lax.all_gather(attn, 'cfg', axis=0, tiled=False)]
    all_to_all x1, blocking collectives: 17.5 us -> 16.7 us  [to_heads(): lax.all_to_all(sent, 'patch', split_axis=0, concat_axis=0, tiled=True, ax...]
    pallas_call x5, Pallas kernels: 6.7 us -> 5.98 us  [call(): pl.pallas_call(kernel, grid=(1,), out_shape=out, in_specs=specs or [vmem]...]
  transfers between devices with their start and end apart: 1 -> 1, of which waited for: 1 -> 1; matrix products, arithmetic and copies ran while one was open for 3% -> 0% of each run, Pallas kernels for 2% -> 2%
where the time goes in v16:
time: 68.4 us; the launch traced here: 68.1 us
  blocking collectives  33.2 us (49%)
  waiting for transfers between devices  13.8 us (20%)
  starting transfers between devices  13.3 us (19%)
  Pallas kernels  5.98 us (9%)
  local copies, waits for them, and re-layouts  1.68 us (2%)
    all_to_all x1, blocking collectives, to_heads(): lax.all_to_all(sent, 'patch', split_axis=0, concat_axis=0, tiled=True, ax...  16.7 us
    all_to_all x1, waiting for transfers between devices, to_heads(): lax.all_to_all(sent, 'patch', split_axis=0, concat_axis=0, tiled=True, ax...  13.8 us
    all_to_all x1, starting transfers between devices, to_heads(): lax.all_to_all(sent, 'patch', split_axis=0, concat_axis=0, tiled=True, ax...  13.3 us
    all_gather x1, blocking collectives, over_y(): lax.all_gather(field, 'patch', axis=0, tiled=False, axis_index_groups=pairs)  12.6 us
    pallas_call x5, Pallas kernels, call(): pl.pallas_call(kernel, grid=(1,), out_shape=out, in_specs=specs or [vmem]...  5.98 us
    all_gather x1, blocking collectives, body(): both = lax.all_gather(attn, 'cfg', axis=0, tiled=False)  3.91 us
  transfers between devices with their start and end apart: 1, of which 1 were waited for; matrix products, arithmetic and copies ran while one was open for 0% of the time, Pallas kernels for 2%

profile of v16, /device:TPU:41, one launch (start us, length us, event | category | flops | bytes accessed | tf_op | source)
XLA Modules:
  0.0 68.1 jit_solution(12379294521619663987)
XLA Ops:
  0.0 0.0 copy-start.2
  0.0 1.0 %slice.6 = bf16[1,1,2,16,4096]{4,3,2,1,0:T(8,128)(2,1)S(1)} slice(bf16[1,2,2,16,4096]{4,3,2,1,0:T(8,128)(2,1)} %param.7), slice={[0:1], [0:1], [0:2], [0:16], [0:4096]} | slice | bytes 524288 | tf_op jit(solution)/shard_map/slice | solution.py:233
  1.0 0.0 copy-done.2
  1.0 43.7 %conditional.1 = (bf16[32,17,2,128]{3,2,1,0:T(2,128)(2,1)S(1)}, f32[512,128]{1,0:T(8,128)S(1)}, f32[512,128]{1,0:T(8,128)S(1)}, f32[512,128]{1,0:T(8,128)S(1)}) conditional(s32[]{:T(128)} %convert_element_type.3, (bf16[1,2,16,4096]{3,2,1,0:T(8,128)(2,1)S(1)}, bf16[1,1,2,16,4096]{4,3,2,1,0:T(8,128)(2,1)S(1)}, ...), branch_computations={%region_0.0_spmd, %region_1.0_spmd} | conditional | flops 536870912 | bytes 9453660 | solution.py:294
  1.0 12.6 %all-gather.1 = bf16[2,1,2,16,4096]{4,3,2,1,0:T(8,128)(2,1)S(1)} all-gather(bf16[1,1,2,16,4096]{4,3,2,1,0:T(8,128)(2,1)S(1)} %get-tuple-element.28), channel_id=3, replica_groups={{0,1},{2,3},{4,5},{6,7},{8,9},{10,11},{12,13},{14,15},{16,17},{18,19},{..., dimensions={0}, use_global_device_ids=true | all-gather | bytes 786432 | tf_op jit(solution)/shard_map/cond/branch_1_fun/all_gather | solution.py:257
  13.7 1.0 %branch_1_fun.3 = bf16[32,96,128]{2,1,0:T(8,128)(2,1)} custom-call(bf16[1,2,16,4096]{3,2,1,0:T(8,128)(2,1)S(1)} %get-tuple-element.27.q_ref, bf16[2,2,16,4096]{3,2,1,0:T(8,128)(2,1)S(1)} %bitcast.4), custom_call_target="tpu_custom_call" | custom-call | bytes 1572864 | tf_op jit(solution)/shard_map/cond/branch_1_fun/pallas_call | solution.py:216
  14.6 0.0 copy-start.4
  14.7 13.3 %all-to-all-start.1 = ((bf16[32,96,128]{2,1,0:T(8,128)(2,1)}), bf16[32,96,128]{2,1,0:T(8,128)(2,1)S(1)}, u32[]{:S(2)}, u32[]{:S(2)}) async-start(bf16[32,96,128]{2,1,0:T(8,128)(2,1)} %branch_1_fun.3), calls=%async_computation.1 | async-start | bytes 1572864 | tf_op jit(solution)/shard_map/cond/branch_1_fun/all_to_all | solution.py:252
  28.0 0.0 copy-done.4
  28.0 1.1 %branch_1_fun.4 = (f32[512,128]{1,0:T(8,128)S(1)}, f32[512,128]{1,0:T(8,128)S(1)}, f32[512,128]{1,0:T(8,128)S(1)}) custom-call(bf16[1,2,16,4096]{3,2,1,0:T(8,128)(2,1)S(1)} %get-tuple-element.27.q_ref, bf16[1,2,2,16,4096]{4,3,2,1,0:T(8,128)(2,1)S(1)} %copy-done.4), custom_call_target="tpu_custom_call" | custom-call | bytes 1572864 | tf_op jit(solution)/shard_map/cond/branch_1_fun/pallas_call | solution.py:216
  29.1 13.8 %all-to-all-done.1.x_ref = bf16[32,96,128]{2,1,0:T(8,128)(2,1)S(1)} async-done(((bf16[32,96,128]{2,1,0:T(8,128)(2,1)}), bf16[32,96,128]{2,1,0:T(8,128)(2,1)S(1)}, u32[]{:S(2)}, u32[]{:S(2)}) %all-to-all-start.1) | async-done | bytes 786464 | tf_op jit(solution)/shard_map/cond/branch_1_fun/all_to_all | solution.py:252
  42.9 1.8 %branch_1_fun.5 = bf16[32,17,2,128]{3,2,1,0:T(2,128)(2,1)S(1)} custom-call(bf16[32,96,128]{2,1,0:T(8,128)(2,1)S(1)} %all-to-all-done.1.x_ref), custom_call_target="tpu_custom_call" | custom-call | flops 536870912 | bytes 1064960 | tf_op jit(solution)/shard_map/cond/branch_1_fun/pallas_call | solution.py:216
  44.7 16.7 %all_to_all.13.y_ref = bf16[32,17,2,128]{3,2,1,0:T(2,128)(2,1)S(1)} all-to-all(bf16[32,17,2,128]{3,2,1,0:T(2,128)(2,1)S(1)} %get-tuple-element.41), channel_id=1, replica_groups={{0,2,4,6,8,10,12,14,16,18,20,22,24,26,28,30,32,34,36,38,40,42,44,46,48,..., dimensions={0} | all-to-all | bytes 557056 | tf_op jit(solution)/shard_map/all_to_all | solution.py:252
  61.4 0.0 copy-start
  61.4 0.5 shard_map.46
  62.0 3.9 %all-gather.2 = bf16[4,512,128]{2,1,0:T(8,128)(2,1)S(1)} all-gather(bf16[2,512,128]{2,1,0:T(8,128)(2,1)S(1)} %shard_map.46), channel_id=4, replica_groups=mesh['clip'=4,'cfg'=2,'patch'=64] {'cfg'}, dimensions={0}, use_global_device_ids=true | all-gather | bytes 786432 | tf_op jit(solution)/shard_map/all_gather | solution.py:297
  65.9 0.0 copy-start.1
  65.9 0.0 copy-done
  65.9 0.7 copy-done.1
  66.5 1.5 %shard_map.47 = bf16[2,16,32,64]{3,2,1,0:T(8,128)(2,1)} custom-call(s32[2]{0:T(128)S(1)} %copy-done.1, bf16[2,2,512,128]{3,2,1,0:T(8,128)(2,1)S(1)} %bitcast.5, f32[50,4096]{1,0:T(8,128)S(1)} %copy-done), custom_call_target="tpu_custom_call" | custom-call | bytes 1474568 | tf_op jit(solution)/shard_map/pallas_call | solution.py:216
Async XLA Ops:
  0.0 1.0 %copy-start.2 = (bf16[1,2,16,4096]{3,2,1,0:T(8,128)(2,1)S(1)}, bf16[1,2,16,4096]{3,2,1,0:T(8,128)(2,1)}, u32[]{:S(2)}) copy-start(bf16[1,2,16,4096]{3,2,1,0:T(8,128)(2,1)} %param.6) | copy-start | bytes 786436
  14.6 13.3 %copy-start.4 = (bf16[1,2,2,16,4096]{4,3,2,1,0:T(8,128)(2,1)S(1)}, bf16[1,2,2,16,4096]{4,3,2,1,0:T(8,128)(2,1)}, u32[]{:S(2)}) copy-start(bf16[1,2,2,16,4096]{4,3,2,1,0:T(8,128)(2,1)} %get-tuple-element.29.kv_ref) | copy-start | bytes 1572868 | tf_op jit(solution)/shard_map/cond
  14.7 28.2 %all-to-all-start.1 = ((bf16[32,96,128]{2,1,0:T(8,128)(2,1)}), bf16[32,96,128]{2,1,0:T(8,128)(2,1)S(1)}, u32[]{:S(2)}, u32[]{:S(2)}) async-start(bf16[32,96,128]{2,1,0:T(8,128)(2,1)} %branch_1_fun.3), calls=%async_computation.1 | async-start | bytes 1572864 | tf_op jit(solution)/shard_map/cond/branch_1_fun/all_to_all | solution.py:252
  61.4 4.5 %copy-start = (f32[50,4096]{1,0:T(8,128)S(1)}, f32[50,4096]{1,0:T(8,128)}, u32[]{:S(2)}) copy-start(f32[50,4096]{1,0:T(8,128)} %table_ref.1) | copy-start | bytes 2457604
  65.9 0.7 copy-start.1

commit v17 on v16

--- a/solution.py
+++ b/solution.py
@@ -184,23 +184,12 @@
     out_ref[1] = jnp.where(lower, pltpu.roll(first, HALF, 1), second).astype(BF16)
 
 
-def guide_kernel(plan_ref, both_ref, table_ref, out_ref, held, gate):
+def guide_kernel(both_ref, gate_ref, out_ref, held):
     core = lax.axis_index("cfg")
-    upper = core == 1
-    lower = lax.broadcasted_iota(jnp.int32, (1, DEPTH), 1) < HALF
-    first, second = (table_ref[pl.ds(plan_ref[step], 1), :] for step in range(2))
-    for h in range(HEADS):
-        lanes = slice(h * DEPTH, (h + 1) * DEPTH)
-        turned = pltpu.roll(jnp.where(upper, first[:, lanes], second[:, lanes]), HALF, 1)
-        gate[h : h + 1] = jnp.where(
-            lower,
-            jnp.where(upper, turned, first[:, lanes]),
-            jnp.where(upper, second[:, lanes], turned),
-        )
     cond = both_ref[0, core].astype(F32)
     uncond = both_ref[1, core].astype(F32)
     mixed = (uncond + 5.0 * (cond - uncond)).reshape(HEADS, TOK, DEPTH)
-    held[...] = (gate[...].reshape(HEADS, 1, DEPTH) * mixed).reshape(NEAR, DEPTH)
+    held[...] = (gate_ref[...].reshape(HEADS, 1, DEPTH) * mixed).reshape(NEAR, DEPTH)
     for t in range(TOK):
         rows = held[pl.ds(t, HEADS, stride=TOK), :]
         out_ref[0, t] = rows[:, :HALF].astype(BF16)
@@ -293,15 +282,17 @@
 
     far, near = lax.cond(lax.axis_index("cfg") == Y_FIRST, y_first, heads_first)
     back = to_heads(far)
+    gates = jnp.take(gate_table, timesteps, axis=0, mode="clip").reshape(2, HEADS, 2, HALF)
+    gate = lax.dynamic_index_in_dim(gates, lax.axis_index("cfg"), 2, keepdims=False)
+    gate = jnp.concatenate([gate[0], gate[1]], axis=1)
+    back, gate = lax.optimization_barrier((back, gate))
     attn = call(merge_kernel, SHAPE((2, NEAR, DEPTH), BF16), (back, *near))
     both = lax.all_gather(attn, "cfg", axis=0, tiled=False)
-    vmem = pl.BlockSpec(memory_space=pltpu.VMEM)
     return call(
         guide_kernel,
         SHAPE((2, TOK, HEADS, HALF), BF16),
-        (timesteps, both, gate_table),
-        [pl.BlockSpec(memory_space=pltpu.SMEM), vmem, vmem],
-        scratch=[pltpu.VMEM((NEAR, DEPTH), F32), pltpu.VMEM((HEADS, DEPTH), F32)],
+        (both, gate),
+        scratch=[pltpu.VMEM((NEAR, DEPTH), F32)],
     )
 
 

time: 68.4 us -> 68.2 us (level)
  blocking collectives: 33.2 us -> 16.5 us
  waiting for transfers between devices: 13.8 us -> 25.1 us
  starting transfers between devices: 13.3 us -> 18.2 us
    all_to_all x1 -> x0, blocking collectives: 16.7 us -> none  [to_heads(): lax.all_to_all(sent, 'patch', split_axis=0, concat_axis=0, tiled=True, ax...]
    all_to_all x1 -> x2, waiting for transfers between devices: 13.8 us -> 25.1 us  [to_heads(): lax.all_to_all(sent, 'patch', split_axis=0, concat_axis=0, tiled=True, ax...]
    all_to_all x1 -> x2, starting transfers between devices: 13.3 us -> 18.2 us  [to_heads(): lax.all_to_all(sent, 'patch', split_axis=0, concat_axis=0, tiled=True, ax...]
  transfers between devices with their start and end apart: 1 -> 2, of which waited for: 1 -> 2; matrix products, arithmetic and copies ran while one was open for 0% -> 1% of each run, Pallas kernels for 2% -> 2%
where the time goes in v17:
time: 68.2 us; the launch traced here: 67.9 us
  waiting for transfers between devices  25.1 us (37%)
  starting transfers between devices  18.2 us (27%)
  blocking collectives  16.5 us (24%)
  Pallas kernels  6.06 us (9%)
  local copies, waits for them, and re-layouts  1.84 us (3%)
    all_to_all x2, waiting for transfers between devices, to_heads(): lax.all_to_all(sent, 'patch', split_axis=0, concat_axis=0, tiled=True, ax...  25.1 us
    all_to_all x2, starting transfers between devices, to_heads(): lax.all_to_all(sent, 'patch', split_axis=0, concat_axis=0, tiled=True, ax...  18.2 us
    all_gather x1, blocking collectives, over_y(): lax.all_gather(field, 'patch', axis=0, tiled=False, axis_index_groups=pairs)  12.6 us
    pallas_call x5, Pallas kernels, call(): pl.pallas_call(kernel, grid=(1,), out_shape=out, in_specs=specs or [vmem]...  6.06 us
    all_gather x1, blocking collectives, body(): both = lax.all_gather(attn, 'cfg', axis=0, tiled=False)  3.91 us
  transfers between devices with their start and end apart: 2, of which 2 were waited for; matrix products, arithmetic and copies ran while one was open for 1% of the time, Pallas kernels for 2%

profile of v17, /device:TPU:41, one launch (start us, length us, event | category | flops | bytes accessed | tf_op | source)
XLA Modules:
  0.0 67.9 jit_solution(12583956441975725671)
XLA Ops:
  0.0 0.0 copy-start
  0.0 0.0 copy-start.1
  0.0 1.1 %slice.14 = bf16[1,1,2,16,4096]{4,3,2,1,0:T(8,128)(2,1)S(1)} slice(bf16[1,2,2,16,4096]{4,3,2,1,0:T(8,128)(2,1)} %param.7), slice={[0:1], [0:1], [0:2], [0:16], [0:4096]} | slice | bytes 524288 | tf_op jit(solution)/shard_map/slice | solution.py:222
  1.1 0.0 copy-done.1
  1.1 44.3 %conditional.1 = (bf16[32,17,2,128]{3,2,1,0:T(2,128)(2,1)}, f32[512,128]{1,0:T(8,128)S(1)}, f32[512,128]{1,0:T(8,128)S(1)}, f32[512,128]{1,0:T(8,128)S(1)}) conditional(s32[]{:T(128)} %convert_element_type.3, (bf16[1,2,16,4096]{3,2,1,0:T(8,128)(2,1)S(1)}, bf16[1,1,2,16,4096]{4,3,2,1,0:T(8,128)(2,1)S(1)}, ...), branch_computations={%region_0.0_spmd, %region_1.0_spmd} | conditional | flops 536870912 | bytes 9453660 | solution.py:283
  1.1 12.6 %all-gather.1 = bf16[2,1,2,16,4096]{4,3,2,1,0:T(8,128)(2,1)S(1)} all-gather(bf16[1,1,2,16,4096]{4,3,2,1,0:T(8,128)(2,1)S(1)} %get-tuple-element.28), channel_id=3, replica_groups={{0,1},{2,3},{4,5},{6,7},{8,9},{10,11},{12,13},{14,15},{16,17},{18,19},{..., dimensions={0}, use_global_device_ids=true | all-gather | bytes 786432 | tf_op jit(solution)/shard_map/cond/branch_1_fun/all_gather | solution.py:246
  13.7 1.0 %branch_1_fun.3 = bf16[32,96,128]{2,1,0:T(8,128)(2,1)} custom-call(bf16[1,2,16,4096]{3,2,1,0:T(8,128)(2,1)S(1)} %get-tuple-element.27.q_ref, bf16[2,2,16,4096]{3,2,1,0:T(8,128)(2,1)S(1)} %bitcast.11), custom_call_target="tpu_custom_call" | custom-call | bytes 1572864 | tf_op jit(solution)/shard_map/cond/branch_1_fun/pallas_call | solution.py:205
  14.7 0.0 copy-start.3
  14.7 13.3 %all-to-all-start.1 = ((bf16[32,96,128]{2,1,0:T(8,128)(2,1)}), bf16[32,96,128]{2,1,0:T(8,128)(2,1)S(1)}, u32[]{:S(2)}, u32[]{:S(2)}) async-start(bf16[32,96,128]{2,1,0:T(8,128)(2,1)} %branch_1_fun.3), calls=%async_computation.1 | async-start | bytes 1572864 | tf_op jit(solution)/shard_map/cond/branch_1_fun/all_to_all | solution.py:241
  28.0 0.0 copy-done.3
  28.0 1.1 %branch_1_fun.4 = (f32[512,128]{1,0:T(8,128)S(1)}, f32[512,128]{1,0:T(8,128)S(1)}, f32[512,128]{1,0:T(8,128)S(1)}) custom-call(bf16[1,2,16,4096]{3,2,1,0:T(8,128)(2,1)S(1)} %get-tuple-element.27.q_ref, bf16[1,2,2,16,4096]{4,3,2,1,0:T(8,128)(2,1)S(1)} %copy-done.3), custom_call_target="tpu_custom_call" | custom-call | bytes 1572864 | tf_op jit(solution)/shard_map/cond/branch_1_fun/pallas_call | solution.py:205
  29.1 13.8 %all-to-all-done.1.x_ref = bf16[32,96,128]{2,1,0:T(8,128)(2,1)S(1)} async-done(((bf16[32,96,128]{2,1,0:T(8,128)(2,1)}), bf16[32,96,128]{2,1,0:T(8,128)(2,1)S(1)}, u32[]{:S(2)}, u32[]{:S(2)}) %all-to-all-start.1) | async-done | bytes 786464 | tf_op jit(solution)/shard_map/cond/branch_1_fun/all_to_all | solution.py:241
  42.9 2.5 %branch_1_fun.5 = bf16[32,17,2,128]{3,2,1,0:T(2,128)(2,1)} custom-call(bf16[32,96,128]{2,1,0:T(8,128)(2,1)S(1)} %all-to-all-done.1.x_ref), custom_call_target="tpu_custom_call" | custom-call | flops 536870912 | bytes 1064960 | tf_op jit(solution)/shard_map/cond/branch_1_fun/pallas_call | solution.py:205
  45.5 0.0 copy-start.4
  45.5 4.8 %all-to-all-start.2 = ((bf16[32,17,2,128]{3,2,1,0:T(2,128)(2,1)}), bf16[32,17,2,128]{3,2,1,0:T(2,128)(2,1)S(1)}, u32[]{:S(2)}, u32[]{:S(2)}) async-start(bf16[32,17,2,128]{3,2,1,0:T(2,128)(2,1)} %get-tuple-element.43), calls=%async_computation.2 | async-start | bytes 557056 | tf_op jit(solution)/shard_map/all_to_all | solution.py:241
  50.3 0.0 copy-done.4
  50.3 0.0 copy-done
  50.3 0.6 gather_fusion
  50.9 0.1 reshape.7
  51.1 0.1 pad_maximum_fusion.gate_ref
  51.2 11.3 %all-to-all-done.2.y_ref = bf16[32,17,2,128]{3,2,1,0:T(2,128)(2,1)S(1)} async-done(((bf16[32,17,2,128]{3,2,1,0:T(2,128)(2,1)}), bf16[32,17,2,128]{3,2,1,0:T(2,128)(2,1)S(1)}, u32[]{:S(2)}, u32[]{:S(2)}) %all-to-all-start.2) | async-done | bytes 278560 | tf_op jit(solution)/shard_map/all_to_all | solution.py:241
  62.5 0.5 shard_map.46
  63.1 3.9 %all-gather.2 = bf16[4,512,128]{2,1,0:T(8,128)(2,1)S(1)} all-gather(bf16[2,512,128]{2,1,0:T(8,128)(2,1)S(1)} %shard_map.46), channel_id=4, replica_groups=mesh['clip'=4,'cfg'=2,'patch'=64] {'cfg'}, dimensions={0}, use_global_device_ids=true | all-gather | bytes 786432 | tf_op jit(solution)/shard_map/all_gather | solution.py:290
  67.0 0.9 %shard_map.47 = bf16[2,16,32,64]{3,2,1,0:T(8,128)(2,1)} custom-call(bf16[2,2,512,128]{3,2,1,0:T(8,128)(2,1)S(1)} %bitcast.12, f32[32,128]{1,0:T(8,128)S(1)} %pad_maximum_fusion.gate_ref), custom_call_target="tpu_custom_call" | custom-call | bytes 671744 | tf_op jit(solution)/shard_map/pallas_call | solution.py:205
  (2 shorter events, 0.0 us)
Async XLA Ops:
  0.0 50.3 %copy-start = (f32[50,4096]{1,0:T(8,128)S(1)}, f32[50,4096]{1,0:T(8,128)}, u32[]{:S(2)}) copy-start(f32[50,4096]{1,0:T(8,128)} %param.9) | copy-start | bytes 2457604
  0.0 1.1 %copy-start.1 = (bf16[1,2,16,4096]{3,2,1,0:T(8,128)(2,1)S(1)}, bf16[1,2,16,4096]{3,2,1,0:T(8,128)(2,1)}, u32[]{:S(2)}) copy-start(bf16[1,2,16,4096]{3,2,1,0:T(8,128)(2,1)} %param.6) | copy-start | bytes 786436
  14.7 13.3 %copy-start.3 = (bf16[1,2,2,16,4096]{4,3,2,1,0:T(8,128)(2,1)S(1)}, bf16[1,2,2,16,4096]{4,3,2,1,0:T(8,128)(2,1)}, u32[]{:S(2)}) copy-start(bf16[1,2,2,16,4096]{4,3,2,1,0:T(8,128)(2,1)} %get-tuple-element.29.kv_ref) | copy-start | bytes 1572868 | tf_op jit(solution)/shard_map/cond
  14.7 28.2 %all-to-all-start.1 = ((bf16[32,96,128]{2,1,0:T(8,128)(2,1)}), bf16[32,96,128]{2,1,0:T(8,128)(2,1)S(1)}, u32[]{:S(2)}, u32[]{:S(2)}) async-start(bf16[32,96,128]{2,1,0:T(8,128)(2,1)} %branch_1_fun.3), calls=%async_computation.1 | async-start | bytes 1572864 | tf_op jit(solution)/shard_map/cond/branch_1_fun/all_to_all | solution.py:241
  45.5 4.9 %copy-start.4 = (s32[2]{0:T(128)S(1)}, s32[2]{0:T(128)}, u32[]{:S(2)}) copy-start(s32[2]{0:T(128)} %param.8) | copy-start | bytes 28
  45.5 17.0 %all-to-all-start.2 = ((bf16[32,17,2,128]{3,2,1,0:T(2,128)(2,1)}), bf16[32,17,2,128]{3,2,1,0:T(2,128)(2,1)S(1)}, u32[]{:S(2)}, u32[]{:S(2)}) async-start(bf16[32,17,2,128]{3,2,1,0:T(2,128)(2,1)} %get-tuple-element.43), calls=%async_computation.2 | async-start | bytes 557056 | tf_op jit(solution)/shard_map/all_to_all | solution.py:241

commit v18 on v17

--- a/solution.py
+++ b/solution.py
@@ -133,7 +133,7 @@
     attend(x_ref, pairs, *refs)
 
 
-def attend(x_ref, pairs, out_ref, score, weight, top, total):
+def attend(x_ref, pairs, out_ref, staged, sems, score, weight, top, total):
     side = lax.axis_index("patch") % SIDES
     row = lax.broadcasted_iota(jnp.int32, (BLOCK, BLOCK), 0)
     col = lax.broadcasted_iota(jnp.int32, (BLOCK, BLOCK), 1)
@@ -145,6 +145,8 @@
         for half in range(SIDES):
             keys = pairs[half][:, 0:TOK, :].reshape(NEAR, DEPTH)
             score[steps[step], half * NEAR : (half + 1) * NEAR] = dot_t(query, keys)
+    values = jnp.concatenate([pair[:, TOK:, :].reshape(NEAR, DEPTH) for pair in pairs], 0)
+    stores = []
     for step in range(2):
         for i in range(NEAR // BLOCK):
             here = slice(step * NEAR + i * BLOCK, step * NEAR + (i + 1) * BLOCK)
@@ -160,14 +162,19 @@
             top[here] = jnp.broadcast_to(most, (BLOCK, DEPTH))
             total[here] = jnp.broadcast_to(added, (BLOCK, DEPTH))
             weight[here] = weights.astype(BF16)
-    values = jnp.concatenate([pair[:, TOK:, :].reshape(NEAR, DEPTH) for pair in pairs], 0)
-    for step in range(2):
         rows = steps[step]
         attn = jnp.dot(weight[rows], values, preferred_element_type=F32) / total[rows]
-        out_ref[:, step * PAIRS : (step + 1) * PAIRS] = write_rows(attn)
-    for i in range(NEAR // BLOCK):
-        rows = slice(NEAR + i * BLOCK, NEAR + (i + 1) * BLOCK)
-        out_ref[i * n : (i + 1) * n, 2 * PAIRS] = write_stats(top[rows], total[rows])
+        done = slice(step * PAIRS, (step + 1) * PAIRS + step)
+        staged[:, step * PAIRS : (step + 1) * PAIRS] = write_rows(attn)
+        if step == 1:
+            for i in range(NEAR // BLOCK):
+                rows = slice(NEAR + i * BLOCK, NEAR + (i + 1) * BLOCK)
+                staged[i * n : (i + 1) * n, 2 * PAIRS] = write_stats(top[rows], total[rows])
+        store = pltpu.make_async_copy(staged.at[:, done], out_ref.at[:, done], sems.at[step])
+        store.start()
+        stores.append(store)
+    for store in stores:
+        store.wait()
 
 
 def merge_kernel(y_ref, near_ref, top_ref, total_ref, out_ref):
@@ -262,12 +269,15 @@
             SHAPE((HEADS, 2 * PAIRS + 1, 2, DEPTH), BF16),
             args,
             scratch=[
+                pltpu.VMEM((HEADS, 2 * PAIRS + 1, 2, DEPTH), BF16),
+                pltpu.SemaphoreType.DMA((2,)),
                 pltpu.VMEM((ROWS, TOKENS), F32),
                 pltpu.VMEM((ROWS, TOKENS), BF16),
                 pltpu.VMEM((ROWS, DEPTH), F32),
                 pltpu.VMEM((ROWS, DEPTH), F32),
             ],
             flops=4 * ROWS * TOKENS * DEPTH,
+            out_space=pltpu.HBM,
         )
 
     def heads_first():

time: 68.2 us -> 68.2 us (level)
  no operation moved by 1% of the time
where the time goes in v18:
time: 68.2 us; the launch traced here: 67.8 us
  waiting for transfers between devices  25.1 us (37%)
  starting transfers between devices  18.1 us (27%)
  blocking collectives  16.5 us (24%)
  Pallas kernels  6.09 us (9%)
  local copies, waits for them, and re-layouts  1.84 us (3%)
    all_to_all x2, waiting for transfers between devices, to_heads(): lax.all_to_all(sent, 'patch', split_axis=0, concat_axis=0, tiled=True, ax...  25.1 us
    all_to_all x2, starting transfers between devices, to_heads(): lax.all_to_all(sent, 'patch', split_axis=0, concat_axis=0, tiled=True, ax...  18.1 us
    all_gather x1, blocking collectives, over_y(): lax.all_gather(field, 'patch', axis=0, tiled=False, axis_index_groups=pairs)  12.6 us
    pallas_call x5, Pallas kernels, call(): pl.pallas_call(kernel, grid=(1,), out_shape=out, in_specs=specs or [vmem]...  6.09 us
    all_gather x1, blocking collectives, body(): both = lax.all_gather(attn, 'cfg', axis=0, tiled=False)  3.91 us
  transfers between devices with their start and end apart: 2, of which 2 were waited for; matrix products, arithmetic and copies ran while one was open for 1% of the time, Pallas kernels for 2%

profile of v18, /device:TPU:41, one launch (start us, length us, event | category | flops | bytes accessed | tf_op | source)
XLA Modules:
  0.0 67.8 jit_solution(17525741461105496115)
XLA Ops:
  0.0 0.0 copy-start
  0.0 0.0 copy-start.1
  0.0 1.1 %slice.14 = bf16[1,1,2,16,4096]{4,3,2,1,0:T(8,128)(2,1)S(1)} slice(bf16[1,2,2,16,4096]{4,3,2,1,0:T(8,128)(2,1)} %param.7), slice={[0:1], [0:1], [0:2], [0:16], [0:4096]} | slice | bytes 524288 | tf_op jit(solution)/shard_map/slice | solution.py:229
  1.1 0.0 copy-done.1
  1.1 44.4 %conditional.1 = (bf16[32,17,2,128]{3,2,1,0:T(2,128)(2,1)}, f32[512,128]{1,0:T(8,128)S(1)}, f32[512,128]{1,0:T(8,128)S(1)}, f32[512,128]{1,0:T(8,128)S(1)}) conditional(s32[]{:T(128)} %convert_element_type.3, (bf16[1,2,16,4096]{3,2,1,0:T(8,128)(2,1)S(1)}, bf16[1,1,2,16,4096]{4,3,2,1,0:T(8,128)(2,1)S(1)}, ...), branch_computations={%region_0.0_spmd, %region_1.0_spmd} | conditional | flops 536870912 | bytes 9453660 | solution.py:293
  1.1 12.6 %all-gather.1 = bf16[2,1,2,16,4096]{4,3,2,1,0:T(8,128)(2,1)S(1)} all-gather(bf16[1,1,2,16,4096]{4,3,2,1,0:T(8,128)(2,1)S(1)} %get-tuple-element.28), channel_id=3, replica_groups={{0,1},{2,3},{4,5},{6,7},{8,9},{10,11},{12,13},{14,15},{16,17},{18,19},{..., dimensions={0}, use_global_device_ids=true | all-gather | bytes 786432 | tf_op jit(solution)/shard_map/cond/branch_1_fun/all_gather | solution.py:253
  13.7 1.0 %branch_1_fun.3 = bf16[32,96,128]{2,1,0:T(8,128)(2,1)} custom-call(bf16[1,2,16,4096]{3,2,1,0:T(8,128)(2,1)S(1)} %get-tuple-element.27.q_ref, bf16[2,2,16,4096]{3,2,1,0:T(8,128)(2,1)S(1)} %bitcast.11), custom_call_target="tpu_custom_call" | custom-call | bytes 1572864 | tf_op jit(solution)/shard_map/cond/branch_1_fun/pallas_call | solution.py:212
  14.7 0.0 copy-start.3
  14.7 13.3 %all-to-all-start.1 = ((bf16[32,96,128]{2,1,0:T(8,128)(2,1)}), bf16[32,96,128]{2,1,0:T(8,128)(2,1)S(1)}, u32[]{:S(2)}, u32[]{:S(2)}) async-start(bf16[32,96,128]{2,1,0:T(8,128)(2,1)} %branch_1_fun.3), calls=%async_computation.1 | async-start | bytes 1572864 | tf_op jit(solution)/shard_map/cond/branch_1_fun/all_to_all | solution.py:248
  28.0 0.0 copy-done.3
  28.0 1.1 %branch_1_fun.4 = (f32[512,128]{1,0:T(8,128)S(1)}, f32[512,128]{1,0:T(8,128)S(1)}, f32[512,128]{1,0:T(8,128)S(1)}) custom-call(bf16[1,2,16,4096]{3,2,1,0:T(8,128)(2,1)S(1)} %get-tuple-element.27.q_ref, bf16[1,2,2,16,4096]{4,3,2,1,0:T(8,128)(2,1)S(1)} %copy-done.3), custom_call_target="tpu_custom_call" | custom-call | bytes 1572864 | tf_op jit(solution)/shard_map/cond/branch_1_fun/pallas_call | solution.py:212
  29.1 13.8 %all-to-all-done.1.x_ref = bf16[32,96,128]{2,1,0:T(8,128)(2,1)S(1)} async-done(((bf16[32,96,128]{2,1,0:T(8,128)(2,1)}), bf16[32,96,128]{2,1,0:T(8,128)(2,1)S(1)}, u32[]{:S(2)}, u32[]{:S(2)}) %all-to-all-start.1) | async-done | bytes 786464 | tf_op jit(solution)/shard_map/cond/branch_1_fun/all_to_all | solution.py:248
  42.9 2.6 %branch_1_fun.5 = bf16[32,17,2,128]{3,2,1,0:T(2,128)(2,1)} custom-call(bf16[32,96,128]{2,1,0:T(8,128)(2,1)S(1)} %all-to-all-done.1.x_ref), custom_call_target="tpu_custom_call" | custom-call | flops 536870912 | bytes 1064960 | tf_op jit(solution)/shard_map/cond/branch_1_fun/pallas_call | solution.py:212
  45.5 0.0 copy-start.4
  45.5 4.7 %all-to-all-start.2 = ((bf16[32,17,2,128]{3,2,1,0:T(2,128)(2,1)}), bf16[32,17,2,128]{3,2,1,0:T(2,128)(2,1)S(1)}, u32[]{:S(2)}, u32[]{:S(2)}) async-start(bf16[32,17,2,128]{3,2,1,0:T(2,128)(2,1)} %get-tuple-element.43), calls=%async_computation.2 | async-start | bytes 557056 | tf_op jit(solution)/shard_map/all_to_all | solution.py:248
  50.2 0.0 copy-done.4
  50.3 0.0 copy-done
  50.3 0.6 gather_fusion
  50.9 0.1 reshape.7
  51.0 0.1 pad_maximum_fusion.gate_ref
  51.1 11.3 %all-to-all-done.2.y_ref = bf16[32,17,2,128]{3,2,1,0:T(2,128)(2,1)S(1)} async-done(((bf16[32,17,2,128]{3,2,1,0:T(2,128)(2,1)}), bf16[32,17,2,128]{3,2,1,0:T(2,128)(2,1)S(1)}, u32[]{:S(2)}, u32[]{:S(2)}) %all-to-all-start.2) | async-done | bytes 278560 | tf_op jit(solution)/shard_map/all_to_all | solution.py:248
  62.4 0.5 shard_map.46
  63.0 3.9 %all-gather.2 = bf16[4,512,128]{2,1,0:T(8,128)(2,1)S(1)} all-gather(bf16[2,512,128]{2,1,0:T(8,128)(2,1)S(1)} %shard_map.46), channel_id=4, replica_groups=mesh['clip'=4,'cfg'=2,'patch'=64] {'cfg'}, dimensions={0}, use_global_device_ids=true | all-gather | bytes 786432 | tf_op jit(solution)/shard_map/all_gather | solution.py:300
  66.9 0.9 %shard_map.47 = bf16[2,16,32,64]{3,2,1,0:T(8,128)(2,1)} custom-call(bf16[2,2,512,128]{3,2,1,0:T(8,128)(2,1)S(1)} %bitcast.12, f32[32,128]{1,0:T(8,128)S(1)} %pad_maximum_fusion.gate_ref), custom_call_target="tpu_custom_call" | custom-call | bytes 671744 | tf_op jit(solution)/shard_map/pallas_call | solution.py:212
  (2 shorter events, 0.0 us)
Async XLA Ops:
  0.0 50.3 %copy-start = (f32[50,4096]{1,0:T(8,128)S(1)}, f32[50,4096]{1,0:T(8,128)}, u32[]{:S(2)}) copy-start(f32[50,4096]{1,0:T(8,128)} %param.9) | copy-start | bytes 2457604
  0.0 1.1 %copy-start.1 = (bf16[1,2,16,4096]{3,2,1,0:T(8,128)(2,1)S(1)}, bf16[1,2,16,4096]{3,2,1,0:T(8,128)(2,1)}, u32[]{:S(2)}) copy-start(bf16[1,2,16,4096]{3,2,1,0:T(8,128)(2,1)} %param.6) | copy-start | bytes 786436
  14.7 13.3 %copy-start.3 = (bf16[1,2,2,16,4096]{4,3,2,1,0:T(8,128)(2,1)S(1)}, bf16[1,2,2,16,4096]{4,3,2,1,0:T(8,128)(2,1)}, u32[]{:S(2)}) copy-start(bf16[1,2,2,16,4096]{4,3,2,1,0:T(8,128)(2,1)} %get-tuple-element.29.kv_ref) | copy-start | bytes 1572868 | tf_op jit(solution)/shard_map/cond
  14.7 28.2 %all-to-all-start.1 = ((bf16[32,96,128]{2,1,0:T(8,128)(2,1)}), bf16[32,96,128]{2,1,0:T(8,128)(2,1)S(1)}, u32[]{:S(2)}, u32[]{:S(2)}) async-start(bf16[32,96,128]{2,1,0:T(8,128)(2,1)} %branch_1_fun.3), calls=%async_computation.1 | async-start | bytes 1572864 | tf_op jit(solution)/shard_map/cond/branch_1_fun/all_to_all | solution.py:248
  45.5 4.8 %copy-start.4 = (s32[2]{0:T(128)S(1)}, s32[2]{0:T(128)}, u32[]{:S(2)}) copy-start(s32[2]{0:T(128)} %param.8) | copy-start | bytes 28
  45.5 16.9 %all-to-all-start.2 = ((bf16[32,17,2,128]{3,2,1,0:T(2,128)(2,1)}), bf16[32,17,2,128]{3,2,1,0:T(2,128)(2,1)S(1)}, u32[]{:S(2)}, u32[]{:S(2)}) async-start(bf16[32,17,2,128]{3,2,1,0:T(2,128)(2,1)} %get-tuple-element.43), calls=%async_computation.2 | async-start | bytes 557056 | tf_op jit(solution)/shard_map/all_to_all | solution.py:248
